TPU v7x, 128 devices: a whole 4x4x4 slice. The times are simulated.
128 devices in a mesh: branch: 2 (over y_lo), dp: 64 (over x, z, y_hi, core).
Axes of the slice: x: 4, y: 4 (y_hi: 2, y_lo: 2; y = y_hi * 2 + y_lo), z: 4, core: 2. Of those that a mesh axis runs over, the one named last changes fastest.
Arguments:
- frames: float32 [3, 128, 256, 512], P(None, 'dp'), may hold values from -16 to 16
- attend_norm: float32 [2, 512], replicated, may hold values from -0.5 to 1.25
- attend_in: bfloat16 [512, 3, 512], P('dp', None, 'branch'), may hold values from -0.25 to 0.25
- attend_out: bfloat16 [512, 512], P('dp', 'branch'), may hold values from -1.5 to 1.5
- position_slope: float32 [8], P('branch'), may hold values from 0.004 to 0.1
- mixer_norm: float32 [2, 512], replicated, may hold values from -0.5 to 1.25
- mixer_in: bfloat16 [512, 2, 1536], P('dp', None, 'branch'), may hold values from -0.25 to 0.25
- gating_norm: float32 [2, 1536], P(None, 'branch'), may hold values from -0.5 to 1.25
- kernel_taps: float32 [31, 1536], P(None, 'branch'), may hold values from -1 to 1
- kernel_bias: float32 [1536], P('branch'), may hold values from -4 to 4
- mixer_out: bfloat16 [512, 1536], P('dp', 'branch'), may hold values from -0.3125 to 0.3125
- merge_logits: float32 [2], replicated, may hold values from -1 to 1
- final_norm: float32 [2, 512], replicated, may hold values from -0.5 to 1.25
- lengths: int32 [3, 128], P(None, 'dp'), may hold values from 64 to 256, as said below
- cotangent: float32 [3, 128, 256, 512], P(None, 'dp'), may hold values from -16 to 16
Outputs:
- layer_out: float32 [3, 128, 256, 512], P(None, 'dp')
- frames_grad: float32 [3, 128, 256, 512], P(None, 'dp')
- attend_norm_grad: float32 [2, 512], replicated
- attend_in_grad: float32 [512, 3, 512], P('dp', None, 'branch')
- attend_out_grad: float32 [512, 512], P('dp', 'branch')
- position_slope_grad: float32 [8], P('branch')
- mixer_norm_grad: float32 [2, 512], replicated
- mixer_in_grad: float32 [512, 2, 1536], P('dp', None, 'branch')
- gating_norm_grad: float32 [2, 1536], P(None, 'branch')
- kernel_taps_grad: float32 [31, 1536], P(None, 'branch')
- kernel_bias_grad: float32 [1536], P('branch')
- mixer_out_grad: float32 [512, 1536], P('dp', 'branch')
- merge_logits_grad: float32 [2], replicated
- final_norm_grad: float32 [2, 512], replicated
Inputs may be any that keep to these rules, and one draw needn't show every extreme that they name: `lengths`: in every micro-batch one utterance fills the slot and one has a quarter of 256 frames.
All inputs are finite; a program needn't handle non-finite values.
Results may differ from a plain program's by a relative error of at most 0.0095.
Values may be sent and summed in bfloat16 or wider, within the bound.
No kernel may reach another device: no remote copies, remote signals or barrier semaphores. Data moves between devices by JAX's collectives and lax.ppermute only.
A program may use at most 448 MiB of HBM per device.

v0:
```python
from functools import partial

import jax
import jax.numpy as jnp
from jax import lax
from jax.sharding import PartitionSpec as P

EPSILON = 1e-05
NEGATIVE = -1e30


def norm_rows(rows_in, params):
    average = jnp.mean(rows_in, axis=-1, keepdims=True)
    centered = rows_in - average
    variance = jnp.mean(centered * centered, axis=-1, keepdims=True)
    return centered * lax.rsqrt(variance + EPSILON) * params[0] + params[1]


def depthwise(field_in, kernel_taps):
    tap_count = kernel_taps.shape[0]
    reach_len = (tap_count - 1) // 2
    slot_len = field_in.shape[1]
    padded = jnp.pad(field_in, ((0, 0), (reach_len, reach_len), (0, 0)))
    result = kernel_taps[0] * padded[:, 0:slot_len]
    for tap in range(1, tap_count):
        result = result + kernel_taps[tap] * padded[:, tap : tap + slot_len]
    return result


def gate_apply(seq_count, slot_len, normed_in, taps_in, bias_in, first_in):
    field_in = normed_in.reshape(seq_count, slot_len, normed_in.shape[1])
    conved = (
        depthwise(field_in, taps_in).reshape(seq_count * slot_len, normed_in.shape[1]) + bias_in
    )
    return first_in * conved


def merge_weights(logits_in):
    merge_top = jnp.max(logits_in)
    merge_exp = jnp.exp(logits_in - merge_top)
    return merge_exp / jnp.sum(merge_exp)


def finish_rows(valid_rows, frames_in, attend_sum, mixer_sum, logits_in, params):
    mixing = merge_weights(logits_in)
    merged = frames_in + mixing[0] * attend_sum + mixing[1] * mixer_sum
    return norm_rows(merged, params) * valid_rows


def attend_logits(queries, key_heads, slopes, distance, key_mask, score_scale):
    scores = (
        jnp.einsum("sihe,sjhe->shij", queries, key_heads, preferred_element_type=jnp.float32)
        * score_scale
    )
    logits = scores - slopes[None, :, None, None] * distance[None, None]
    return jnp.where(key_mask, logits, NEGATIVE)


def shards(
    frames,
    attend_norm,
    attend_in,
    attend_out,
    position_slope,
    mixer_norm,
    mixer_in,
    gating_norm,
    kernel_taps,
    kernel_bias,
    mixer_out,
    merge_logits,
    final_norm,
    lengths,
    cotangent,
):
    micro_count, seq_count, slot_len, model_width = frames.shape
    row_count = seq_count * slot_len
    head_count = position_slope.shape[0]
    head_dim = attend_in.shape[2] // head_count
    score_scale = head_dim ** (-0.5)
    channels = gating_norm.shape[1]
    half_total = channels * lax.axis_size("branch")
    positions = jnp.arange(slot_len, dtype=jnp.int32)
    offsets = (positions[None, :] - positions[:, None]).astype(jnp.float32)
    distance = jnp.sqrt(offsets * offsets + 1.0)
    small_sums = (
        jnp.zeros((2, model_width), jnp.float32),
        jnp.zeros((2, model_width), jnp.float32),
        jnp.zeros((2, model_width), jnp.float32),
        jnp.zeros((2,), jnp.float32),
        jnp.zeros((head_count,), jnp.float32),
        jnp.zeros((2, channels), jnp.float32),
        jnp.zeros(kernel_taps.shape, jnp.float32),
        jnp.zeros((channels,), jnp.float32),
    )
    shard_sums = tuple(
        (
            jnp.zeros(tensor.shape, jnp.float32)
            for tensor in (attend_in, attend_out, mixer_in, mixer_out)
        )
    )
    outputs = []
    frame_grads = []
    for batch_index in range(micro_count):
        full_in, full_out, full_mix_in, full_mix_out = (
            lax.all_gather(attend_in, "dp", axis=0, tiled=True),
            lax.all_gather(attend_out, "dp", axis=0, tiled=True),
            lax.all_gather(mixer_in, "dp", axis=0, tiled=True),
            lax.all_gather(mixer_out, "dp", axis=0, tiled=True),
        )
        frame_rows = frames[batch_index].reshape(row_count, model_width)
        cot_rows = cotangent[batch_index].reshape(row_count, model_width)
        valid_mask = (positions[None, :] < lengths[batch_index][:, None]).astype(jnp.float32)
        valid_rows = valid_mask.reshape(row_count, 1)
        key_mask = valid_mask[:, None, None, :] > 0.5
        attend_normed, attend_pullback = jax.vjp(norm_rows, frame_rows, attend_norm)
        attend_low = attend_normed.astype(jnp.bfloat16)
        triple = jnp.einsum(
            "td,dkc->tkc", attend_low, full_in, preferred_element_type=jnp.float32
        ).astype(jnp.bfloat16)
        queries = triple[:, 0].reshape(seq_count, slot_len, head_count, head_dim)
        key_heads = triple[:, 1].reshape(seq_count, slot_len, head_count, head_dim)
        value_heads = triple[:, 2].reshape(seq_count, slot_len, head_count, head_dim)
        logits = attend_logits(queries, key_heads, position_slope, distance, key_mask, score_scale)
        highest = jnp.max(logits, axis=-1, keepdims=True)
        exponent = jnp.exp(logits - highest)
        denominator = jnp.sum(exponent, axis=-1, keepdims=True)
        log_total = highest + jnp.log(denominator)
        prob_low = (exponent / denominator).astype(jnp.bfloat16)
        context = jnp.einsum(
            "shij,sjhe->sihe", prob_low, value_heads, preferred_element_type=jnp.float32
        )
        context = context.astype(jnp.bfloat16).reshape(row_count, head_count * head_dim)
        attend_part = jnp.einsum("tc,dc->td", context, full_out, preferred_element_type=jnp.float32)
        mixer_normed, mixer_pullback = jax.vjp(norm_rows, frame_rows, mixer_norm)
        mixer_low = mixer_normed.astype(jnp.bfloat16)
        hidden = jnp.einsum(
            "td,dkc->tkc", mixer_low, full_mix_in, preferred_element_type=jnp.float32
        )
        active, gelu_pullback = jax.vjp(jax.nn.gelu, hidden)
        first_half = active[:, 0]
        second = active[:, 1]
        gate_sums = lax.psum(
            (jnp.sum(second, axis=-1), jnp.sum(second * second, axis=-1)), "branch"
        )
        average = gate_sums[0] / half_total
        variance = gate_sums[1] / half_total - average * average
        inverse = lax.rsqrt(variance + EPSILON)[:, None]
        standard = (second - average[:, None]) * inverse
        gate_in = (standard * gating_norm[0] + gating_norm[1]) * valid_rows
        gated_out, gate_pullback = jax.vjp(
            partial(gate_apply, seq_count, slot_len), gate_in, kernel_taps, kernel_bias, first_half
        )
        gated_low = gated_out.astype(jnp.bfloat16)
        mixer_part = jnp.einsum(
            "tc,dc->td", gated_low, full_mix_out, preferred_element_type=jnp.float32
        )
        attend_sum, mixer_sum = lax.psum((attend_part, mixer_part), "branch")
        layer_rows, finish_pullback = jax.vjp(
            partial(finish_rows, valid_rows),
            frame_rows,
            attend_sum,
            mixer_sum,
            merge_logits,
            final_norm,
        )
        grad_direct, grad_attend, grad_mixer, grad_merge_now, grad_final_now = finish_pullback(
            cot_rows
        )
        outputs.append(layer_rows.reshape(seq_count, slot_len, model_width))
        attend_grad_low = grad_attend.astype(jnp.bfloat16)
        mixer_grad_low = grad_mixer.astype(jnp.bfloat16)
        grad_mix_out = jnp.einsum(
            "td,tc->dc", mixer_grad_low, gated_low, preferred_element_type=jnp.float32
        )
        grad_gated = jnp.einsum(
            "td,dc->tc", mixer_grad_low, full_mix_out, preferred_element_type=jnp.float32
        )
        grad_gate_in, grad_taps_now, grad_kbias_now, grad_first = gate_pullback(grad_gated)
        grad_pre = grad_gate_in * valid_rows
        grad_gnorm_now = jnp.stack(
            [jnp.sum(grad_pre * standard, axis=0), jnp.sum(grad_pre, axis=0)]
        )
        grad_standard = grad_pre * gating_norm[0]
        back_sums = lax.psum(
            (jnp.sum(grad_standard, axis=-1), jnp.sum(grad_standard * standard, axis=-1)), "branch"
        )
        grad_second = inverse * (
            grad_standard
            - back_sums[0][:, None] / half_total
            - standard * back_sums[1][:, None] / half_total
        )
        grad_hidden = gelu_pullback(jnp.stack([grad_first, grad_second], axis=1))[0].astype(
            jnp.bfloat16
        )
        grad_mix_in = jnp.einsum(
            "td,tkc->dkc", mixer_low, grad_hidden, preferred_element_type=jnp.float32
        )
        grad_mixer_normed = jnp.einsum(
            "tkc,dkc->td", grad_hidden, full_mix_in, preferred_element_type=jnp.float32
        )
        grad_att_out = jnp.einsum(
            "td,tc->dc", attend_grad_low, context, preferred_element_type=jnp.float32
        )
        grad_context = jnp.einsum(
            "td,dc->tc", attend_grad_low, full_out, preferred_element_type=jnp.float32
        )
        grad_context = grad_context.astype(jnp.bfloat16).reshape(
            seq_count, slot_len, head_count, head_dim
        )
        logits = attend_logits(queries, key_heads, position_slope, distance, key_mask, score_scale)
        prob_full = jnp.exp(logits - log_total)
        grad_probs = jnp.einsum(
            "sihe,sjhe->shij", grad_context, value_heads, preferred_element_type=jnp.float32
        )
        grad_values = jnp.einsum(
            "shij,sihe->sjhe", prob_low, grad_context, preferred_element_type=jnp.float32
        )
        row_dot = jnp.sum(prob_full * grad_probs, axis=-1, keepdims=True)
        grad_logits = prob_full * (grad_probs - row_dot)
        grad_slope_now = -jnp.einsum("shij,ij->h", grad_logits, distance)
        grad_scores = grad_logits.astype(jnp.bfloat16)
        grad_queries = (
            jnp.einsum(
                "shij,sjhe->sihe", grad_scores, key_heads, preferred_element_type=jnp.float32
            )
            * score_scale
        )
        grad_keys = (
            jnp.einsum("shij,sihe->sjhe", grad_scores, queries, preferred_element_type=jnp.float32)
            * score_scale
        )
        grad_triple = jnp.stack(
            [
                grad_queries.reshape(row_count, head_count * head_dim),
                grad_keys.reshape(row_count, head_count * head_dim),
                grad_values.reshape(row_count, head_count * head_dim),
            ],
            axis=1,
        ).astype(jnp.bfloat16)
        grad_att_in = jnp.einsum(
            "td,tkc->dkc", attend_low, grad_triple, preferred_element_type=jnp.float32
        )
        grad_attend_normed = jnp.einsum(
            "tkc,dkc->td", grad_triple, full_in, preferred_element_type=jnp.float32
        )
        total_attend, total_mixer = (
            lax.psum(grad_attend_normed.astype(jnp.bfloat16), "branch").astype(jnp.float32),
            lax.psum(grad_mixer_normed.astype(jnp.bfloat16), "branch").astype(jnp.float32),
        )
        grad_from_attend, grad_anorm_now = attend_pullback(total_attend)
        grad_from_mixer, grad_mnorm_now = mixer_pullback(total_mixer)
        frame_total = grad_direct + grad_from_attend + grad_from_mixer
        frame_grads.append(frame_total.reshape(seq_count, slot_len, model_width))
        small_sums = jax.tree.map(
            jnp.add,
            small_sums,
            (
                grad_anorm_now,
                grad_mnorm_now,
                grad_final_now,
                grad_merge_now,
                grad_slope_now,
                grad_gnorm_now,
                grad_taps_now,
                grad_kbias_now,
            ),
        )
        weight_grads = (grad_att_in, grad_att_out, grad_mix_in, grad_mix_out)
        shards_now = (
            lax.psum_scatter(weight_grads[0], "dp", scatter_dimension=0, tiled=True),
            lax.psum_scatter(weight_grads[1], "dp", scatter_dimension=0, tiled=True),
            lax.psum_scatter(weight_grads[2], "dp", scatter_dimension=0, tiled=True),
            lax.psum_scatter(weight_grads[3], "dp", scatter_dimension=0, tiled=True),
        )
        shard_sums = jax.tree.map(jnp.add, shard_sums, shards_now)
    small_total = lax.psum(small_sums, "dp")
    return (
        jnp.stack(outputs),
        jnp.stack(frame_grads),
        small_total[0],
        shard_sums[0],
        shard_sums[1],
        small_total[4],
        small_total[1],
        shard_sums[2],
        small_total[5],
        small_total[6],
        small_total[7],
        shard_sums[3],
        small_total[3],
        small_total[2],
    )


def solution(mesh):
    placed = (
        P(None, "dp", None, None),
        P(),
        P("dp", None, "branch"),
        P("dp", "branch"),
        P("branch"),
        P(),
        P("dp", None, "branch"),
        P(None, "branch"),
        P(None, "branch"),
        P("branch"),
        P("dp", "branch"),
        P(),
        P(),
        P(None, "dp"),
        P(None, "dp", None, None),
    )
    return jax.shard_map(
        shards,
        mesh=mesh,
        in_specs=placed,
        out_specs=(
            P(None, "dp", None, None),
            P(None, "dp", None, None),
            P(),
            P("dp", None, "branch"),
            P("dp", "branch"),
            P("branch"),
            P(),
            P("dp", None, "branch"),
            P(None, "branch"),
            P(None, "branch"),
            P("branch"),
            P("dp", "branch"),
            P(),
            P(),
        ),
        check_vma=False,
    )
```

profile of v0, /device:TPU:16, one launch (start us, length us, event | category | flops | bytes accessed | tf_op | source)
XLA Modules:
  0.0 2463.1 jit_solution(297875086414960532)
XLA Ops:
  10.3 2.4 multiply_reduce_fusion.128
  14.4 92.4 %all_gather.8 = bf16[512,3,256]{2,0,1:T(8,128)(2,1)S(1)} all-gather(bf16[8,3,256]{2,0,1:T(8,128)(2,1)S(1)} %copy-done.225), channel_id=1, replica_groups=mesh['branch'=2,'dp'=64] {'dp'}, dimensions={0}, use_global_device_ids=true | all-gather | bytes 798720 | tf_op jit(solution)/shard_map/all_gather | solution.py:106
  106.8 2.4 add_convert_fusion.1
  160.3 96.1 %all_gather.9 = bf16[512,256]{1,0:T(8,128)(2,1)S(1)} all-gather(bf16[8,256]{1,0:T(8,128)(2,1)S(1)} %copy-done.237), channel_id=1, replica_groups=mesh['branch'=2,'dp'=64] {'dp'}, dimensions={0}, use_global_device_ids=true | all-gather | bytes 266240 | tf_op jit(solution)/shard_map/all_gather | solution.py:107
  260.5 95.8 %all_gather.11 = bf16[512,768]{1,0:T(8,128)(2,1)} all-gather(bf16[8,768]{1,0:T(8,128)(2,1)S(1)} %copy-done.226), channel_id=1, replica_groups=mesh['branch'=2,'dp'=64] {'dp'}, dimensions={0}, use_global_device_ids=true | all-gather | bytes 798720 | tf_op jit(solution)/shard_map/all_gather | solution.py:109
  356.3 4.5 multiply_multiply_fusion.7
  363.9 3.0 multiply_multiply_fusion.6
  368.3 3.0 multiply_multiply_fusion.8
  371.3 2.7 slice_reduce_fusion.39
  374.8 9.6 all-reduce.215
  395.9 3.0 add_multiply_fusion.2
  399.0 6.1 multiply_add_fusion
  405.2 6.1 multiply_add_fusion.1
  411.3 6.1 multiply_add_fusion.2
  436.4 4.4 multiply_reduce_fusion.113
  440.8 141.3 %all-reduce.224.cloned.1.call-done = (f32[512,512]{1,0:T(8,128)}, f32[512,512]{1,0:T(8,128)}, f32[512,512]{1,0:T(8,128)}, f32[512,512]{1,0:T(8,128)}, f32[512,512]{1,0:T(8,128)}, /*index=5*/f32[512,512]{1,0:T(8,128)}) async-done(((f32[512,512]{1,0:T(8,128)}, f32[512,512]{1,0:T(8,128)}, f32[512,512]{1,0:T(8,128)}, f32[512,512]{1,0:T(8,128)}, f32[512,512]{1,0:T(8,128)}, /*index=5*/f32[512,512]{1,0:T(8,128)}), ...) | async-done | bytes 6291472 | tf_op jit(solution)/shard_map/psum | solution.py:158
  582.1 3.2 fusion.181
  593.4 3.3 multiply_reduce_fusion.110
  596.8 2.4 fusion.176
  601.1 7.8 multiply_reduce_fusion.92
  608.9 10.5 broadcast_multiply_fusion.2
  619.4 7.7 multiply_reduce_fusion.32
  627.1 10.7 broadcast_multiply_fusion
  637.9 7.8 multiply_reduce_fusion.62
  645.7 19.7 broadcast_multiply_fusion.3
  665.5 9.8 broadcast_multiply_fusion.1
  680.9 2.5 multiply_reduce_fusion
  693.9 2.5 multiply_reduce_fusion.1
  703.0 2.1 reshape.1653
  713.7 13.0 pad_add_fusion.2
  726.8 5.5 multiply_reduce_fusion.95
  732.8 12.9 pad_add_fusion
  745.8 5.5 multiply_reduce_fusion.93
  751.8 12.6 pad_add_fusion.1
  764.5 4.6 multiply_reduce_fusion.94
  769.1 7.9 all-reduce.214
  803.4 2.9 fusion.62
  807.5 2.9 fusion.61
  813.9 2.8 fusion.60
  822.0 2.1 fusion.13
  826.2 2.1 fusion.6
  828.4 2.1 fusion.20
  836.1 2.2 fusion.125
  839.8 2.7 add_add_fusion
  844.0 5.4 fusion.165
  849.4 2.4 multiply_reduce_fusion.91
  852.0 2.4 multiply_reduce_fusion.31
  855.0 2.4 multiply_reduce_fusion.61
  875.7 2.8 convolution_add_fusion
  878.6 2.6 fusion.156
  882.7 2.6 add_add_fusion.1
  896.5 34.0 %all-reduce.226.cloned.1.call-done = (bf16[512,512]{1,0:T(8,128)(2,1)}, bf16[512,512]{1,0:T(8,128)(2,1)}, bf16[512,512]{1,0:T(8,128)(2,1)}, bf16[512,512]{1,0:T(...) async-done(((bf16[512,512]{1,0:T(8,128)(2,1)}, bf16[512,512]{1,0:T(8,128)(2,1)}, bf16[512,512]{1,0:T(8,128)(2,1)}, bf16[512,512]{1,0:T(8,128)(2,1)}, ...) | async-done | bytes 3145744 | tf_op jit(solution)/shard_map/psum | solution.py:249
  932.4 3.6 fusion.103
  936.1 2.3 fusion.105
  938.6 2.6 multiply_reduce_fusion.119
  943.1 2.6 multiply_reduce_fusion.115
  945.7 4.6 multiply_reduce_fusion.131
  952.2 5.3 fusion.171
  961.9 322.8 %all-reduce.213 = (f32[2,512]{1,0:T(2,128)}, f32[4]{0:T(128)}, f32[2,512]{1,0:T(2,128)}, f32[2,768]{1,0:T(2,128)}, f32[768]{0:T(1024)}, /*index=5*/f32[2]{0:T(128)}, f32[2,512]{1,0:T(2,128)}) all-reduce(f32[2,512]{1,0:T(2,128)S(1)} %add_add_fusion.19, f32[4]{0:T(128)S(1)} %negate_add_fusion, ...), channel_id=1, replica_groups=mesh['branch'=2,'dp'=64] {'dp'}, use_global_device_ids=true, to_apply=%region_83.84 | all-reduce | flops 5382 | bytes 43056 | tf_op jit(solution)/shard_map/psum | solution.py:277
  1284.7 3.3 pad_maximum_fusion.4
  1289.5 359.1 %all-reduce.222.cloned.1.call-done = f32[31,768]{1,0:T(8,128)} async-done(((f32[31,768]{1,0:T(8,128)}), f32[31,768]{1,0:T(8,128)}) %all-reduce.222.cloned.1.call-update) | async-done | bytes 95248 | tf_op jit(solution)/shard_map/psum | solution.py:277
  1648.6 327.5 %reduce-scatter.7.cloned.1.call-done = f32[8,256]{1,0:T(8,128)} async-done(((f32[512,256]{1,0:T(8,128)}), f32[8,256]{1,0:T(8,128)}) %reduce-scatter.7.cloned.1.call-update) | async-done | bytes 8208 | tf_op jit(solution)/shard_map/reduce_scatter | solution.py:272
  1976.1 149.2 %reduce-scatter.11.cloned.1.call-done = f32[8,768]{1,0:T(8,128)} async-done(((f32[512,768]{1,0:T(8,128)}), f32[8,768]{1,0:T(8,128)}) %reduce-scatter.11.cloned.1.call-update) | async-done | bytes 24592 | tf_op jit(solution)/shard_map/reduce_scatter | solution.py:274
  2125.3 329.2 %reduce-scatter.5.cloned.1.call-done = f32[8,3,256]{2,0,1:T(8,128)} async-done(((f32[512,3,256]{2,0,1:T(8,128)}), f32[8,3,256]{2,0,1:T(8,128)}) %reduce-scatter.5.cloned.1.call-update) | async-done | bytes 24592 | tf_op jit(solution)/shard_map/reduce_scatter | solution.py:271
  (886 shorter events, 219.9 us)
Async XLA Ops:
  7.2 349.1 %all-gather.2.cloned.1.call-start = ((), (), s32[]{:S(2)}) async-start(), calls=%async_computation.4 | async-start | bytes 1597440 | tf_op jit(solution)/shard_map/all_gather | solution.py:108
  8.6 573.5 %all-reduce.224.cloned.1.call-start = ((), (), s32[]{:S(2)}) async-start(), calls=%async_computation.10 | async-start | bytes 12582912 | tf_op jit(solution)/shard_map/psum | solution.py:158
  8.8 104.5 %copy-start.133 = (f32[256,256]{0,1:T(8,128)}, f32[256,256]{0,1:T(8,128)S(1)}, u32[]{:S(2)}) copy-start(f32[256,256]{0,1:T(8,128)S(1)} %add_sqrt_fusion) | copy-start | bytes 786436
  13.6 95.6 %copy-start.6 = (f32[1,2,256,512]{3,2,1,0:T(8,128)}, f32[1,2,256,512]{3,2,1,0:T(8,128)S(1)}, u32[]{:S(2)}) copy-start(f32[1,2,256,512]{3,2,1,0:T(8,128)S(1)} %get-tuple-element.333) | copy-start | bytes 3145732
  13.6 95.6 %copy-start.9 = (f32[1,2,256,512]{3,2,1,0:T(8,128)}, f32[1,2,256,512]{3,2,1,0:T(8,128)S(1)}, u32[]{:S(2)}) copy-start(f32[1,2,256,512]{3,2,1,0:T(8,128)S(1)} %get-tuple-element.332) | copy-start | bytes 3145732
  13.6 568.6 %copy-start.4 = (f32[1,2,256,512]{3,2,1,0:T(8,128)}, f32[1,2,256,512]{3,2,1,0:T(8,128)S(1)}, u32[]{:S(2)}) copy-start(f32[1,2,256,512]{3,2,1,0:T(8,128)S(1)} %get-tuple-element.336) | copy-start | bytes 3145732
  13.6 95.6 %copy-start.217 = (f32[1,2,2,128]{3,1,2,0:T(2,128)}, f32[1,2,2,128]{3,1,2,0:T(2,128)S(1)}, u32[]{:S(2)}) copy-start(f32[1,2,2,128]{3,1,2,0:T(2,128)S(1)} %copy.311) | copy-start | bytes 6148
  13.6 95.6 %copy-start.198 = (f32[512]{0:T(512)}, f32[512]{0:T(512)S(1)}, u32[]{:S(2)}) copy-start(f32[512]{0:T(512)S(1)} %rsqrt.81) | copy-start | bytes 6148
  13.7 95.5 %copy-start.219 = (f32[1,2,2,128]{3,1,2,0:T(2,128)}, f32[1,2,2,128]{3,1,2,0:T(2,128)S(1)}, u32[]{:S(2)}) copy-start(f32[1,2,2,128]{3,1,2,0:T(2,128)S(1)} %copy.315) | copy-start | bytes 6148
  13.7 95.5 %copy-start.196 = (f32[512]{0:T(512)}, f32[512]{0:T(512)S(1)}, u32[]{:S(2)}) copy-start(f32[512]{0:T(512)S(1)} %rsqrt.84) | copy-start | bytes 6148
  13.7 95.5 %copy-start.177 = (f32[1,2,2,128]{3,1,2,0:T(2,128)}, f32[1,2,2,128]{3,1,2,0:T(2,128)S(1)}, u32[]{:S(2)}) copy-start(f32[1,2,2,128]{3,1,2,0:T(2,128)S(1)} %copy.310) | copy-start | bytes 6148
  13.8 95.5 %copy-start.175 = (f32[1,2,2,128]{3,1,2,0:T(2,128)}, f32[1,2,2,128]{3,1,2,0:T(2,128)S(1)}, u32[]{:S(2)}) copy-start(f32[1,2,2,128]{3,1,2,0:T(2,128)S(1)} %copy.314) | copy-start | bytes 6148
  13.8 95.5 %copy-start.162 = (f32[1,512]{1,0:T(1,128)}, f32[1,512]{1,0:T(1,128)S(1)}, u32[]{:S(2)}) copy-start(f32[1,512]{1,0:T(1,128)S(1)} %get-tuple-element.508) | copy-start | bytes 6148
  13.8 95.5 %copy-start.164 = (f32[1,512]{1,0:T(1,128)}, f32[1,512]{1,0:T(1,128)S(1)}, u32[]{:S(2)}) copy-start(f32[1,512]{1,0:T(1,128)S(1)} %get-tuple-element.506) | copy-start | bytes 6148
  14.4 94.9 %copy-start.194 = (f32[512]{0:T(512)}, f32[512]{0:T(512)S(1)}, u32[]{:S(2)}) copy-start(f32[512]{0:T(512)S(1)} %rsqrt.78) | copy-start | bytes 6148
  14.4 94.9 %copy-start.179 = (f32[1,2,2,128]{3,1,2,0:T(2,128)}, f32[1,2,2,128]{3,1,2,0:T(2,128)S(1)}, u32[]{:S(2)}) copy-start(f32[1,2,2,128]{3,1,2,0:T(2,128)S(1)} %copy.306) | copy-start | bytes 6148
  119.1 20.6 copy-start.120
  157.5 100.3 %copy-start.67 = (bf16[2,4,256,256]{2,3,1,0:T(8,128)(2,1)}, bf16[2,4,256,256]{2,3,1,0:T(8,128)(2,1)S(1)}, u32[]{:S(2)}) copy-start(bf16[2,4,256,256]{2,3,1,0:T(8,128)(2,1)S(1)} %divide_convert_fusion) | copy-start | bytes 3145732
  157.5 98.9 %copy-start.127 = (bf16[32,8,2,256]{3,1,2,0:T(8,128)(2,1)S(1)}, bf16[32,8,2,256]{3,1,2,0:T(8,128)(2,1)}, u32[]{:S(2)}) copy-start(bf16[32,8,2,256]{3,1,2,0:T(8,128)(2,1)} %copy.309) | copy-start | bytes 786436
  157.8 99.9 %copy-start.129 = (bf16[32,8,2,256]{3,1,2,0:T(8,128)(2,1)S(1)}, bf16[32,8,2,256]{3,1,2,0:T(8,128)(2,1)}, u32[]{:S(2)}) copy-start(bf16[32,8,2,256]{3,1,2,0:T(8,128)(2,1)} %copy.313) | copy-start | bytes 786436
  158.2 100.9 %copy-start.131 = (bf16[32,8,2,256]{3,1,2,0:T(8,128)(2,1)}, bf16[32,8,2,256]{3,1,2,0:T(8,128)(2,1)S(1)}, u32[]{:S(2)}) copy-start(bf16[32,8,2,256]{3,1,2,0:T(8,128)(2,1)S(1)} %copy.317) | copy-start | bytes 786436
  399.0 18.6 copy-start.37
  424.0 506.4 %all-reduce.226.cloned.1.call-start = ((), (), s32[]{:S(2)}) async-start(), calls=%async_computation.11 | async-start | bytes 6291456 | tf_op jit(solution)/shard_map/psum | solution.py:249
  599.2 38.6 %copy-start.18 = (f32[512,512]{1,0:T(8,128)}, f32[512,512]{1,0:T(8,128)S(1)}, u32[]{:S(2)}) copy-start(f32[512,512]{1,0:T(8,128)S(1)} %get-tuple-element.490) | copy-start | bytes 3145732
  599.2 283.5 %copy-start.12 = (f32[512,512]{1,0:T(8,128)}, f32[512,512]{1,0:T(8,128)S(1)}, u32[]{:S(2)}) copy-start(f32[512,512]{1,0:T(8,128)S(1)} %get-tuple-element.310) | copy-start | bytes 3145732
  599.2 38.6 %copy-start.185 = (f32[512]{0:T(512)}, f32[512]{0:T(512)S(1)}, u32[]{:S(2)}) copy-start(f32[512]{0:T(512)S(1)} %negate_multiply_fusion.5) | copy-start | bytes 6148
  599.3 76.0 %copy-start.181 = (f32[512]{0:T(512)}, f32[512]{0:T(512)S(1)}, u32[]{:S(2)}) copy-start(f32[512]{0:T(512)S(1)} %negate_multiply_fusion.2) | copy-start | bytes 6148
  608.9 36.8 %copy-start.22 = (f32[512,768]{1,0:T(8,128)}, f32[512,768]{1,0:T(8,128)S(1)}, u32[]{:S(2)}) copy-start(f32[512,768]{1,0:T(8,128)S(1)} %get-tuple-element.293) | copy-start | bytes 4718596
  627.1 18.6 copy-start.24
  645.7 19.7 copy-start.26
  713.7 13.0 copy-start.53
  713.7 13.0 copy-start.201
  713.7 13.0 copy-start.214
  713.7 13.0 copy-start.215
  803.4 13.3 copy-start.151
  803.4 13.3 copy-start.152
  836.1 452.0 %reduce-scatter.9.cloned.1.call-start = ((), (), s32[]{:S(2)}) async-start(), calls=%async_computation.8 | async-start | bytes 3194880 | tf_op jit(solution)/shard_map/reduce_scatter | solution.py:273
  842.6 806.0 %all-reduce.222.cloned.1.call-start = ((), (), s32[]{:S(2)}) async-start(), calls=%async_computation.5 | async-start | bytes 196608 | tf_op jit(solution)/shard_map/psum | solution.py:277
  854.9 16.3 copy-start.270
  854.9 16.3 copy-start.267
  854.9 16.3 copy-start.264
  854.9 16.3 copy-start.261
  854.9 16.4 copy-start.258
  854.9 16.4 copy-start.255
  854.9 16.4 copy-start.252
  855.0 16.4 copy-start.249
  855.0 17.7 copy-start.16
  855.0 17.7 copy-start.128
  857.4 16.3 copy-start.20
  875.6 1100.4 %reduce-scatter.7.cloned.1.call-start = ((), (), s32[]{:S(2)}) async-start(), calls=%async_computation.7 | async-start | bytes 532480 | tf_op jit(solution)/shard_map/reduce_scatter | solution.py:272
  878.6 1246.7 %reduce-scatter.11.cloned.1.call-start = ((), (), s32[]{:S(2)}) async-start(), calls=%async_computation.9 | async-start | bytes 1597440 | tf_op jit(solution)/shard_map/reduce_scatter | solution.py:274
  885.3 1569.1 %reduce-scatter.5.cloned.1.call-start = ((), (), s32[]{:S(2)}) async-start(), calls=%async_computation.6 | async-start | bytes 1597440 | tf_op jit(solution)/shard_map/reduce_scatter | solution.py:271
  894.3 36.2 %copy-start.11 = (f32[1,2,256,512]{3,2,1,0:T(8,128)S(1)}, f32[1,2,256,512]{3,2,1,0:T(8,128)}, u32[]{:S(2)}) copy-start(f32[1,2,256,512]{3,2,1,0:T(8,128)} %copy-done.9) | copy-start | bytes 3145732
  894.3 36.2 %copy-start.163 = (f32[1,512]{1,0:T(1,128)S(1)}, f32[1,512]{1,0:T(1,128)}, u32[]{:S(2)}) copy-start(f32[1,512]{1,0:T(1,128)} %copy-done.162) | copy-start | bytes 6148
  894.3 36.2 %copy-start.165 = (f32[1,512]{1,0:T(1,128)S(1)}, f32[1,512]{1,0:T(1,128)}, u32[]{:S(2)}) copy-start(f32[1,512]{1,0:T(1,128)} %copy-done.164) | copy-start | bytes 6148
  894.3 36.2 %copy-start.180 = (f32[1,2,2,128]{3,1,2,0:T(2,128)S(1)}, f32[1,2,2,128]{3,1,2,0:T(2,128)}, u32[]{:S(2)}) copy-start(f32[1,2,2,128]{3,1,2,0:T(2,128)} %copy-done.179) | copy-start | bytes 6148
  896.3 35.9 %copy-start.222 = (f32[1,2,2,128]{3,1,2,0:T(2,128)S(1)}, f32[1,2,2,128]{3,1,2,0:T(2,128)}, u32[]{:S(2)}) copy-start(f32[1,2,2,128]{3,1,2,0:T(2,128)} %copy-done.221) | copy-start | bytes 6148
  896.3 36.0 %copy-start.5 = (f32[1,2,256,512]{3,2,1,0:T(8,128)S(1)}, f32[1,2,256,512]{3,2,1,0:T(8,128)}, u32[]{:S(2)}) copy-start(f32[1,2,256,512]{3,2,1,0:T(8,128)} %copy-done.4) | copy-start | bytes 3145732
  896.3 36.0 %copy-start.8 = (f32[1,2,256,512]{3,2,1,0:T(8,128)S(1)}, f32[1,2,256,512]{3,2,1,0:T(8,128)}, u32[]{:S(2)}) copy-start(f32[1,2,256,512]{3,2,1,0:T(8,128)} %copy-done.6) | copy-start | bytes 3145732
  896.3 36.0 %copy-start.176 = (f32[1,2,2,128]{3,1,2,0:T(2,128)S(1)}, f32[1,2,2,128]{3,1,2,0:T(2,128)}, u32[]{:S(2)}) copy-start(f32[1,2,2,128]{3,1,2,0:T(2,128)} %copy-done.175) | copy-start | bytes 6148
  896.3 36.0 %copy-start.178 = (f32[1,2,2,128]{3,1,2,0:T(2,128)S(1)}, f32[1,2,2,128]{3,1,2,0:T(2,128)}, u32[]{:S(2)}) copy-start(f32[1,2,2,128]{3,1,2,0:T(2,128)} %copy-done.177) | copy-start | bytes 6148
  896.3 36.0 %copy-start.195 = (f32[512]{0:T(512)S(1)}, f32[512]{0:T(512)}, u32[]{:S(2)}) copy-start(f32[512]{0:T(512)} %copy-done.194) | copy-start | bytes 6148
  943.0 18.2 copy-start.275
  943.0 341.7 %copy-start.113 = (f32[512,512]{1,0:T(8,128)S(1)}, f32[512,512]{1,0:T(8,128)}, u32[]{:S(2)}) copy-start(f32[512,512]{1,0:T(8,128)} %get-tuple-element.441) | copy-start | bytes 3145732
  (223 other events, 921.3 us)
Sparse Core Ops, SparseCore 0:
  11.7 65.1 all-gather.1
  424.2 157.9 all-reduce.223
  836.2 94.2 all-reduce.225
  935.6 147.2 reduce-scatter.8
  1085.8 562.7 all-reduce.221
  1651.5 324.5 reduce-scatter.6
  1981.8 143.4 reduce-scatter.10
  2128.3 326.0 reduce-scatter.4
where the time goes:
time: 2480 us; the launch traced here: 2460 us
  waiting for transfers between devices  1340 us (54%)
  blocking collectives  625 us (25%)
  other arithmetic  233 us (9%)
  local copies, waits for them, and re-layouts  128 us (5%)
  matrix products  110 us (4%)
  between operations  25.8 us (1%)
    psum x1, waiting for transfers between devices, shards(): small_total = lax.psum(small_sums, 'dp')  359 us
    reduce_scatter x1, waiting for transfers between devices, shards(): lax.psum_scatter(weight_grads[0], 'dp', scatter_dimension=0, tiled=True)  329 us
    reduce_scatter x1, waiting for transfers between devices, shards(): lax.psum_scatter(weight_grads[1], 'dp', scatter_dimension=0, tiled=True)  327 us
    psum x1, blocking collectives, shards(): small_total = lax.psum(small_sums, 'dp')  323 us
    reduce_scatter x1, waiting for transfers between devices, shards(): lax.psum_scatter(weight_grads[3], 'dp', scatter_dimension=0, tiled=True)  149 us
    psum x1, waiting for transfers between devices, shards(): attend_sum, mixer_sum = lax.psum((attend_part, mixer_part), 'branch')  141 us
    all_gather x1, blocking collectives, shards(): lax.all_gather(attend_out, 'dp', axis=0, tiled=True)  96.1 us
    all_gather x1, blocking collectives, shards(): lax.all_gather(mixer_out, 'dp', axis=0, tiled=True)  95.8 us
  transfers between devices with their start and end apart: 8, of which 6 were waited for; matrix products, arithmetic and copies ran while one was open for 6% of the time, Pallas kernels for 0%

commit v1 on v0

v1 whole, which is shorter than its diff:
```python
from functools import partial

import jax
import jax.numpy as jnp
import numpy as np
from jax import lax
from jax.experimental import pallas as pl
from jax.experimental.pallas import tpu as pltpu
from jax.sharding import PartitionSpec as P

EPSILON = 1e-05
NEGATIVE = -1e30
F32 = jnp.float32
BF16 = jnp.bfloat16
SLOT = 256
WIDTH = 512
HEADS = 8
HEAD = 64
HALF = 1536
TAPS = 31
REACH = 15
UTTS = 3
ROWS = UTTS * SLOT
PERIOD = SLOT + REACH
BINS = (PERIOD + 1) // 2
SPEC = 2 * BINS
BLOCK = 256
BLOCKS = HALF // BLOCK
PER_BRANCH = 768 // BLOCK
GELU_A = 0.7978845608028654
GELU_B = GELU_A * 0.044715
VMEM_LIMIT = 60 * 1024 * 1024


def transform_tables():
    bins = np.arange(BINS)[:, None]
    angle = 2 * np.pi * bins * np.arange(SLOT)[None, :] / PERIOD
    lag_angle = 2 * np.pi * bins * (np.arange(TAPS) - REACH)[None, :] / PERIOD
    weight = np.where(bins == 0, 1.0, 2.0) / PERIOD
    forward = np.concatenate([np.cos(angle), -np.sin(angle)], 0)
    inverse = np.concatenate([np.cos(angle) * weight, -np.sin(angle) * weight], 0).T
    tap_forward = np.concatenate([np.cos(lag_angle), -np.sin(lag_angle)], 0)
    tap_inverse = np.concatenate([np.cos(lag_angle) * weight, -np.sin(lag_angle) * weight], 0).T
    tap_forward = np.pad(tap_forward, ((0, 0), (0, 1)))
    tap_inverse = np.pad(tap_inverse, ((0, 1), (0, 0)))
    return forward, inverse, tap_forward, tap_inverse


def dot_nn(a, b):
    return lax.dot_general(a, b, (((1,), (0,)), ((), ())), preferred_element_type=F32)


def dot_nt(a, b):
    return lax.dot_general(a, b, (((1,), (1,)), ((), ())), preferred_element_type=F32)


def dot_tn(a, b):
    return lax.dot_general(a, b, (((0,), (0,)), ((), ())), preferred_element_type=F32)


def standardize(rows_in):
    average = jnp.mean(rows_in, axis=-1, keepdims=True)
    centered = rows_in - average
    variance = jnp.mean(centered * centered, axis=-1, keepdims=True)
    rstd = lax.rsqrt(variance + EPSILON)
    return centered * rstd, rstd


def gelu_pair(v):
    square = v * v
    half = 0.5 + 0.5 * jnp.tanh(v * (GELU_A + GELU_B * square))
    active = v * half
    slope = half + active * (1.0 - half) * (2 * GELU_A + 6 * GELU_B * square)
    return active, slope


def fill_distance(distance):
    key_at = lax.broadcasted_iota(jnp.int32, (SLOT, SLOT), 0)
    query_at = lax.broadcasted_iota(jnp.int32, (SLOT, SLOT), 1)
    offset = (key_at - query_at).astype(F32)
    distance[...] = jnp.sqrt(offset * offset + 1.0)


def attend_forward(info, slopes, frames, norm, weights, triple, context, log_total, distance):
    step = pl.program_id(0)

    @pl.when(step == 0)
    def _():
        fill_distance(distance)

    normed, _ = standardize(frames[0, 0])
    low = (normed * norm[0:1] + norm[1:2]).astype(BF16)
    for b in range(2):
        part = dot_nn(low, weights[b, :, 0:768])
        part = jnp.concatenate([part[:, 0:256] * (HEAD**-0.5), part[:, 256:768]], axis=1)
        triple[0, b * 768 : (b + 1) * 768, :] = part.astype(BF16).T
    length = info[1 + step]
    is_key = lax.broadcasted_iota(jnp.int32, (SLOT, SLOT), 0) < length

    def head(h, carry):
        base = pl.multiple_of((h // 4) * 768 + (h % 4) * HEAD, HEAD)
        q = triple[0, pl.ds(base, HEAD), :]
        k = triple[0, pl.ds(base + 256, HEAD), :]
        v = triple[0, pl.ds(base + 512, HEAD), :]
        logits = dot_tn(k, q) - slopes[h] * distance[...]
        logits = jnp.where(is_key, logits, NEGATIVE)
        highest = jnp.max(logits, axis=0, keepdims=True)
        exponent = jnp.exp(logits - highest)
        total = jnp.sum(exponent, axis=0, keepdims=True)
        prob = (exponent * (1.0 / total)).astype(BF16)
        context[0, pl.ds(pl.multiple_of(h * HEAD, HEAD), HEAD), :] = dot_nn(v, prob).astype(BF16)
        log_total[0, pl.ds(h, 1), :] = highest + jnp.log(total)
        return carry

    lax.fori_loop(0, HEADS, head, 0)


def mixer_both(
    info,
    mixing,
    frames,
    cotangent,
    context,
    mixer_norm,
    final_norm,
    gating_norm,
    taps,
    kernel_bias,
    weights,
    out_weights,
    forward,
    inverse,
    tap_forward,
    tap_inverse,
    layer,
    grad_merged_out,
    grad_mixer_out,
    weight_grads,
    small_wide,
    small_narrow,
    tap_spec,
    second_s,
    second_slope,
    first_s,
    first_slope,
    conv_s,
    spec_s,
    cross_s,
    back_s,
    sums,
    part_s,
    gated_s,
    hidden_s,
    low_t,
    grad_t,
):
    step = pl.program_id(0)
    here = pl.ds(pl.multiple_of(step * SLOT, SLOT), SLOT)

    @pl.when(step == 0)
    def _():
        for k in range(BLOCKS):
            tap_spec[k] = jnp.dot(
                tap_forward[...],
                taps[:, k * BLOCK : (k + 1) * BLOCK],
                precision=lax.Precision.HIGHEST,
                preferred_element_type=F32,
            )
        cross_s[...] = jnp.zeros_like(cross_s)
        small_wide[...] = jnp.zeros_like(small_wide)
        small_narrow[...] = jnp.zeros_like(small_narrow)

    rows_in = frames[0, 0]
    normed, rstd = standardize(rows_in)
    low = (normed * mixer_norm[0:1] + mixer_norm[1:2]).astype(BF16)
    low_t[:, here] = low.T
    length = info[1 + step]
    valid = (lax.broadcasted_iota(jnp.int32, (SLOT, 1), 0) < length).astype(F32)

    def place(k):
        b = k // PER_BRANCH
        return b, (k - b * PER_BRANCH) * BLOCK

    def lanes(offset):
        return pl.ds(pl.multiple_of(offset, BLOCK), BLOCK)

    def fold(v):
        return v[:, 0:128] + v[:, 128:256]

    sums[...] = jnp.zeros_like(sums)

    def second_step(k, carry):
        b, off = place(k)
        active, slope = gelu_pair(dot_nn(low, weights[b, :, lanes(768 + off)]))
        second_s[k] = active
        second_slope[k] = slope
        sums[0] += fold(active)
        return carry

    lax.fori_loop(0, BLOCKS, second_step, 0)
    average = jnp.sum(sums[0], axis=-1, keepdims=True) / HALF

    def variance_step(k, carry):
        centered = second_s[k] - average
        second_s[k] = centered
        sums[1] += fold(centered * centered)
        return carry

    lax.fori_loop(0, BLOCKS, variance_step, 0)
    gate_rstd = lax.rsqrt(jnp.sum(sums[1], axis=-1, keepdims=True) / HALF + EPSILON)

    part_s[...] = jnp.zeros_like(part_s)

    def conv_step(k, carry):
        b, off = place(k)
        wide = lanes(k * BLOCK)
        standard = second_s[k] * gate_rstd
        second_s[k] = standard
        gate_in = (standard * gating_norm[0:1, wide] + gating_norm[1:2, wide]) * valid
        spec = dot_nn(forward[...], gate_in.astype(BF16))
        spec_s[k] = spec
        real, imag = spec[0:BINS], spec[BINS:SPEC]
        tap_real, tap_imag = tap_spec[k, 0:BINS], tap_spec[k, BINS:SPEC]
        product = jnp.concatenate(
            [real * tap_real + imag * tap_imag, imag * tap_real - real * tap_imag], axis=0
        )
        conved = dot_nn(inverse[...], product.astype(BF16)) + kernel_bias[0:1, wide]
        conv_s[k] = conved
        active, slope = gelu_pair(dot_nn(low, weights[b, :, lanes(off)]))
        first_s[k] = active
        first_slope[k] = slope
        gated = (active * conved).astype(BF16)
        gated_s[k, here, :] = gated
        part_s[...] += dot_nt(gated, weights[b, :, lanes(1536 + off)])
        return carry

    lax.fori_loop(0, BLOCKS, conv_step, 0)

    mixer_part = part_s[...]
    attend_part = dot_tn(context[0, 0:256, :], out_weights[0].T) + dot_tn(
        context[0, 256:512, :], out_weights[1].T
    )
    merged = rows_in + mixing[0] * attend_part + mixing[1] * mixer_part
    merged_normed, merged_rstd = standardize(merged)
    layer[0] = ((merged_normed * final_norm[0:1] + final_norm[1:2]) * valid).astype(BF16)
    grad_out = cotangent[0, 0] * valid
    scaled = grad_out * final_norm[0:1]
    grad_merged = merged_rstd * (
        scaled
        - jnp.mean(scaled, axis=-1, keepdims=True)
        - merged_normed * jnp.mean(scaled * merged_normed, axis=-1, keepdims=True)
    )
    grad_merged_out[0] = grad_merged
    small_narrow[0:1] += jnp.sum(grad_out * merged_normed, axis=0, keepdims=True)
    small_narrow[1:2] += jnp.sum(grad_out, axis=0, keepdims=True)
    small_narrow[2:3] += jnp.sum(grad_merged * attend_part, axis=0, keepdims=True)
    small_narrow[3:4] += jnp.sum(grad_merged * mixer_part, axis=0, keepdims=True)
    grad_mixer = (mixing[1] * grad_merged).astype(BF16)
    grad_t[:, here] = grad_mixer.T
    sums[...] = jnp.zeros_like(sums)

    def back_step(k, carry):
        b, off = place(k)
        wide = lanes(k * BLOCK)
        grad_gated = dot_nn(grad_mixer, weights[b, :, lanes(1536 + off)])
        grad_conved = grad_gated * first_s[k]
        hidden_s[k, here, :] = (first_slope[k] * (grad_gated * conv_s[k])).astype(BF16)
        small_wide[31:32, wide] += jnp.sum(grad_conved, axis=0, keepdims=True)
        grad_spec = dot_nn(forward[...], grad_conved.astype(BF16))
        grad_real, grad_imag = grad_spec[0:BINS], grad_spec[BINS:SPEC]
        real, imag = spec_s[k, 0:BINS], spec_s[k, BINS:SPEC]
        cross_s[k, 0:BINS] += grad_real * real + grad_imag * imag
        cross_s[k, BINS:SPEC] += grad_real * imag - grad_imag * real
        tap_real, tap_imag = tap_spec[k, 0:BINS], tap_spec[k, BINS:SPEC]
        product = jnp.concatenate(
            [
                grad_real * tap_real - grad_imag * tap_imag,
                grad_real * tap_imag + grad_imag * tap_real,
            ],
            axis=0,
        )
        grad_gate = dot_nn(inverse[...], product.astype(BF16)) * valid
        standard = second_s[k]
        small_wide[32:33, wide] += jnp.sum(grad_gate * standard, axis=0, keepdims=True)
        small_wide[33:34, wide] += jnp.sum(grad_gate, axis=0, keepdims=True)
        grad_standard = grad_gate * gating_norm[0:1, wide]
        back_s[k] = grad_standard
        sums[0] += fold(grad_standard)
        sums[1] += fold(grad_standard * standard)
        return carry

    lax.fori_loop(0, BLOCKS, back_step, 0)
    back_average = jnp.sum(sums[0], axis=-1, keepdims=True) / HALF
    back_scale = jnp.sum(sums[1], axis=-1, keepdims=True) / HALF
    part_s[...] = jnp.zeros_like(part_s)

    def hidden_step(k, carry):
        b, off = place(k)
        grad_second = gate_rstd * (back_s[k] - back_average - second_s[k] * back_scale)
        grad_hidden = (second_slope[k] * grad_second).astype(BF16)
        hidden_s[BLOCKS + k, here, :] = grad_hidden
        part_s[...] += dot_nt(hidden_s[k, here, :], weights[b, :, lanes(off)]) + dot_nt(
            grad_hidden, weights[b, :, lanes(768 + off)]
        )
        return carry

    lax.fori_loop(0, BLOCKS, hidden_step, 0)
    grad_low = part_s[...]
    small_narrow[4:5] += jnp.sum(grad_low * normed, axis=0, keepdims=True)
    small_narrow[5:6] += jnp.sum(grad_low, axis=0, keepdims=True)
    grad_mixer_out[0] = grad_low * mixer_norm[0:1]

    @pl.when(step == UTTS - 1)
    def _():
        def weight_step(k, carry):
            b, off = place(k)
            weight_grads[b, :, lanes(off)] = dot_nn(low_t[...], hidden_s[k]).astype(BF16)
            weight_grads[b, :, lanes(768 + off)] = dot_nn(low_t[...], hidden_s[BLOCKS + k]).astype(
                BF16
            )
            weight_grads[b, :, lanes(1536 + off)] = dot_nn(grad_t[...], gated_s[k]).astype(BF16)
            tap_grad = jnp.dot(
                tap_inverse[...],
                cross_s[k],
                precision=lax.Precision.HIGHEST,
                preferred_element_type=F32,
            )
            small_wide[0:31, lanes(k * BLOCK)] = tap_grad[0:31]
            return carry

        lax.fori_loop(0, BLOCKS, weight_step, 0)


def attend_backward(
    info,
    slopes,
    mixing,
    frames,
    grad_merged,
    grad_mixer,
    triple,
    context,
    log_total,
    norm,
    weights,
    frames_grad,
    weight_grads,
    small_narrow,
    slope_grads,
    distance,
    low_t,
    grad_t,
    context_t,
    triple_t,
    grad_context,
):
    step = pl.program_id(0)
    here = pl.ds(pl.multiple_of(step * SLOT, SLOT), SLOT)

    @pl.when(step == 0)
    def _():
        fill_distance(distance)
        small_narrow[...] = jnp.zeros_like(small_narrow)
        slope_grads[...] = jnp.zeros_like(slope_grads)

    normed, rstd = standardize(frames[0, 0])
    low = (normed * norm[0:1] + norm[1:2]).astype(BF16)
    low_t[:, here] = low.T
    grad_attend = (mixing[0] * grad_merged[0]).astype(BF16)
    grad_t[:, here] = grad_attend.T
    context_t[:, here] = context[0]
    for b in range(2):
        grad_context[b * 256 : (b + 1) * 256, :] = (
            dot_nn(grad_attend, weights[b, :, 768:1024]).astype(BF16).T
        )
    length = info[1 + step]
    is_key = lax.broadcasted_iota(jnp.int32, (SLOT, SLOT), 0) < length

    def head(h, carry):
        base = pl.multiple_of((h // 4) * 768 + (h % 4) * HEAD, HEAD)
        at = pl.multiple_of(h * HEAD, HEAD)
        q = triple[0, pl.ds(base, HEAD), :]
        k = triple[0, pl.ds(base + 256, HEAD), :]
        v = triple[0, pl.ds(base + 512, HEAD), :]
        grad_here = grad_context[pl.ds(at, HEAD), :]
        logits = dot_tn(k, q) - slopes[h] * distance[...]
        logits = jnp.where(is_key, logits, NEGATIVE)
        prob = jnp.exp(logits - log_total[0, pl.ds(h, 1), :])
        grad_prob = dot_tn(v, grad_here)
        row_dot = jnp.sum(prob * grad_prob, axis=0, keepdims=True)
        grad_logits = prob * (grad_prob - row_dot)
        slope_grads[pl.ds(h, 1), :] -= jnp.sum(grad_logits * distance[...], axis=0, keepdims=True)
        grad_scores = grad_logits.astype(BF16)
        grad_q = dot_nn(k, grad_scores) * (HEAD**-0.5)
        grad_k = dot_nt(q, grad_scores)
        grad_v = dot_nt(grad_here, prob.astype(BF16))
        triple_t[pl.ds(base, HEAD), here] = grad_q.astype(BF16)
        triple_t[pl.ds(base + 256, HEAD), here] = grad_k.astype(BF16)
        triple_t[pl.ds(base + 512, HEAD), here] = grad_v.astype(BF16)
        return carry

    lax.fori_loop(0, HEADS, head, 0)
    grad_low = dot_nt(triple_t[0:768, here].T, weights[0, :, 0:768]) + dot_nt(
        triple_t[768:1536, here].T, weights[1, :, 0:768]
    )
    small_narrow[0:1] += jnp.sum(grad_low * normed, axis=0, keepdims=True)
    small_narrow[1:2] += jnp.sum(grad_low, axis=0, keepdims=True)
    scaled = grad_low * norm[0:1] + grad_mixer[0]
    frames_grad[0] = (
        grad_merged[0]
        + rstd
        * (
            scaled
            - jnp.mean(scaled, axis=-1, keepdims=True)
            - normed * jnp.mean(scaled * normed, axis=-1, keepdims=True)
        )
    ).astype(BF16)

    @pl.when(step == UTTS - 1)
    def _():
        for b in range(2):
            weight_grads[b, :, 0:768] = dot_nt(
                low_t[...], triple_t[b * 768 : (b + 1) * 768, :]
            ).astype(BF16)
            weight_grads[b, :, 768:1024] = dot_nt(
                grad_t[...], context_t[b * 256 : (b + 1) * 256, :]
            ).astype(BF16)


def whole(shape):
    return pl.BlockSpec(shape, lambda i, *_: (0,) * len(shape), pipeline_mode=pl.Buffered(1))


def kept(shape):
    return pl.BlockSpec(shape, lambda i, *_: (0,) * len(shape))


def per_utt(shape):
    return pl.BlockSpec((1,) + shape, lambda i, *_: (i,) + (0,) * len(shape))


OWN_FRAMES = pl.BlockSpec((1, 1, SLOT, WIDTH), lambda i, info, *_: (i, info[0], 0, 0))


def scratch(*shape, dtype=F32):
    return pltpu.VMEM(shape, dtype)


def struct(*shape, dtype=F32):
    return jax.ShapeDtypeStruct(shape, dtype)


def params():
    return pltpu.CompilerParams(
        dimension_semantics=("arbitrary",), vmem_limit_bytes=VMEM_LIMIT
    )


def run_attend_forward(info, slopes, frames, norm, weights):
    return pl.pallas_call(
        attend_forward,
        grid_spec=pltpu.PrefetchScalarGridSpec(
            num_scalar_prefetch=2,
            grid=(UTTS,),
            in_specs=[OWN_FRAMES, whole((2, WIDTH)), whole((2, WIDTH, 1024))],
            out_specs=[
                per_utt((HALF, SLOT)),
                per_utt((WIDTH, SLOT)),
                per_utt((HEADS, SLOT)),
            ],
            scratch_shapes=[scratch(SLOT, SLOT)],
        ),
        out_shape=[
            struct(UTTS, HALF, SLOT, dtype=BF16),
            struct(UTTS, WIDTH, SLOT, dtype=BF16),
            struct(UTTS, HEADS, SLOT),
        ],
        compiler_params=params(),
        cost_estimate=pl.CostEstimate(
            flops=2 * ROWS * 512 * 1536, bytes_accessed=8 << 20, transcendentals=0
        ),
        name="attend_forward",
    )(info, slopes, frames, norm, weights)


def run_mixer(
    info, mixing, frames, cotangent, context, mnorm, fnorm, gnorm, taps, bias, weights, attend_w
):
    forward, inverse, tap_forward, tap_inverse = transform_tables()
    tables = (
        jnp.asarray(forward, BF16),
        jnp.asarray(inverse, BF16),
        jnp.asarray(tap_forward, F32),
        jnp.asarray(tap_inverse, F32),
    )
    block = (BLOCKS, SLOT, BLOCK)
    return pl.pallas_call(
        mixer_both,
        grid_spec=pltpu.PrefetchScalarGridSpec(
            num_scalar_prefetch=2,
            grid=(UTTS,),
            in_specs=[
                OWN_FRAMES,
                OWN_FRAMES,
                per_utt((WIDTH, SLOT)),
                whole((2, WIDTH)),
                whole((2, WIDTH)),
                whole((2, HALF)),
                whole((32, HALF)),
                whole((1, HALF)),
                whole((2, WIDTH, 2304)),
                pl.BlockSpec(
                    (2, WIDTH, 256), lambda i, *_: (0, 0, 3), pipeline_mode=pl.Buffered(1)
                ),
                whole((SPEC, SLOT)),
                whole((SLOT, SPEC)),
                whole((SPEC, 32)),
                whole((32, SPEC)),
            ],
            out_specs=[
                per_utt((SLOT, WIDTH)),
                per_utt((SLOT, WIDTH)),
                per_utt((SLOT, WIDTH)),
                whole((2, WIDTH, 2304)),
                kept((40, HALF)),
                kept((8, WIDTH)),
            ],
            scratch_shapes=[
                scratch(BLOCKS, SPEC, BLOCK),
                scratch(*block),
                scratch(*block),
                scratch(*block),
                scratch(*block),
                scratch(*block),
                scratch(BLOCKS, SPEC, BLOCK),
                scratch(BLOCKS, SPEC, BLOCK),
                scratch(*block),
                scratch(2, SLOT, 128),
                scratch(SLOT, WIDTH),
                scratch(BLOCKS, ROWS, BLOCK, dtype=BF16),
                scratch(2 * BLOCKS, ROWS, BLOCK, dtype=BF16),
                scratch(WIDTH, ROWS, dtype=BF16),
                scratch(WIDTH, ROWS, dtype=BF16),
            ],
        ),
        out_shape=[
            struct(UTTS, SLOT, WIDTH, dtype=BF16),
            struct(UTTS, SLOT, WIDTH),
            struct(UTTS, SLOT, WIDTH),
            struct(2, WIDTH, 2304, dtype=BF16),
            struct(40, HALF),
            struct(8, WIDTH),
        ],
        compiler_params=params(),
        cost_estimate=pl.CostEstimate(
            flops=6 * ROWS * 512 * 4608, bytes_accessed=20 << 20, transcendentals=0
        ),
        name="mixer_both",
    )(
        info,
        mixing,
        frames,
        cotangent,
        context,
        mnorm,
        fnorm,
        gnorm,
        taps,
        bias,
        weights,
        attend_w,
        *tables,
    )


def run_attend_backward(
    info, slopes, mixing, frames, grad_merged, grad_mixer, triple, context, log_total, norm, weights
):
    return pl.pallas_call(
        attend_backward,
        grid_spec=pltpu.PrefetchScalarGridSpec(
            num_scalar_prefetch=3,
            grid=(UTTS,),
            in_specs=[
                OWN_FRAMES,
                per_utt((SLOT, WIDTH)),
                per_utt((SLOT, WIDTH)),
                per_utt((HALF, SLOT)),
                per_utt((WIDTH, SLOT)),
                per_utt((HEADS, SLOT)),
                whole((2, WIDTH)),
                whole((2, WIDTH, 1024)),
            ],
            out_specs=[
                per_utt((SLOT, WIDTH)),
                whole((2, WIDTH, 1024)),
                kept((8, WIDTH)),
                kept((HEADS, SLOT)),
            ],
            scratch_shapes=[
                scratch(SLOT, SLOT),
                scratch(WIDTH, ROWS, dtype=BF16),
                scratch(WIDTH, ROWS, dtype=BF16),
                scratch(WIDTH, ROWS, dtype=BF16),
                scratch(HALF, ROWS, dtype=BF16),
                scratch(WIDTH, SLOT, dtype=BF16),
            ],
        ),
        out_shape=[
            struct(UTTS, SLOT, WIDTH, dtype=BF16),
            struct(2, WIDTH, 1024, dtype=BF16),
            struct(8, WIDTH),
            struct(HEADS, SLOT),
        ],
        compiler_params=params(),
        cost_estimate=pl.CostEstimate(
            flops=6 * ROWS * 512 * 1536, bytes_accessed=20 << 20, transcendentals=0
        ),
        name="attend_backward",
    )(
        info,
        slopes,
        mixing,
        frames,
        grad_merged,
        grad_mixer,
        triple,
        context,
        log_total,
        norm,
        weights,
    )


EXTENT = {"x": 4, "y": 4, "z": 4, "core": 2, "branch": 2}


def device_index(x, y, z, core):
    return (y % 2) * 64 + ((x * 4 + z) * 2 + y // 2) * 2 + core


def shift(value, axis, distance):
    pairs = []
    for x in range(4):
        for y in range(4):
            for z in range(4):
                for core in range(2):
                    at = {"x": x, "y": y, "z": z, "core": core}
                    to = dict(at)
                    if axis == "branch":
                        to["y"] = y ^ 1
                    else:
                        to[axis] = (at[axis] + distance) % EXTENT[axis]
                    pairs.append((device_index(**at), device_index(**to)))
    return lax.ppermute(value, ("branch", "dp"), pairs)


def gather_weights(local, core, place):
    columns = local.shape[1]
    half = columns // 2
    other = shift(local, "core", 1)
    pair = jnp.where(
        core == 0, jnp.concatenate([local, other]), jnp.concatenate([other, local])
    )
    block = lax.dynamic_slice_in_dim(pair, core * half, half, 1)
    full = jnp.zeros((4, 16, half), BF16)
    pieces = [block] + [shift(block, "y", s) for s in (1, 3, 2)]
    for s, piece in zip((0, 1, 3, 2), pieces):
        at = (place["y"] - s) % 4
        full = lax.dynamic_update_slice(full, piece[None], ((at % 2) * 2 + at // 2, 0, 0))
    block = full.reshape(2, 32, half)
    for axis, rows in (("z", 32), ("x", 128)):
        full = jnp.zeros((2, 4 * rows, half), BF16)
        pieces = [block] + [shift(block, axis, s) for s in (1, 3, 2)]
        for s, piece in zip((0, 1, 3, 2), pieces):
            at = (place[axis] - s) % 4
            full = lax.dynamic_update_slice(full, piece, (0, at * rows, 0))
        block = full
    other = shift(block, "core", 1)
    return jnp.where(
        core == 0,
        jnp.concatenate([block, other], axis=2),
        jnp.concatenate([other, block], axis=2),
    )


def add_low(terms):
    total = (terms[0].astype(F32) + terms[1].astype(F32)) + (
        terms[2].astype(F32) + terms[3].astype(F32)
    )
    return total


def scatter_grads(grads, core, place):
    half = grads.shape[2] // 2
    keep = lax.dynamic_slice_in_dim(grads, core * half, half, 2)
    send = lax.dynamic_slice_in_dim(grads, (1 - core) * half, half, 2)
    block = (keep.astype(F32) + shift(send, "core", 1).astype(F32)).astype(BF16)
    for axis, rows in (("x", 128), ("z", 32)):
        terms = [lax.dynamic_slice_in_dim(block, place[axis] * rows, rows, 1)]
        for s in (2, 1, 3):
            piece = lax.dynamic_slice_in_dim(block, ((place[axis] + s) % 4) * rows, rows, 1)
            terms.append(shift(piece, axis, s))
        block = add_low(terms).astype(BF16)
    block = block.reshape(4, 16, half)

    def at_y(y):
        return lax.dynamic_slice_in_dim(block, (y % 2) * 2 + y // 2, 1, 0)[0]

    terms = [at_y(place["y"])]
    for s in (2, 1, 3):
        terms.append(shift(at_y((place["y"] + s) % 4), "y", s))
    total = add_low(terms)
    keep = lax.dynamic_slice_in_dim(total, core * 8, 8, 0)
    send = lax.dynamic_slice_in_dim(total, (1 - core) * 8, 8, 0)
    other = shift(send, "core", 1)
    return jnp.where(
        core == 0,
        jnp.concatenate([keep, other], axis=1),
        jnp.concatenate([other, keep], axis=1),
    )


def sum_all(values):
    values = values + shift(values, "core", 1)
    for axis in ("x", "z", "y"):
        values = (values + shift(values, axis, 2)) + (shift(values, axis, 1) + shift(values, axis, 3))
    return values


def shards(
    frames,
    attend_norm,
    attend_in,
    attend_out,
    position_slope,
    mixer_norm,
    mixer_in,
    gating_norm,
    kernel_taps,
    kernel_bias,
    mixer_out,
    merge_logits,
    final_norm,
    lengths,
    cotangent,
):
    branch = lax.axis_index("branch")
    dp = lax.axis_index("dp")
    core = dp % 2
    place = {"x": dp // 16, "z": (dp // 4) % 4, "y": ((dp // 2) % 2) * 2 + branch}
    attend_w = gather_weights(
        jnp.concatenate([attend_in.reshape(8, 768), attend_out], axis=1), core, place
    )
    mixer_w = gather_weights(
        jnp.concatenate([mixer_in.reshape(8, 1536), mixer_out], axis=1), core, place
    )
    slopes_row = jnp.pad(position_slope, (0, 764))[None]
    local = jnp.concatenate([gating_norm, kernel_taps, kernel_bias[None], slopes_row])
    other = shift(local, "branch", 1)
    wide = jnp.where(
        branch == 0,
        jnp.concatenate([local, other], axis=1),
        jnp.concatenate([other, local], axis=1),
    )
    gnorm = wide[0:2]
    taps = jnp.pad(wide[2:33], ((0, 1), (0, 0)))
    bias = wide[33:34]
    slopes = jnp.concatenate([wide[34, 0:4], wide[34, 768:772]])
    own_lengths = lax.dynamic_slice_in_dim(lengths, branch, 1, 1)[:, 0]
    info = jnp.concatenate([branch[None].astype(jnp.int32), own_lengths])
    merge_exp = jnp.exp(merge_logits - jnp.max(merge_logits))
    mixing = merge_exp / jnp.sum(merge_exp)

    triple, context, log_total = run_attend_forward(info, slopes, frames, attend_norm, attend_w)
    layer, grad_merged, grad_mixer, mixer_grads, small_wide, small_mixer = run_mixer(
        info,
        mixing,
        frames,
        cotangent,
        context,
        mixer_norm,
        final_norm,
        gnorm,
        taps,
        bias,
        mixer_w,
        attend_w,
    )
    frame_grads, attend_grads, small_attend, slope_grads = run_attend_backward(
        info,
        slopes,
        mixing,
        frames,
        grad_merged,
        grad_mixer,
        triple,
        context,
        log_total,
        attend_norm,
        attend_w,
    )

    def both(own):
        other = shift(own, "branch", 1)
        pair = jnp.where(
            branch == 0, jnp.stack([own, other], axis=1), jnp.stack([other, own], axis=1)
        )
        return pair.astype(F32)

    layer_out = both(layer)
    frames_out = both(frame_grads)
    mixer_sums = scatter_grads(mixer_grads, core, place)
    attend_sums = scatter_grads(attend_grads, core, place)
    small = sum_all(
        jnp.concatenate(
            [
                small_wide[0:34].reshape(-1),
                small_mixer[0:6].reshape(-1),
                small_attend[0:2].reshape(-1),
                slope_grads.reshape(-1),
            ]
        )
    )
    wide_sum = small[0 : 34 * HALF].reshape(34, HALF)
    narrow = small[34 * HALF : 34 * HALF + 8 * WIDTH].reshape(8, WIDTH)
    slope_sum = jnp.sum(small[34 * HALF + 8 * WIDTH :].reshape(HEADS, SLOT), axis=1)
    wide_own = lax.dynamic_slice_in_dim(wide_sum, branch * 768, 768, 1)
    slope_own = lax.dynamic_slice_in_dim(slope_sum, branch * 4, 4, 0)
    branch_sums = jnp.sum(narrow[2:4], axis=1)
    merge_grad = mixing * (branch_sums - jnp.sum(mixing * branch_sums))
    return (
        layer_out,
        frames_out,
        narrow[6:8],
        attend_sums[:, 0:768].reshape(8, 3, 256),
        attend_sums[:, 768:1024],
        slope_own,
        narrow[4:6],
        mixer_sums[:, 0:1536].reshape(8, 2, 768),
        wide_own[32:34],
        wide_own[0:31],
        wide_own[31],
        mixer_sums[:, 1536:2304],
        merge_grad,
        narrow[0:2],
    )


def solution(mesh):
    placed = (
        P(None, "dp", None, None),
        P(),
        P("dp", None, "branch"),
        P("dp", "branch"),
        P("branch"),
        P(),
        P("dp", None, "branch"),
        P(None, "branch"),
        P(None, "branch"),
        P("branch"),
        P("dp", "branch"),
        P(),
        P(),
        P(None, "dp"),
        P(None, "dp", None, None),
    )
    return jax.shard_map(
        shards,
        mesh=mesh,
        in_specs=placed,
        out_specs=(
            P(None, "dp", None, None),
            P(None, "dp", None, None),
            P(),
            P("dp", None, "branch"),
            P("dp", "branch"),
            P("branch"),
            P(),
            P("dp", None, "branch"),
            P(None, "branch"),
            P(None, "branch"),
            P("branch"),
            P("dp", "branch"),
            P(),
            P(),
        ),
        check_vma=False,
    )
```

time: 2480 us -> 346 us (0.14)
  waiting for transfers between devices: 1340 us -> 99.1 us
  blocking collectives: 625 us -> 0 us
  other arithmetic: 233 us -> 29.6 us
  matrix products: 110 us -> 0 us
  Pallas kernels: 0 us -> 101 us
  local copies, waits for them, and re-layouts: 128 us -> 30.2 us
  starting transfers between devices: 0.58 us -> 81.7 us
    reduce_scatter x4 -> x0, waiting for transfers between devices: 806 us -> none  [the longest x1 329 us: shards(): lax.psum_scatter(weight_grads[0], 'dp', scatter_dimension=0, tiled=True)]
    psum x3 -> x0, waiting for transfers between devices: 534 us -> none  [the longest x1 359 us: shards(): small_total = lax.psum(small_sums, 'dp')]
    psum x3 -> x0, blocking collectives: 340 us -> none  [the longest x1 323 us: shards(): small_total = lax.psum(small_sums, 'dp')]
    all_gather x3 -> x0, blocking collectives: 284 us -> none  [the longest x1 96.1 us: shards(): lax.all_gather(attend_out, 'dp', axis=0, tiled=True)]
    dot_general x54 -> x0, matrix products: 110 us -> none  [the longest x3 23.2 us: shards(): jnp.einsum('td,dc->tc', mixer_grad_low, full_mix_out, preferred_element_t...]
    pallas_call x0 -> x3, Pallas kernels: none -> 101 us  [the longest x1 59 us: run_mixer(): pl.pallas_call(mixer_both, grid_spec=pltpu.PrefetchScalarGridSpec(num_sca...]
    ppermute x0 -> x57, waiting for transfers between devices: none -> 99.1 us  [shift(): return lax.ppermute(value, ('branch', 'dp'), pairs)]
    reduce_sum x38 -> x4, other arithmetic: 87.5 us -> 3.39 us  [the longest x1 1.9 us: shards(): merge_grad = mixing * (branch_sums - jnp.sum(mixing * branch_sums))]
  transfers between devices with their start and end apart: 8 -> 57, of which waited for: 6 -> 29; matrix products, arithmetic and copies ran while one was open for 6% -> 14% of each run, Pallas kernels for 0% -> 5%
where the time goes in v1:
time: 346 us; the launch traced here: 343 us
  Pallas kernels  101 us (29%)
  waiting for transfers between devices  99.1 us (29%)
  starting transfers between devices  81.7 us (24%)
  local copies, waits for them, and re-layouts  30.2 us (9%)
  other arithmetic  29.6 us (9%)
    ppermute x57, waiting for transfers between devices, shift(): return lax.ppermute(value, ('branch', 'dp'), pairs)  99.1 us
    ppermute x57, starting transfers between devices, shift(): return lax.ppermute(value, ('branch', 'dp'), pairs)  81.7 us
    pallas_call x1, Pallas kernels, run_mixer(): pl.pallas_call(mixer_both, grid_spec=pltpu.PrefetchScalarGridSpec(num_sca...  59 us
    pallas_call x1, Pallas kernels, run_attend_backward(): pl.pallas_call(attend_backward, grid_spec=pltpu.PrefetchScalarGridSpec(nu...  24.4 us
    pallas_call x1, Pallas kernels, run_attend_forward(): pl.pallas_call(attend_forward, grid_spec=pltpu.PrefetchScalarGridSpec(num...  17.8 us
    select_n x2, other arithmetic, gather_weights(): jnp.where(core == 0, jnp.concatenate([block, other], axis=2), jnp.concate...  8.81 us
  transfers between devices with their start and end apart: 57, of which 29 were waited for; matrix products, arithmetic and copies ran while one was open for 14% of the time, Pallas kernels for 5%

profile of v1, /device:TPU:16, one launch (start us, length us, event | category | flops | bytes accessed | tf_op | source)
XLA Modules:
  0.0 343.0 jit_solution(1425956817464880431)
XLA Ops:
  7.1 1.5 collective-permute-start.4
  10.7 3.3 collective-permute-start.15
  14.2 2.0 collective-permute-done.15
  16.2 2.0 collective-permute-start.16
  18.2 2.2 collective-permute-start.17
  20.4 1.8 collective-permute-start.18
  22.3 2.8 collective-permute-done.16
  25.1 2.0 collective-permute-done.18
  27.0 1.6 collective-permute-start.19
  29.6 2.4 collective-permute-start.6
  31.9 1.7 collective-permute-start.20
  35.0 1.8 collective-permute-start.21
  37.2 6.4 %collective-permute-done.19 = bf16[2,128,1152]{2,1,0:T(8,128)(2,1)S(1)} collective-permute-done((bf16[2,128,1152]{2,1,0:T(8,128)(2,1)S(1)}, bf16[2,128,1152]{2,1,0:T(8,128)(2,1)S(1)}, u32[]{:S(2)}, u32[]{:S(2)}) %collective-permute-start.19) | collective-permute-done | bytes 589856 | tf_op jit(solution)/shard_map/ppermute | solution.py:655
  43.6 1.8 collective-permute-start.7
  45.5 9.8 %collective-permute-done.20 = bf16[2,128,1152]{2,1,0:T(8,128)(2,1)S(1)} collective-permute-done((bf16[2,128,1152]{2,1,0:T(8,128)(2,1)S(1)}, bf16[2,128,1152]{2,1,0:T(8,128)(2,1)S(1)}, u32[]{:S(2)}, u32[]{:S(2)}) %collective-permute-start.20) | collective-permute-done | bytes 589856 | tf_op jit(solution)/shard_map/ppermute | solution.py:655
  57.4 2.7 collective-permute-start.8
  61.9 1.7 collective-permute-start
  63.5 1.5 collective-permute-start.10
  66.1 2.3 collective-permute-done.8
  70.7 4.4 %collective-permute-done.10 = bf16[2,128,512]{2,1,0:T(8,128)(2,1)S(1)} collective-permute-done((bf16[2,128,512]{2,1,0:T(8,128)(2,1)}, bf16[2,128,512]{2,1,0:T(8,128)(2,1)S(1)}, u32[]{:S(2)}, u32[]{:S(2)}) %collective-permute-start.10) | collective-permute-done | bytes 262176 | tf_op jit(solution)/shard_map/ppermute | solution.py:655
  77.2 1.8 broadcast_divide_fusion.mixing
  83.2 3.6 %maximum_select_fusion.1.weights.out_weights = bf16[2,512,1024]{2,1,0:T(8,128)(2,1)} fusion(bf16[2,512,512]{2,1,0:T(8,128)(2,1)} %collective-permute-done.11, bf16[2,512,512]{2,1,0:T(8,128)(2,1)S(1)} %constant_dynamic-update-slice_fusion.8, pred[]{:T(512)S(6)} %eq.76), kind=kLoop, calls=%fused_computation.2 | loop fusion | flops 9437184 | bytes 4194305 | tf_op jit(solution)/shard_map/jit(_where)/select_n | solution.py:680
  86.8 17.8 %attend_forward.1 = (bf16[3,1536,256]{2,1,0:T(8,128)(2,1)}, bf16[3,512,256]{2,1,0:T(8,128)(2,1)}, f32[3,8,256]{2,1,0:T(8,128)}) custom-call(s32[4]{0:T(128)} %pad_add_fusion.info, f32[8]{0:T(128)} %pad_maximum_fusion.2.slopes, f32[3,2,256,512]{3,2,1,0:T(8,128)} %frames.5, f32[2,512]{1,0:T(2,128)} %norm.3, ...), custom_call_target="tpu_custom_call" | custom-call | flops 1207959552 | bytes 8388608 | tf_op jit(solution)/shard_map/attend_forward/pallas_call | solution.py:460
  104.7 5.2 %maximum_select_fusion.weights = bf16[2,512,2304]{2,1,0:T(8,128)(2,1)} fusion(bf16[2,512,1152]{2,1,0:T(8,128)(2,1)} %collective-permute-done.22, bf16[2,512,1152]{2,1,0:T(8,128)(2,1)S(1)} %constant_dynamic-update-slice_fusion, pred[]{:T(512)S(6)} %eq.76), kind=kLoop, calls=%fused_computation | loop fusion | flops 21233664 | bytes 9437185 | tf_op jit(solution)/shard_map/jit(_where)/select_n | solution.py:680
  109.9 59.0 %mixer_both.1 = (bf16[3,256,512]{2,1,0:T(8,128)(2,1)}, f32[3,256,512]{2,1,0:T(8,128)}, f32[3,256,512]{2,1,0:T(8,128)}, bf16[2,512,2304]{2,1,0:T(8,128)(2,1)}, f32[40,1536]{1,0:T(8,128)}, /*index=5*/f32[8,512]{1,0:T(8,128)}) custom-call(s32[4]{0:T(128)} %pad_add_fusion.info, f32[2]{0:T(128)} %broadcast_divide_fusion.mixing, f32[3,2,256,512]{3,2,1,0:T(8,128)} %frames.5, ...), custom_call_target="tpu_custom_call" | custom-call | flops 10871635968 | bytes 20971520 | tf_op jit(solution)/shard_map/mixer_both/pallas_call | solution.py:497
  170.6 24.4 %attend_backward.1 = (bf16[3,256,512]{2,1,0:T(8,128)(2,1)}, bf16[2,512,1024]{2,1,0:T(8,128)(2,1)}, f32[8,512]{1,0:T(8,128)}, f32[8,256]{1,0:T(8,128)}) custom-call(s32[4]{0:T(128)} %pad_add_fusion.info, f32[8]{0:T(128)} %pad_maximum_fusion.2.slopes, f32[2]{0:T(128)} %broadcast_divide_fusion.mixing, f32[3,2,256,512]{3,2,1,0:T(8,128)} %frames.5, ...), custom_call_target="tpu_custom_call" | custom-call | flops 3623878656 | bytes 20971520 | tf_op jit(solution)/shard_map/attend_backward/pallas_call | solution.py:579
  199.3 1.8 collective-permute-start.27
  201.2 1.4 collective-permute-start.28
  202.6 5.7 %collective-permute-done.26 = f32[58368]{0:T(1024)S(1)} collective-permute-done((f32[58368]{0:T(1024)S(1)}, f32[58368]{0:T(1024)S(1)}, u32[]{:S(2)}, u32[]{:S(2)}) %collective-permute-start.26) | collective-permute-done | bytes 233504 | tf_op jit(solution)/shard_map/ppermute | solution.py:655
  208.2 4.4 %collective-permute-done.27 = f32[58368]{0:T(1024)S(1)} collective-permute-done((f32[58368]{0:T(1024)S(1)}, f32[58368]{0:T(1024)S(1)}, u32[]{:S(2)}, u32[]{:S(2)}) %collective-permute-start.27) | collective-permute-done | bytes 233504 | tf_op jit(solution)/shard_map/ppermute | solution.py:655
  212.7 1.4 collective-permute-start.29
  214.9 2.4 collective-permute-start.31
  217.3 2.0 constant_dynamic-slice_fusion.9
  219.4 1.5 collective-permute-start.24
  221.0 2.1 collective-permute-done.29
  223.1 1.7 collective-permute-start.23
  224.8 2.4 collective-permute-done.30
  227.2 3.0 collective-permute-start.32
  230.9 9.0 %collective-permute-done.24 = bf16[3,256,512]{2,1,0:T(8,128)(2,1)S(1)} collective-permute-done((bf16[3,256,512]{2,1,0:T(8,128)(2,1)S(1)}, bf16[3,256,512]{2,1,0:T(8,128)(2,1)S(1)}, u32[]{:S(2)}, u32[]{:S(2)}) %collective-permute-start.24) | collective-permute-done | bytes 786464 | tf_op jit(solution)/shard_map/ppermute | solution.py:655
  239.9 1.9 collective-permute-start.34
  242.0 2.0 copy.36
  244.1 12.7 %collective-permute-done.23 = bf16[3,256,512]{2,1,0:T(8,128)(2,1)S(1)} collective-permute-done((bf16[3,256,512]{2,1,0:T(8,128)(2,1)S(1)}, bf16[3,256,512]{2,1,0:T(8,128)(2,1)S(1)}, u32[]{:S(2)}, u32[]{:S(2)}) %collective-permute-start.23) | collective-permute-done | bytes 786464 | tf_op jit(solution)/shard_map/ppermute | solution.py:655
  257.0 2.0 copy.35
  259.0 4.0 %collective-permute-done.32 = f32[58368]{0:T(1024)S(1)} collective-permute-done((f32[58368]{0:T(1024)S(1)}, f32[58368]{0:T(1024)S(1)}, u32[]{:S(2)}, u32[]{:S(2)}) %collective-permute-start.32) | collective-permute-done | bytes 233504 | tf_op jit(solution)/shard_map/ppermute | solution.py:655
  263.0 2.1 collective-permute-done.33
  267.7 1.9 collective-permute-start.36
  270.7 2.2 collective-permute-start.38
  273.6 1.9 multiply_reduce_fusion
  275.5 3.3 collective-permute-done.36
  278.8 4.2 %collective-permute-done.37 = bf16[2,128,512]{2,1,0:T(8,128)(2,1)} collective-permute-done((bf16[2,128,512]{2,1,0:T(8,128)(2,1)}, bf16[2,128,512]{2,1,0:T(8,128)(2,1)}, u32[]{:S(2)}, u32[]{:S(2)}) %collective-permute-start.37) | collective-permute-done | bytes 262176 | tf_op jit(solution)/shard_map/ppermute | solution.py:655
  286.3 2.9 add_convert_fusion
  290.5 1.9 collective-permute-start.47
  293.4 2.1 collective-permute-start.49
  295.6 2.5 subtract_multiply_fusion
  301.9 3.2 collective-permute-start.41
  305.8 1.8 collective-permute-done.40
  308.5 3.0 collective-permute-start.42
  313.5 6.4 %collective-permute-done.48 = bf16[2,128,1152]{2,1,0:T(8,128)(2,1)} collective-permute-done((bf16[2,128,1152]{2,1,0:T(8,128)(2,1)}, bf16[2,128,1152]{2,1,0:T(8,128)(2,1)}, u32[]{:S(2)}, u32[]{:S(2)}) %collective-permute-start.48) | collective-permute-done | bytes 589856 | tf_op jit(solution)/shard_map/ppermute | solution.py:655
  319.9 1.8 add_convert_fusion.2
  321.7 2.4 collective-permute-start.50
  324.1 3.2 collective-permute-start.52
  327.3 2.7 collective-permute-done.50
  330.0 2.2 collective-permute-done.51
  332.4 3.0 collective-permute-start.53
  (194 shorter events, 58.7 us)
Async XLA Ops:
  0.6 74.7 %copy-start = (s32[3,2]{0,1:T(2,128)S(1)}, s32[3,2]{0,1:T(2,128)}, u32[]{:S(2)}) copy-start(s32[3,2]{0,1:T(2,128)} %param.32) | copy-start | bytes 76
  2.1 6.4 %collective-permute-start.12 = (bf16[8,2304]{1,0:T(8,128)(2,1)S(1)}, bf16[8,2304]{1,0:T(8,128)(2,1)S(1)}, u32[]{:S(2)}, u32[]{:S(2)}) collective-permute-start(bf16[8,2304]{1,0:T(8,128)(2,1)S(1)} %constant_dynamic-update-slice_fusion.20), channel_id=1, source_target_pairs={{0,1},{1,0},{4,5},{5,4},{8,9},{9,8},{12,13},{13,12},{64,65},{65,64... | collective-permute-start | bytes 110600 | tf_op jit(solution)/shard_map/ppermute | solution.py:655
  2.9 1.3 collective-permute-start.1
  5.0 4.7 %collective-permute-start.2 = (bf16[16,512]{1,0:T(8,128)(2,1)S(1)}, bf16[16,512]{1,0:T(8,128)(2,1)S(1)}, u32[]{:S(2)}, u32[]{:S(2)}) collective-permute-start(bf16[16,512]{1,0:T(8,128)(2,1)S(1)} %get-tuple-element.71), channel_id=1, source_target_pairs={{0,64},{1,65},{4,68},{5,69},{8,72},{9,73},{12,76},{13,77},{64,2},{... | collective-permute-start | bytes 49160 | tf_op jit(solution)/shard_map/ppermute | solution.py:655
  6.4 22.3 %collective-permute-start.3 = (bf16[16,512]{1,0:T(8,128)(2,1)S(1)}, bf16[16,512]{1,0:T(8,128)(2,1)S(1)}, u32[]{:S(2)}, u32[]{:S(2)}) collective-permute-start(bf16[16,512]{1,0:T(8,128)(2,1)S(1)} %get-tuple-element.71), channel_id=1, source_target_pairs={{0,66},{1,67},{4,70},{5,71},{8,74},{9,75},{12,78},{13,79},{64,0},{... | collective-permute-start | bytes 49160 | tf_op jit(solution)/shard_map/ppermute | solution.py:655
  7.1 21.5 %collective-permute-start.4 = (bf16[16,512]{1,0:T(8,128)(2,1)S(1)}, bf16[16,512]{1,0:T(8,128)(2,1)S(1)}, u32[]{:S(2)}, u32[]{:S(2)}) collective-permute-start(bf16[16,512]{1,0:T(8,128)(2,1)S(1)} %get-tuple-element.71), channel_id=1, source_target_pairs={{0,2},{1,3},{4,6},{5,7},{8,10},{9,11},{12,14},{13,15},{64,66},{65,... | collective-permute-start | bytes 49160 | tf_op jit(solution)/shard_map/ppermute | solution.py:655
  8.6 5.4 %collective-permute-start.13 = (bf16[16,1152]{1,0:T(8,128)(2,1)S(1)}, bf16[16,1152]{1,0:T(8,128)(2,1)S(1)}, u32[]{:S(2)}, u32[]{:S(2)}) collective-permute-start(bf16[16,1152]{1,0:T(8,128)(2,1)S(1)} %get-tuple-element.69), channel_id=1, source_target_pairs={{0,64},{1,65},{4,68},{5,69},{8,72},{9,73},{12,76},{13,77},{64,2},{... | collective-permute-start | bytes 110600 | tf_op jit(solution)/shard_map/ppermute | solution.py:655
  9.7 4.4 %collective-permute-start.14 = (bf16[16,1152]{1,0:T(8,128)(2,1)S(1)}, bf16[16,1152]{1,0:T(8,128)(2,1)S(1)}, u32[]{:S(2)}, u32[]{:S(2)}) collective-permute-start(bf16[16,1152]{1,0:T(8,128)(2,1)S(1)} %get-tuple-element.69), channel_id=1, source_target_pairs={{0,66},{1,67},{4,70},{5,71},{8,74},{9,75},{12,78},{13,79},{64,0},{... | collective-permute-start | bytes 110600 | tf_op jit(solution)/shard_map/ppermute | solution.py:655
  10.7 5.5 %collective-permute-start.15 = (bf16[16,1152]{1,0:T(8,128)(2,1)S(1)}, bf16[16,1152]{1,0:T(8,128)(2,1)S(1)}, u32[]{:S(2)}, u32[]{:S(2)}) collective-permute-start(bf16[16,1152]{1,0:T(8,128)(2,1)S(1)} %get-tuple-element.69), channel_id=1, source_target_pairs={{0,2},{1,3},{4,6},{5,7},{8,10},{9,11},{12,14},{13,15},{64,66},{65,... | collective-permute-start | bytes 110600 | tf_op jit(solution)/shard_map/ppermute | solution.py:655
  16.2 8.8 %collective-permute-start.16 = (bf16[2,32,1152]{2,1,0:T(8,128)(2,1)S(1)}, bf16[2,32,1152]{2,1,0:T(8,128)(2,1)S(1)}, u32[]{:S(2)}, u32[]{:S(2)}) collective-permute-start(bf16[2,32,1152]{2,1,0:T(8,128)(2,1)S(1)} %bitcast.72), channel_id=1, source_target_pairs={{0,4},{1,5},{4,8},{5,9},{8,12},{9,13},{12,0},{13,1},{64,68},{65,69... | collective-permute-start | bytes 442376 | tf_op jit(solution)/shard_map/ppermute | solution.py:655
  18.2 6.8 %collective-permute-start.17 = (bf16[2,32,1152]{2,1,0:T(8,128)(2,1)S(1)}, bf16[2,32,1152]{2,1,0:T(8,128)(2,1)S(1)}, u32[]{:S(2)}, u32[]{:S(2)}) collective-permute-start(bf16[2,32,1152]{2,1,0:T(8,128)(2,1)S(1)} %bitcast.73), channel_id=1, source_target_pairs={{0,12},{1,13},{4,0},{5,1},{8,4},{9,5},{12,8},{13,9},{64,76},{65,77... | collective-permute-start | bytes 442376 | tf_op jit(solution)/shard_map/ppermute | solution.py:655
  20.4 6.6 %collective-permute-start.18 = (bf16[2,32,1152]{2,1,0:T(8,128)(2,1)S(1)}, bf16[2,32,1152]{2,1,0:T(8,128)(2,1)S(1)}, u32[]{:S(2)}, u32[]{:S(2)}) collective-permute-start(bf16[2,32,1152]{2,1,0:T(8,128)(2,1)S(1)} %bitcast.74), channel_id=1, source_target_pairs={{0,8},{1,9},{4,12},{5,13},{8,0},{9,1},{12,4},{13,5},{64,72},{65,73... | collective-permute-start | bytes 442376 | tf_op jit(solution)/shard_map/ppermute | solution.py:655
  27.0 16.6 %collective-permute-start.19 = (bf16[2,128,1152]{2,1,0:T(8,128)(2,1)S(1)}, bf16[2,128,1152]{2,1,0:T(8,128)(2,1)S(1)}, u32[]{:S(2)}, u32[]{:S(2)}) collective-permute-start(bf16[2,128,1152]{2,1,0:T(8,128)(2,1)S(1)} %constant_dynamic-update-slice_fusion.4), channel_id=1, source_target_pairs={{0,16},{1,17},{4,20},{5,21},{8,24},{9,25},{12,28},{13,29},{64,80},... | collective-permute-start | bytes 1769480 | tf_op jit(solution)/shard_map/ppermute | solution.py:655
  28.6 26.9 %collective-permute-start.5 = (bf16[2,32,512]{2,1,0:T(8,128)(2,1)S(1)}, bf16[2,32,512]{2,1,0:T(8,128)(2,1)S(1)}, u32[]{:S(2)}, u32[]{:S(2)}) collective-permute-start(bf16[2,32,512]{2,1,0:T(8,128)(2,1)S(1)} %bitcast.78), channel_id=1, source_target_pairs={{0,4},{1,5},{4,8},{5,9},{8,12},{9,13},{12,0},{13,1},{64,68},{65,69... | collective-permute-start | bytes 196616 | tf_op jit(solution)/shard_map/ppermute | solution.py:655
  29.6 26.6 %collective-permute-start.6 = (bf16[2,32,512]{2,1,0:T(8,128)(2,1)S(1)}, bf16[2,32,512]{2,1,0:T(8,128)(2,1)S(1)}, u32[]{:S(2)}, u32[]{:S(2)}) collective-permute-start(bf16[2,32,512]{2,1,0:T(8,128)(2,1)S(1)} %bitcast.79), channel_id=1, source_target_pairs={{0,12},{1,13},{4,0},{5,1},{8,4},{9,5},{12,8},{13,9},{64,76},{65,77... | collective-permute-start | bytes 196616 | tf_op jit(solution)/shard_map/ppermute | solution.py:655
  31.9 23.3 %collective-permute-start.20 = (bf16[2,128,1152]{2,1,0:T(8,128)(2,1)S(1)}, bf16[2,128,1152]{2,1,0:T(8,128)(2,1)S(1)}, u32[]{:S(2)}, u32[]{:S(2)}) collective-permute-start(bf16[2,128,1152]{2,1,0:T(8,128)(2,1)S(1)} %constant_dynamic-update-slice_fusion.4), channel_id=1, source_target_pairs={{0,48},{1,49},{4,52},{5,53},{8,56},{9,57},{12,60},{13,61},{64,112}... | collective-permute-start | bytes 1769480 | tf_op jit(solution)/shard_map/ppermute | solution.py:655
  35.0 20.3 %collective-permute-start.21 = (bf16[2,128,1152]{2,1,0:T(8,128)(2,1)S(1)}, bf16[2,128,1152]{2,1,0:T(8,128)(2,1)S(1)}, u32[]{:S(2)}, u32[]{:S(2)}) collective-permute-start(bf16[2,128,1152]{2,1,0:T(8,128)(2,1)S(1)} %constant_dynamic-update-slice_fusion.4), channel_id=1, source_target_pairs={{0,32},{1,33},{4,36},{5,37},{8,40},{9,41},{12,44},{13,45},{64,96},... | collective-permute-start | bytes 1769480 | tf_op jit(solution)/shard_map/ppermute | solution.py:655
  37.0 23.1 %copy-start.13 = (f32[4]{0:T(128)S(1)}, f32[4]{0:T(128)}, u32[]{:S(2)}) copy-start(f32[4]{0:T(128)} %param.23) | copy-start | bytes 52
  37.0 23.1 %copy-start.12 = (f32[768]{0:T(1024)S(1)}, f32[768]{0:T(1024)}, u32[]{:S(2)}) copy-start(f32[768]{0:T(1024)} %param.28) | copy-start | bytes 9220
  37.1 24.2 %copy-start.7 = (f32[31,768]{1,0:T(8,128)S(1)}, f32[31,768]{1,0:T(8,128)}, u32[]{:S(2)}) copy-start(f32[31,768]{1,0:T(8,128)} %param.27) | copy-start | bytes 285700
  37.1 24.1 %copy-start.8 = (f32[2,768]{1,0:T(2,128)S(1)}, f32[2,768]{1,0:T(2,128)}, u32[]{:S(2)}) copy-start(f32[2,768]{1,0:T(2,128)} %param.26) | copy-start | bytes 18436
  43.6 13.2 %collective-permute-start.7 = (bf16[2,32,512]{2,1,0:T(8,128)(2,1)S(1)}, bf16[2,32,512]{2,1,0:T(8,128)(2,1)S(1)}, u32[]{:S(2)}, u32[]{:S(2)}) collective-permute-start(bf16[2,32,512]{2,1,0:T(8,128)(2,1)S(1)} %bitcast.81), channel_id=1, source_target_pairs={{0,8},{1,9},{4,12},{5,13},{8,0},{9,1},{12,4},{13,5},{64,72},{65,73... | collective-permute-start | bytes 196616 | tf_op jit(solution)/shard_map/ppermute | solution.py:655
  55.3 20.1 %copy-start.10 = (f32[2]{0:T(128)S(1)}, f32[2]{0:T(128)}, u32[]{:S(2)}) copy-start(f32[2]{0:T(128)} %param.30) | copy-start | bytes 28
  55.4 49.3 %collective-permute-start.22 = (bf16[2,512,1152]{2,1,0:T(8,128)(2,1)S(1)}, bf16[2,512,1152]{2,1,0:T(8,128)(2,1)}, u32[]{:S(2)}, u32[]{:S(2)}) collective-permute-start(bf16[2,512,1152]{2,1,0:T(8,128)(2,1)S(1)} %constant_dynamic-update-slice_fusion), channel_id=1, source_target_pairs={{0,1},{1,0},{4,5},{5,4},{8,9},{9,8},{12,13},{13,12},{64,65},{65,64... | collective-permute-start | bytes 7077896 | tf_op jit(solution)/shard_map/ppermute | solution.py:655
  57.4 10.9 %collective-permute-start.8 = (bf16[2,128,512]{2,1,0:T(8,128)(2,1)}, bf16[2,128,512]{2,1,0:T(8,128)(2,1)}, u32[]{:S(2)}, u32[]{:S(2)}) collective-permute-start(bf16[2,128,512]{2,1,0:T(8,128)(2,1)} %constant_dynamic-update-slice_fusion.12), channel_id=1, source_target_pairs={{0,16},{1,17},{4,20},{5,21},{8,24},{9,25},{12,28},{13,29},{64,80},... | collective-permute-start | bytes 786440 | tf_op jit(solution)/shard_map/ppermute | solution.py:655
  60.2 9.5 %collective-permute-start.9 = (bf16[2,128,512]{2,1,0:T(8,128)(2,1)}, bf16[2,128,512]{2,1,0:T(8,128)(2,1)}, u32[]{:S(2)}, u32[]{:S(2)}) collective-permute-start(bf16[2,128,512]{2,1,0:T(8,128)(2,1)} %constant_dynamic-update-slice_fusion.12), channel_id=1, source_target_pairs={{0,48},{1,49},{4,52},{5,53},{8,56},{9,57},{12,60},{13,61},{64,112}... | collective-permute-start | bytes 786440 | tf_op jit(solution)/shard_map/ppermute | solution.py:655
  61.9 17.8 %collective-permute-start = (f32[35,768]{1,0:T(8,128)}, f32[35,768]{1,0:T(8,128)}, u32[]{:S(2)}, u32[]{:S(2)}) collective-permute-start(f32[35,768]{1,0:T(8,128)} %pad_maximum_fusion), channel_id=1, source_target_pairs={{0,64},{1,65},{4,68},{5,69},{8,72},{9,73},{12,76},{13,77},{64,0},{... | collective-permute-start | bytes 322568 | tf_op jit(solution)/shard_map/ppermute | solution.py:655
  63.5 11.5 %collective-permute-start.10 = (bf16[2,128,512]{2,1,0:T(8,128)(2,1)}, bf16[2,128,512]{2,1,0:T(8,128)(2,1)S(1)}, u32[]{:S(2)}, u32[]{:S(2)}) collective-permute-start(bf16[2,128,512]{2,1,0:T(8,128)(2,1)} %constant_dynamic-update-slice_fusion.12), channel_id=1, source_target_pairs={{0,32},{1,33},{4,36},{5,37},{8,40},{9,41},{12,44},{13,45},{64,96},... | collective-permute-start | bytes 786440 | tf_op jit(solution)/shard_map/ppermute | solution.py:655
  75.1 8.2 %collective-permute-start.11 = (bf16[2,512,512]{2,1,0:T(8,128)(2,1)S(1)}, bf16[2,512,512]{2,1,0:T(8,128)(2,1)}, u32[]{:S(2)}, u32[]{:S(2)}) collective-permute-start(bf16[2,512,512]{2,1,0:T(8,128)(2,1)S(1)} %constant_dynamic-update-slice_fusion.8), channel_id=1, source_target_pairs={{0,1},{1,0},{4,5},{5,4},{8,9},{9,8},{12,13},{13,12},{64,65},{65,64... | collective-permute-start | bytes 3145736 | tf_op jit(solution)/shard_map/ppermute | solution.py:655
  196.4 1.7 collective-permute-start.25
  198.1 10.2 %collective-permute-start.26 = (f32[58368]{0:T(1024)S(1)}, f32[58368]{0:T(1024)S(1)}, u32[]{:S(2)}, u32[]{:S(2)}) collective-permute-start(f32[58368]{0:T(1024)S(1)} %add.477), channel_id=1, source_target_pairs={{0,32},{1,33},{4,36},{5,37},{8,40},{9,41},{12,44},{13,45},{64,96},... | collective-permute-start | bytes 700424 | tf_op jit(solution)/shard_map/ppermute | solution.py:655
  199.3 13.3 %collective-permute-start.27 = (f32[58368]{0:T(1024)S(1)}, f32[58368]{0:T(1024)S(1)}, u32[]{:S(2)}, u32[]{:S(2)}) collective-permute-start(f32[58368]{0:T(1024)S(1)} %add.477), channel_id=1, source_target_pairs={{0,16},{1,17},{4,20},{5,21},{8,24},{9,25},{12,28},{13,29},{64,80},... | collective-permute-start | bytes 700424 | tf_op jit(solution)/shard_map/ppermute | solution.py:655
  201.2 11.5 %collective-permute-start.28 = (f32[58368]{0:T(1024)S(1)}, f32[58368]{0:T(1024)S(1)}, u32[]{:S(2)}, u32[]{:S(2)}) collective-permute-start(f32[58368]{0:T(1024)S(1)} %add.477), channel_id=1, source_target_pairs={{0,48},{1,49},{4,52},{5,53},{8,56},{9,57},{12,60},{13,61},{64,112}... | collective-permute-start | bytes 700424 | tf_op jit(solution)/shard_map/ppermute | solution.py:655
  212.7 10.4 %collective-permute-start.29 = (f32[58368]{0:T(1024)S(1)}, f32[58368]{0:T(1024)S(1)}, u32[]{:S(2)}, u32[]{:S(2)}) collective-permute-start(f32[58368]{0:T(1024)S(1)} %add_add_fusion.2), channel_id=1, source_target_pairs={{0,8},{1,9},{4,12},{5,13},{8,0},{9,1},{12,4},{13,5},{64,72},{65,73... | collective-permute-start | bytes 700424 | tf_op jit(solution)/shard_map/ppermute | solution.py:655
  214.1 13.1 %collective-permute-start.30 = (f32[58368]{0:T(1024)S(1)}, f32[58368]{0:T(1024)S(1)}, u32[]{:S(2)}, u32[]{:S(2)}) collective-permute-start(f32[58368]{0:T(1024)S(1)} %add_add_fusion.2), channel_id=1, source_target_pairs={{0,4},{1,5},{4,8},{5,9},{8,12},{9,13},{12,0},{13,1},{64,68},{65,69... | collective-permute-start | bytes 700424 | tf_op jit(solution)/shard_map/ppermute | solution.py:655
  214.9 12.3 %collective-permute-start.31 = (f32[58368]{0:T(1024)S(1)}, f32[58368]{0:T(1024)S(1)}, u32[]{:S(2)}, u32[]{:S(2)}) collective-permute-start(f32[58368]{0:T(1024)S(1)} %add_add_fusion.2), channel_id=1, source_target_pairs={{0,12},{1,13},{4,0},{5,1},{8,4},{9,5},{12,8},{13,9},{64,76},{65,77... | collective-permute-start | bytes 700424 | tf_op jit(solution)/shard_map/ppermute | solution.py:655
  219.3 66.9 %collective-permute-start.46 = (bf16[2,512,1152]{2,1,0:T(8,128)(2,1)S(1)}, bf16[2,512,1152]{2,1,0:T(8,128)(2,1)}, u32[]{:S(2)}, u32[]{:S(2)}) collective-permute-start(bf16[2,512,1152]{2,1,0:T(8,128)(2,1)S(1)} %constant_dynamic-slice_fusion.9), channel_id=1, source_target_pairs={{0,1},{1,0},{4,5},{5,4},{8,9},{9,8},{12,13},{13,12},{64,65},{65,64... | collective-permute-start | bytes 7077896 | tf_op jit(solution)/shard_map/ppermute | solution.py:655
  219.4 20.4 %collective-permute-start.24 = (bf16[3,256,512]{2,1,0:T(8,128)(2,1)S(1)}, bf16[3,256,512]{2,1,0:T(8,128)(2,1)S(1)}, u32[]{:S(2)}, u32[]{:S(2)}) collective-permute-start(bf16[3,256,512]{2,1,0:T(8,128)(2,1)S(1)} %copy-done.6), channel_id=1, source_target_pairs={{0,64},{1,65},{4,68},{5,69},{8,72},{9,73},{12,76},{13,77},{64,0},{... | collective-permute-start | bytes 2359304 | tf_op jit(solution)/shard_map/ppermute | solution.py:655
  223.1 33.6 %collective-permute-start.23 = (bf16[3,256,512]{2,1,0:T(8,128)(2,1)S(1)}, bf16[3,256,512]{2,1,0:T(8,128)(2,1)S(1)}, u32[]{:S(2)}, u32[]{:S(2)}) collective-permute-start(bf16[3,256,512]{2,1,0:T(8,128)(2,1)S(1)} %copy-done.5), channel_id=1, source_target_pairs={{0,64},{1,65},{4,68},{5,69},{8,72},{9,73},{12,76},{13,77},{64,0},{... | collective-permute-start | bytes 2359304 | tf_op jit(solution)/shard_map/ppermute | solution.py:655
  227.2 35.8 %collective-permute-start.32 = (f32[58368]{0:T(1024)S(1)}, f32[58368]{0:T(1024)S(1)}, u32[]{:S(2)}, u32[]{:S(2)}) collective-permute-start(f32[58368]{0:T(1024)S(1)} %add_add_fusion.1), channel_id=1, source_target_pairs={{0,2},{1,3},{4,6},{5,7},{8,10},{9,11},{12,14},{13,15},{64,66},{65,... | collective-permute-start | bytes 700424 | tf_op jit(solution)/shard_map/ppermute | solution.py:655
  230.2 35.0 %collective-permute-start.33 = (f32[58368]{0:T(1024)S(1)}, f32[58368]{0:T(1024)S(1)}, u32[]{:S(2)}, u32[]{:S(2)}) collective-permute-start(f32[58368]{0:T(1024)S(1)} %add_add_fusion.1), channel_id=1, source_target_pairs={{0,64},{1,65},{4,68},{5,69},{8,72},{9,73},{12,76},{13,77},{64,2},{... | collective-permute-start | bytes 700424 | tf_op jit(solution)/shard_map/ppermute | solution.py:655
  239.9 26.4 %collective-permute-start.34 = (f32[58368]{0:T(1024)S(1)}, f32[58368]{0:T(1024)S(1)}, u32[]{:S(2)}, u32[]{:S(2)}) collective-permute-start(f32[58368]{0:T(1024)S(1)} %add_add_fusion.1), channel_id=1, source_target_pairs={{0,66},{1,67},{4,70},{5,71},{8,74},{9,75},{12,78},{13,79},{64,0},{... | collective-permute-start | bytes 700424 | tf_op jit(solution)/shard_map/ppermute | solution.py:655
  256.7 9.6 %collective-permute-start.35 = (bf16[2,512,512]{2,1,0:T(8,128)(2,1)S(1)}, bf16[2,512,512]{2,1,0:T(8,128)(2,1)S(1)}, u32[]{:S(2)}, u32[]{:S(2)}) collective-permute-start(bf16[2,512,512]{2,1,0:T(8,128)(2,1)S(1)} %constant_dynamic-slice_fusion.22), channel_id=1, source_target_pairs={{0,1},{1,0},{4,5},{5,4},{8,9},{9,8},{12,13},{13,12},{64,65},{65,64... | collective-permute-start | bytes 3145736 | tf_op jit(solution)/shard_map/ppermute | solution.py:655
  267.7 11.1 %collective-permute-start.36 = (bf16[2,128,512]{2,1,0:T(8,128)(2,1)}, bf16[2,128,512]{2,1,0:T(8,128)(2,1)}, u32[]{:S(2)}, u32[]{:S(2)}) collective-permute-start(bf16[2,128,512]{2,1,0:T(8,128)(2,1)} %get-tuple-element.75), channel_id=1, source_target_pairs={{0,32},{1,33},{4,36},{5,37},{8,40},{9,41},{12,44},{13,45},{64,96},... | collective-permute-start | bytes 786440 | tf_op jit(solution)/shard_map/ppermute | solution.py:655
  269.6 13.4 %collective-permute-start.37 = (bf16[2,128,512]{2,1,0:T(8,128)(2,1)}, bf16[2,128,512]{2,1,0:T(8,128)(2,1)}, u32[]{:S(2)}, u32[]{:S(2)}) collective-permute-start(bf16[2,128,512]{2,1,0:T(8,128)(2,1)} %get-tuple-element.77), channel_id=1, source_target_pairs={{0,16},{1,17},{4,20},{5,21},{8,24},{9,25},{12,28},{13,29},{64,80},... | collective-permute-start | bytes 786440 | tf_op jit(solution)/shard_map/ppermute | solution.py:655
  270.7 12.3 %collective-permute-start.38 = (bf16[2,128,512]{2,1,0:T(8,128)(2,1)}, bf16[2,128,512]{2,1,0:T(8,128)(2,1)}, u32[]{:S(2)}, u32[]{:S(2)}) collective-permute-start(bf16[2,128,512]{2,1,0:T(8,128)(2,1)} %get-tuple-element.76), channel_id=1, source_target_pairs={{0,48},{1,49},{4,52},{5,53},{8,56},{9,57},{12,60},{13,61},{64,112}... | collective-permute-start | bytes 786440 | tf_op jit(solution)/shard_map/ppermute | solution.py:655
  285.0 16.9 %collective-permute-start.39 = (bf16[2,32,512]{2,1,0:T(8,128)(2,1)}, bf16[2,32,512]{2,1,0:T(8,128)(2,1)S(1)}, u32[]{:S(2)}, u32[]{:S(2)}) collective-permute-start(bf16[2,32,512]{2,1,0:T(8,128)(2,1)} %get-tuple-element.81), channel_id=1, source_target_pairs={{0,8},{1,9},{4,12},{5,13},{8,0},{9,1},{12,4},{13,5},{64,72},{65,73... | collective-permute-start | bytes 196616 | tf_op jit(solution)/shard_map/ppermute | solution.py:655
  290.5 22.1 %collective-permute-start.47 = (bf16[2,128,1152]{2,1,0:T(8,128)(2,1)}, bf16[2,128,1152]{2,1,0:T(8,128)(2,1)}, u32[]{:S(2)}, u32[]{:S(2)}) collective-permute-start(bf16[2,128,1152]{2,1,0:T(8,128)(2,1)} %get-tuple-element.72), channel_id=1, source_target_pairs={{0,32},{1,33},{4,36},{5,37},{8,40},{9,41},{12,44},{13,45},{64,96},... | collective-permute-start | bytes 1769480 | tf_op jit(solution)/shard_map/ppermute | solution.py:655
  292.4 27.5 %collective-permute-start.48 = (bf16[2,128,1152]{2,1,0:T(8,128)(2,1)}, bf16[2,128,1152]{2,1,0:T(8,128)(2,1)}, u32[]{:S(2)}, u32[]{:S(2)}) collective-permute-start(bf16[2,128,1152]{2,1,0:T(8,128)(2,1)} %get-tuple-element.74), channel_id=1, source_target_pairs={{0,16},{1,17},{4,20},{5,21},{8,24},{9,25},{12,28},{13,29},{64,80},... | collective-permute-start | bytes 1769480 | tf_op jit(solution)/shard_map/ppermute | solution.py:655
  293.4 26.5 %collective-permute-start.49 = (bf16[2,128,1152]{2,1,0:T(8,128)(2,1)S(1)}, bf16[2,128,1152]{2,1,0:T(8,128)(2,1)}, u32[]{:S(2)}, u32[]{:S(2)}) collective-permute-start(bf16[2,128,1152]{2,1,0:T(8,128)(2,1)S(1)} %get-tuple-element.73), channel_id=1, source_target_pairs={{0,48},{1,49},{4,52},{5,53},{8,56},{9,57},{12,60},{13,61},{64,112}... | collective-permute-start | bytes 1769480 | tf_op jit(solution)/shard_map/ppermute | solution.py:655
  301.9 5.7 %collective-permute-start.40 = (bf16[2,32,512]{2,1,0:T(8,128)(2,1)}, bf16[2,32,512]{2,1,0:T(8,128)(2,1)S(1)}, u32[]{:S(2)}, u32[]{:S(2)}) collective-permute-start(bf16[2,32,512]{2,1,0:T(8,128)(2,1)} %get-tuple-element.83), channel_id=1, source_target_pairs={{0,4},{1,5},{4,8},{5,9},{8,12},{9,13},{12,0},{13,1},{64,68},{65,69... | collective-permute-start | bytes 196616 | tf_op jit(solution)/shard_map/ppermute | solution.py:655
  301.9 5.7 %collective-permute-start.41 = (bf16[2,32,512]{2,1,0:T(8,128)(2,1)S(1)}, bf16[2,32,512]{2,1,0:T(8,128)(2,1)S(1)}, u32[]{:S(2)}, u32[]{:S(2)}) collective-permute-start(bf16[2,32,512]{2,1,0:T(8,128)(2,1)S(1)} %get-tuple-element.82), channel_id=1, source_target_pairs={{0,12},{1,13},{4,0},{5,1},{8,4},{9,5},{12,8},{13,9},{64,76},{65,77... | collective-permute-start | bytes 196616 | tf_op jit(solution)/shard_map/ppermute | solution.py:655
  308.5 15.6 %collective-permute-start.42 = (bf16[16,512]{1,0:T(8,128)(2,1)S(1)}, bf16[16,512]{1,0:T(8,128)(2,1)S(1)}, u32[]{:S(2)}, u32[]{:S(2)}) collective-permute-start(bf16[16,512]{1,0:T(8,128)(2,1)S(1)} %get-tuple-element.95), channel_id=1, source_target_pairs={{0,2},{1,3},{4,6},{5,7},{8,10},{9,11},{12,14},{13,15},{64,66},{65,... | collective-permute-start | bytes 49160 | tf_op jit(solution)/shard_map/ppermute | solution.py:655
  311.5 15.9 %collective-permute-start.43 = (bf16[16,512]{1,0:T(8,128)(2,1)S(1)}, bf16[16,512]{1,0:T(8,128)(2,1)S(1)}, u32[]{:S(2)}, u32[]{:S(2)}) collective-permute-start(bf16[16,512]{1,0:T(8,128)(2,1)S(1)} %get-tuple-element.97), channel_id=1, source_target_pairs={{0,64},{1,65},{4,68},{5,69},{8,72},{9,73},{12,76},{13,77},{64,2},{... | collective-permute-start | bytes 49160 | tf_op jit(solution)/shard_map/ppermute | solution.py:655
  312.5 30.5 %copy-start.1 = (s32[3,2]{0,1:T(2,128)S(1)}, s32[3,2]{0,1:T(2,128)}, u32[]{:S(2)}) copy-start(s32[3,2]{0,1:T(2,128)} %param.32) | copy-start | bytes 76
  312.5 14.8 %collective-permute-start.44 = (bf16[16,512]{1,0:T(8,128)(2,1)S(1)}, bf16[16,512]{1,0:T(8,128)(2,1)S(1)}, u32[]{:S(2)}, u32[]{:S(2)}) collective-permute-start(bf16[16,512]{1,0:T(8,128)(2,1)S(1)} %get-tuple-element.96), channel_id=1, source_target_pairs={{0,66},{1,67},{4,70},{5,71},{8,74},{9,75},{12,78},{13,79},{64,0},{... | collective-permute-start | bytes 49160 | tf_op jit(solution)/shard_map/ppermute | solution.py:655
  321.7 8.3 %collective-permute-start.50 = (bf16[2,32,1152]{2,1,0:T(8,128)(2,1)S(1)}, bf16[2,32,1152]{2,1,0:T(8,128)(2,1)S(1)}, u32[]{:S(2)}, u32[]{:S(2)}) collective-permute-start(bf16[2,32,1152]{2,1,0:T(8,128)(2,1)S(1)} %get-tuple-element.78), channel_id=1, source_target_pairs={{0,8},{1,9},{4,12},{5,13},{8,0},{9,1},{12,4},{13,5},{64,72},{65,73... | collective-permute-start | bytes 442376 | tf_op jit(solution)/shard_map/ppermute | solution.py:655
  324.1 8.1 %collective-permute-start.51 = (bf16[2,32,1152]{2,1,0:T(8,128)(2,1)S(1)}, bf16[2,32,1152]{2,1,0:T(8,128)(2,1)S(1)}, u32[]{:S(2)}, u32[]{:S(2)}) collective-permute-start(bf16[2,32,1152]{2,1,0:T(8,128)(2,1)S(1)} %get-tuple-element.80), channel_id=1, source_target_pairs={{0,4},{1,5},{4,8},{5,9},{8,12},{9,13},{12,0},{13,1},{64,68},{65,69... | collective-permute-start | bytes 442376 | tf_op jit(solution)/shard_map/ppermute | solution.py:655
  324.1 8.1 %collective-permute-start.52 = (bf16[2,32,1152]{2,1,0:T(8,128)(2,1)S(1)}, bf16[2,32,1152]{2,1,0:T(8,128)(2,1)S(1)}, u32[]{:S(2)}, u32[]{:S(2)}) collective-permute-start(bf16[2,32,1152]{2,1,0:T(8,128)(2,1)S(1)} %get-tuple-element.79), channel_id=1, source_target_pairs={{0,12},{1,13},{4,0},{5,1},{8,4},{9,5},{12,8},{13,9},{64,76},{65,77... | collective-permute-start | bytes 442376 | tf_op jit(solution)/shard_map/ppermute | solution.py:655
  332.4 5.6 %collective-permute-start.53 = (bf16[16,1152]{1,0:T(8,128)(2,1)S(1)}, bf16[16,1152]{1,0:T(8,128)(2,1)S(1)}, u32[]{:S(2)}, u32[]{:S(2)}) collective-permute-start(bf16[16,1152]{1,0:T(8,128)(2,1)S(1)} %get-tuple-element.90), channel_id=1, source_target_pairs={{0,2},{1,3},{4,6},{5,7},{8,10},{9,11},{12,14},{13,15},{64,66},{65,... | collective-permute-start | bytes 110600 | tf_op jit(solution)/shard_map/ppermute | solution.py:655
  335.3 4.0 %collective-permute-start.54 = (bf16[16,1152]{1,0:T(8,128)(2,1)S(1)}, bf16[16,1152]{1,0:T(8,128)(2,1)S(1)}, u32[]{:S(2)}, u32[]{:S(2)}) collective-permute-start(bf16[16,1152]{1,0:T(8,128)(2,1)S(1)} %get-tuple-element.92), channel_id=1, source_target_pairs={{0,64},{1,65},{4,68},{5,69},{8,72},{9,73},{12,76},{13,77},{64,2},{... | collective-permute-start | bytes 110600 | tf_op jit(solution)/shard_map/ppermute | solution.py:655
  336.4 4.0 %collective-permute-start.55 = (bf16[16,1152]{1,0:T(8,128)(2,1)S(1)}, bf16[16,1152]{1,0:T(8,128)(2,1)S(1)}, u32[]{:S(2)}, u32[]{:S(2)}) collective-permute-start(bf16[16,1152]{1,0:T(8,128)(2,1)S(1)} %get-tuple-element.91), channel_id=1, source_target_pairs={{0,66},{1,67},{4,70},{5,71},{8,74},{9,75},{12,78},{13,79},{64,0},{... | collective-permute-start | bytes 110600 | tf_op jit(solution)/shard_map/ppermute | solution.py:655
  337.4 3.1 collective-permute-start.45
  340.4 1.3 collective-permute-start.56
  (9 other events, 53.1 us)

commit v2 on v0

v2 whole, which is shorter than its diff:
```python
from functools import partial

import jax
import jax.numpy as jnp
import numpy as np
from jax import lax
from jax.experimental import pallas as pl
from jax.experimental.pallas import tpu as pltpu
from jax.sharding import Mesh
from jax.sharding import PartitionSpec as P

EPSILON = 1e-05
NEGATIVE = -1e30
F32 = jnp.float32
BF16 = jnp.bfloat16
SLOT = 256
WIDTH = 512
HEADS = 8
HEAD = 64
HALF = 1536
TAPS = 31
REACH = 15
UTTS = 3
ROWS = UTTS * SLOT
PERIOD = SLOT + REACH
BINS = (PERIOD + 1) // 2
SPEC = 2 * BINS
BLOCK = 256
BLOCKS = HALF // BLOCK
PER_BRANCH = 768 // BLOCK
GELU_A = 0.7978845608028654
GELU_B = GELU_A * 0.044715
HEAD_UNROLL = 8
VMEM_LIMIT = 60 * 1024 * 1024


def transform_tables():
    bins = np.arange(BINS)[:, None]
    angle = 2 * np.pi * bins * np.arange(SLOT)[None, :] / PERIOD
    lag_angle = 2 * np.pi * bins * (np.arange(TAPS) - REACH)[None, :] / PERIOD
    weight = np.where(bins == 0, 1.0, 2.0) / PERIOD
    forward = np.concatenate([np.cos(angle), -np.sin(angle)], 0)
    inverse = np.concatenate([np.cos(angle) * weight, -np.sin(angle) * weight], 0).T
    tap_forward = np.concatenate([np.cos(lag_angle), -np.sin(lag_angle)], 0)
    tap_inverse = np.concatenate([np.cos(lag_angle) * weight, -np.sin(lag_angle) * weight], 0).T
    tap_forward = np.pad(tap_forward, ((0, 0), (0, 1)))
    tap_high = np.asarray(tap_forward.astype(BF16)).astype(np.float64)
    tap_forward = np.concatenate([tap_high, tap_high, tap_forward - tap_high], 1)
    tap_inverse = np.pad(tap_inverse, ((0, 1), (0, 0)))
    return forward, inverse, tap_forward, tap_inverse


def dot_nn(a, b):
    return lax.dot_general(a, b, (((1,), (0,)), ((), ())), preferred_element_type=F32)


def dot_nt(a, b):
    return lax.dot_general(a, b, (((1,), (1,)), ((), ())), preferred_element_type=F32)


def dot_tn(a, b):
    return lax.dot_general(a, b, (((0,), (0,)), ((), ())), preferred_element_type=F32)


def dot_tt(a, b):
    return lax.dot_general(a, b, (((0,), (1,)), ((), ())), preferred_element_type=F32)


def standardize(rows_in):
    average = jnp.mean(rows_in, axis=-1, keepdims=True)
    centered = rows_in - average
    variance = jnp.mean(centered * centered, axis=-1, keepdims=True)
    rstd = lax.rsqrt(variance + EPSILON)
    return centered * rstd, rstd


def gelu_pair(v):
    square = v * v
    half = 0.5 + 0.5 * jnp.tanh(v * (GELU_A + GELU_B * square))
    active = v * half
    slope = half + active * (1.0 - half) * (2 * GELU_A + 6 * GELU_B * square)
    return active, slope


def merge_mix(merge_logits):
    exponent = jnp.exp(merge_logits[...] - jnp.max(merge_logits[...], axis=1, keepdims=True))
    mixing = exponent / jnp.sum(exponent, axis=1, keepdims=True)
    return mixing[:, 0:1], mixing[:, 1:2]


INFO_BRANCH, INFO_CORE, INFO_X, INFO_LENGTH = 0, 1, 2, 3
SHIFTS = (0, 1, 3, 2)


def piece_copies(info, pieces, target, sems):
    core = info[INFO_CORE]
    half = pieces[0].shape[2]
    copies = []
    for i, piece in enumerate(pieces):
        at = lax.rem(info[INFO_X] + (4 - SHIFTS[i // 2]), 4)
        side = core if i % 2 == 0 else 1 - core
        rows = pl.ds(pl.multiple_of(at * 128, 128), 128)
        columns = pl.ds(pl.multiple_of(side * half, 128), half)
        for b in range(2):
            copies.append(
                pltpu.make_async_copy(
                    piece.at[b], target.at[b, rows, columns], sems.at[2 * i + b]
                )
            )
    return copies


def pack_local(info, att_in, att_out, mix_in, mix_out, out):
    for i in range(3):
        out[:, i * 256 : (i + 1) * 256] = att_in[i]
    for i in range(2):
        out[:, 768 + i * 768 : 768 + (i + 1) * 768] = mix_in[:, i, :]
    out[:, 2304:3072] = mix_out[...]
    out[:, 3072:3328] = att_out[...]


def spread_block(info, local, other, out):
    core = info[INFO_CORE]
    mine, theirs = local[...].astype(F32), other[...].astype(F32)
    rows = jnp.concatenate(
        [jnp.where(core == 0, mine, theirs), jnp.where(core == 0, theirs, mine)], axis=0
    )
    block = jnp.concatenate(
        [
            jnp.where(core == 0, rows[:, 0:384], rows[:, 384:768]),
            jnp.where(core == 0, rows[:, 768:2048], rows[:, 2048:3328]),
        ],
        axis=1,
    ).astype(BF16)
    for j in range(16):
        out[j] = block


def fill_distance(distance):
    key_at = lax.broadcasted_iota(jnp.int32, (SLOT, SLOT), 0)
    query_at = lax.broadcasted_iota(jnp.int32, (SLOT, SLOT), 1)
    offset = (key_at - query_at).astype(F32)
    distance[...] = jnp.sqrt(offset * offset + 1.0)


def attend_forward(
    info,
    frames,
    norm,
    own,
    other,
    *rest,
):
    pieces, (triple, context, log_total, weights, slopes, bias_s, sems) = rest[:8], rest[8:]
    step = pl.program_id(0)
    copies = piece_copies(info, pieces, weights, sems)

    @pl.when(step == 0)
    def _():
        for copy in copies:
            copy.start()
        branch = info[INFO_BRANCH]
        key_at = lax.broadcasted_iota(jnp.int32, (SLOT, SLOT), 0)
        query_at = lax.broadcasted_iota(jnp.int32, (SLOT, SLOT), 1)
        offset = (key_at - query_at).astype(F32)
        distance = jnp.sqrt(offset * offset + 1.0)
        for h in range(HEADS):
            lane = slice(h % 4, h % 4 + 1)
            slope = jnp.where(branch == h // 4, own[34:35, lane], other[34:35, lane])
            slopes[h : h + 1, :] = jnp.broadcast_to(slope, (1, 128))
            bias_s[h] = slope * distance
        for copy in copies:
            copy.wait()

    normed, _ = standardize(frames[0, 0])
    low = (normed * norm[0:1] + norm[1:2]).astype(BF16)
    for b in range(2):
        part = dot_tt(weights[b, :, 0:256], low) * (HEAD**-0.5)
        triple[0, b * 768 : b * 768 + 256, :] = part.astype(BF16)
        part = dot_tt(weights[b, :, 256:768], low)
        triple[0, b * 768 + 256 : (b + 1) * 768, :] = part.astype(BF16)
    is_key = lax.broadcasted_iota(jnp.int32, (SLOT, SLOT), 0) < info[INFO_LENGTH + step]

    def head(h, carry):
        base = pl.multiple_of((h // 4) * 768 + (h % 4) * HEAD, HEAD)
        q = triple[0, pl.ds(base, HEAD), :]
        k = triple[0, pl.ds(base + 256, HEAD), :]
        v = triple[0, pl.ds(base + 512, HEAD), :]
        logits = jnp.where(is_key, dot_tn(k, q) - bias_s[h], NEGATIVE)
        highest = jnp.max(logits, axis=0, keepdims=True)
        exponent = jnp.exp(logits - highest)
        total = jnp.sum(exponent, axis=0, keepdims=True)
        prob = (exponent * (1.0 / total)).astype(BF16)
        context[0, pl.ds(pl.multiple_of(h * HEAD, HEAD), HEAD), :] = dot_nn(v, prob).astype(BF16)
        log_total[0, pl.ds(h, 1), :] = highest + jnp.log(total)
        return carry

    lax.fori_loop(0, HEADS, head, 0, unroll=HEAD_UNROLL)


def mixer_both(
    info,
    frames,
    cotangent,
    context,
    mixer_norm,
    final_norm,
    merge_logits,
    own,
    other,
    forward,
    inverse,
    tap_forward,
    tap_inverse,
    *rest,
):
    pieces, rest = rest[:8], rest[8:]
    (
        layer,
        grad_frames,
        grad_context,
        keep,
        send,
        small,
        weights,
        params_s,
        small_wide,
        small_narrow,
        tap_spec,
        second_s,
        second_slope,
        first_s,
        first_slope,
        conv_s,
        spec_s,
        cross_s,
        back_s,
        gated_s,
        hidden_s,
        low_s,
        grad_s,
        attend_s,
        context_s,
        grads_s,
        sems,
    ) = rest
    step = pl.program_id(0)
    branch, core = info[INFO_BRANCH], info[INFO_CORE]
    here = pl.ds(pl.multiple_of(step * SLOT, SLOT), SLOT)
    copies = piece_copies(info, pieces, weights, sems)

    @pl.when(step == 0)
    def _():
        for copy in copies:
            copy.start()
        params_s[branch] = own[...]
        params_s[1 - branch] = other[...]
        for b in range(2):
            high, low = split_low(params_s[b, 0:32, :])
            stacked = jnp.concatenate([high, low, high], axis=0).astype(BF16)
            tap_spec[:, b * 768 : (b + 1) * 768] = dot_nn(tap_forward[...], stacked)
        cross_s[...] = jnp.zeros_like(cross_s)
        small_wide[...] = jnp.zeros_like(small_wide)
        small_narrow[...] = jnp.zeros_like(small_narrow)
        for copy in copies:
            copy.wait()

    mix_attend, mix_mixer = merge_mix(merge_logits)
    rows_in = frames[0, 0]
    normed, rstd = standardize(rows_in)
    low = (normed * mixer_norm[0:1] + mixer_norm[1:2]).astype(BF16)
    low_s[here, :] = low
    length = info[INFO_LENGTH + step]
    valid = (lax.broadcasted_iota(jnp.int32, (SLOT, 1), 0) < length).astype(F32)

    places = [
        (k // PER_BRANCH, slice((k % PER_BRANCH) * BLOCK, (k % PER_BRANCH + 1) * BLOCK),
         slice(k * BLOCK, (k + 1) * BLOCK))
        for k in range(BLOCKS)
    ]

    def weight(b, kind, off):
        return weights[b, :, kind * 768 + off.start : kind * 768 + off.stop]

    def fold(v):
        return v[:, 0:128] + v[:, 128:256]

    def lane_sum(v):
        return jnp.sum(v, axis=-1, keepdims=True)

    total = jnp.zeros((SLOT, 128), F32)
    for b, off, wide in places:
        active, slope = gelu_pair(dot_nn(low, weight(b, 1, off)))
        second_s[:, wide] = active
        second_slope[:, wide] = slope
        total += fold(active)
    average = lane_sum(total) / HALF
    total = jnp.zeros((SLOT, 128), F32)
    for b, off, wide in places:
        centered = second_s[:, wide] - average
        total += fold(centered * centered)
    gate_rstd = lax.rsqrt(lane_sum(total) / HALF + EPSILON)

    for b, off, wide in places:
        standard = (second_s[:, wide] - average) * gate_rstd
        gate_in = (standard * params_s[b, 32:33, off] + params_s[b, 33:34, off]) * valid
        spec = dot_nn(forward[...], gate_in.astype(BF16))
        spec_s[:, wide] = spec
        real, imag = spec[0:BINS], spec[BINS:SPEC]
        tap_real, tap_imag = tap_spec[0:BINS, wide], tap_spec[BINS:SPEC, wide]
        product = jnp.concatenate(
            [real * tap_real + imag * tap_imag, imag * tap_real - real * tap_imag], axis=0
        )
        conved = dot_nn(inverse[...], product.astype(BF16)) + params_s[b, 31:32, off]
        conv_s[:, wide] = conved
        active, slope = gelu_pair(dot_nn(low, weight(b, 0, off)))
        first_s[:, wide] = active
        first_slope[:, wide] = slope
        gated_s[here, wide] = (active * conved).astype(BF16)

    mixer_part = dot_nt(gated_s[here, 0:768], weights[0, :, 1536:2304]) + dot_nt(
        gated_s[here, 768:1536], weights[1, :, 1536:2304]
    )
    context_s[:, here] = context[0]
    attend_part = dot_tt(context[0, 0:256, :], weights[0, :, 2304:2560]) + dot_tt(
        context[0, 256:512, :], weights[1, :, 2304:2560]
    )
    merged = rows_in + mix_attend * attend_part + mix_mixer * mixer_part
    merged_normed, merged_rstd = standardize(merged)
    layer[0] = ((merged_normed * final_norm[0:1] + final_norm[1:2]) * valid).astype(BF16)
    grad_out = cotangent[0, 0] * valid
    scaled = grad_out * final_norm[0:1]
    grad_merged = merged_rstd * (
        scaled
        - jnp.mean(scaled, axis=-1, keepdims=True)
        - merged_normed * jnp.mean(scaled * merged_normed, axis=-1, keepdims=True)
    )
    small_narrow[0:1] += jnp.sum(grad_out * merged_normed, axis=0, keepdims=True)
    small_narrow[1:2] += jnp.sum(grad_out, axis=0, keepdims=True)
    small_narrow[2:3] += jnp.sum(grad_merged * attend_part, axis=0, keepdims=True)
    small_narrow[3:4] += jnp.sum(grad_merged * mixer_part, axis=0, keepdims=True)
    grad_mixer = (mix_mixer * grad_merged).astype(BF16)
    grad_s[here, :] = grad_mixer
    grad_attend = (mix_attend * grad_merged).astype(BF16)
    attend_s[here, :] = grad_attend
    for b in range(2):
        grad_context[0, b * 256 : (b + 1) * 256, :] = dot_tt(
            weights[b, :, 2304:2560], grad_attend
        ).astype(BF16)

    total, cross_total = jnp.zeros((SLOT, 128), F32), jnp.zeros((SLOT, 128), F32)
    for b, off, wide in places:
        grad_gated = dot_nn(grad_mixer, weight(b, 2, off))
        grad_conved = grad_gated * first_s[:, wide]
        hidden_s[here, wide] = (first_slope[:, wide] * (grad_gated * conv_s[:, wide])).astype(BF16)
        small_wide[31:32, wide] += jnp.sum(grad_conved, axis=0, keepdims=True)
        grad_spec = dot_nn(forward[...], grad_conved.astype(BF16))
        grad_real, grad_imag = grad_spec[0:BINS], grad_spec[BINS:SPEC]
        real, imag = spec_s[0:BINS, wide], spec_s[BINS:SPEC, wide]
        cross_s[0:BINS, wide] += grad_real * real + grad_imag * imag
        cross_s[BINS:SPEC, wide] += grad_real * imag - grad_imag * real
        tap_real, tap_imag = tap_spec[0:BINS, wide], tap_spec[BINS:SPEC, wide]
        product = jnp.concatenate(
            [
                grad_real * tap_real - grad_imag * tap_imag,
                grad_real * tap_imag + grad_imag * tap_real,
            ],
            axis=0,
        )
        grad_gate = dot_nn(inverse[...], product.astype(BF16)) * valid
        standard = (second_s[:, wide] - average) * gate_rstd
        small_wide[32:33, wide] += jnp.sum(grad_gate * standard, axis=0, keepdims=True)
        small_wide[33:34, wide] += jnp.sum(grad_gate, axis=0, keepdims=True)
        grad_standard = grad_gate * params_s[b, 32:33, off]
        back_s[:, wide] = grad_standard
        total += fold(grad_standard)
        cross_total += fold(grad_standard * standard)
    back_average = lane_sum(total) / HALF
    back_scale = lane_sum(cross_total) / HALF

    for b, off, wide in places:
        standard = (second_s[:, wide] - average) * gate_rstd
        grad_second = gate_rstd * (back_s[:, wide] - back_average - standard * back_scale)
        hidden_s[here, HALF + wide.start : HALF + wide.stop] = (
            second_slope[:, wide] * grad_second
        ).astype(BF16)
    grad_low = (
        dot_nt(hidden_s[here, 0:768], weights[0, :, 0:768])
        + dot_nt(hidden_s[here, 768:1536], weights[1, :, 0:768])
    ) + (
        dot_nt(hidden_s[here, 1536:2304], weights[0, :, 768:1536])
        + dot_nt(hidden_s[here, 2304:3072], weights[1, :, 768:1536])
    )
    small_narrow[4:5] += jnp.sum(grad_low * normed, axis=0, keepdims=True)
    small_narrow[5:6] += jnp.sum(grad_low, axis=0, keepdims=True)
    scaled = grad_low * mixer_norm[0:1]
    grad_frames[0] = grad_merged + rstd * (
        scaled
        - jnp.mean(scaled, axis=-1, keepdims=True)
        - normed * jnp.mean(scaled * normed, axis=-1, keepdims=True)
    )

    @pl.when(step == UTTS - 1)
    def _():
        outs = []
        for half in range(2):
            for b in range(2):
                if half == 0:
                    parts = [
                        dot_tn(low_s[...], hidden_s[:, b * 768 : (b + 1) * 768]),
                        dot_tn(low_s[...], hidden_s[:, HALF + b * 768 : HALF + b * 768 + 512]),
                    ]
                else:
                    parts = [
                        dot_tn(
                            low_s[...], hidden_s[:, HALF + b * 768 + 512 : HALF + (b + 1) * 768]
                        ),
                        dot_tn(grad_s[...], gated_s[:, b * 768 : (b + 1) * 768]),
                        dot_tt(attend_s[...], context_s[b * 256 : (b + 1) * 256, :]),
                    ]
                column = 0
                for part in parts:
                    grads_s[half, b, :, column : column + part.shape[1]] = part.astype(BF16)
                    column += part.shape[1]
                for i, target in enumerate((keep, send)):
                    copy = pltpu.make_async_copy(
                        grads_s.at[half, b], target.at[b], sems.at[half * 2 + b]
                    )
                    outs.append((core == half if i == 0 else core != half, copy))
                    pl.when(outs[-1][0])(copy.start)
        tap_grad = dot_nn(tap_inverse[...], cross_s[...].astype(BF16))
        small_wide[0:31, :] = tap_grad[0:31]
        for g in range(12):
            small[g * 40 : (g + 1) * 40, :] = small_wide[:, g * 128 : (g + 1) * 128]
        for j in range(4):
            small[480 + 8 * j : 488 + 8 * j, :] = small_narrow[:, j * 128 : (j + 1) * 128]
        for wanted, copy in outs:
            pl.when(wanted)(copy.wait)


def attend_backward(
    info,
    frames,
    grad_mixed,
    triple,
    log_total,
    grad_context,
    norm,
    slopes,
    weights,
    frames_grad,
    keep,
    send,
    distance,
    low_s,
    triple_t,
    small,
    grads_s,
    sems,
):
    step = pl.program_id(0)
    here = pl.ds(pl.multiple_of(step * SLOT, SLOT), SLOT)
    core = info[INFO_CORE]

    @pl.when(step == 0)
    def _():
        fill_distance(distance)
        small[...] = jnp.zeros_like(small)

    normed, rstd = standardize(frames[0, 0])
    low_s[here, :] = (normed * norm[0:1] + norm[1:2]).astype(BF16)
    is_key = lax.broadcasted_iota(jnp.int32, (SLOT, SLOT), 0) < info[INFO_LENGTH + step]

    def head(h, carry):
        base = pl.multiple_of((h // 4) * 768 + (h % 4) * HEAD, HEAD)
        q = triple[0, pl.ds(base, HEAD), :]
        k = triple[0, pl.ds(base + 256, HEAD), :]
        v = triple[0, pl.ds(base + 512, HEAD), :]
        grad_here = grad_context[0, pl.ds(pl.multiple_of(h * HEAD, HEAD), HEAD), :]
        logits = dot_tn(k, q) - slopes[pl.ds(h, 1), 0:1] * distance[...]
        logits = jnp.where(is_key, logits, NEGATIVE)
        prob = jnp.exp(logits - log_total[0, pl.ds(h, 1), :])
        grad_prob = dot_tn(v, grad_here)
        row_dot = jnp.sum(prob * grad_prob, axis=0, keepdims=True)
        grad_logits = prob * (grad_prob - row_dot)
        slope_row = -jnp.sum(grad_logits * distance[...], axis=0, keepdims=True)
        small[pl.ds(8 + h, 1), :] += slope_row[:, 0:128] + slope_row[:, 128:256]
        grad_scores = grad_logits.astype(BF16)
        grad_q = dot_nn(k, grad_scores) * (HEAD**-0.5)
        grad_k = dot_nt(q, grad_scores)
        grad_v = dot_nt(grad_here, prob.astype(BF16))
        triple_t[pl.ds(base, HEAD), here] = grad_q.astype(BF16)
        triple_t[pl.ds(base + 256, HEAD), here] = grad_k.astype(BF16)
        triple_t[pl.ds(base + 512, HEAD), here] = grad_v.astype(BF16)
        return carry

    lax.fori_loop(0, HEADS, head, 0, unroll=HEAD_UNROLL)
    grad_low = dot_tt(triple_t[0:768, here], weights[0]) + dot_tt(
        triple_t[768:1536, here], weights[1]
    )
    gain_row = jnp.sum(grad_low * normed, axis=0, keepdims=True)
    bias_row = jnp.sum(grad_low, axis=0, keepdims=True)
    for j in range(4):
        small[j : j + 1, :] += gain_row[:, j * 128 : (j + 1) * 128]
        small[4 + j : 5 + j, :] += bias_row[:, j * 128 : (j + 1) * 128]
    scaled = grad_low * norm[0:1]
    frames_grad[0] = (
        grad_mixed[0]
        + rstd
        * (
            scaled
            - jnp.mean(scaled, axis=-1, keepdims=True)
            - normed * jnp.mean(scaled * normed, axis=-1, keepdims=True)
        )
    ).astype(BF16)

    @pl.when(step == UTTS - 1)
    def _():
        high, low = split_low(small[...])
        pair = jnp.concatenate([high, low], axis=1).astype(BF16)
        outs = []
        for half in range(2):
            for b in range(2):
                rows = b * 768 + half * 512
                if half == 0:
                    grads_s[half, b] = dot_tt(low_s[...], triple_t[rows : rows + 512, :]).astype(
                        BF16
                    )
                else:
                    grads_s[half, b, :, 0:256] = dot_tt(
                        low_s[...], triple_t[rows : rows + 256, :]
                    ).astype(BF16)
                    for m in range(32):
                        grads_s[half, b, 16 * m : 16 * m + 16, 256:512] = pair
                for i, target in enumerate((keep, send)):
                    copy = pltpu.make_async_copy(
                        grads_s.at[half, b], target.at[b], sems.at[half * 2 + b]
                    )
                    outs.append((core == half if i == 0 else core != half, copy))
                    pl.when(outs[-1][0])(copy.start)
        for wanted, copy in outs:
            pl.when(wanted)(copy.wait)


def split_low(value):
    high = value.astype(BF16).astype(F32)
    return high, value - high


def start_all(copies):
    for copy in copies:
        copy.start()
    return copies


def chunk_copies(source, target, count, sems):
    size = target.shape[0] // count
    return start_all(
        [
            pltpu.make_async_copy(
                source.at[pl.ds(i * size, size)], target.at[pl.ds(i * size, size)], sems.at[i]
            )
            for i in range(count)
        ]
    )


CHUNKS = 8


def sum_mixer(info, keep, other, small, small_other, out, keep_s, other_s, out_s, sems):
    first = chunk_copies(keep, keep_s, CHUNKS, sems.at[0])
    second = chunk_copies(other, other_s, CHUNKS, sems.at[1])
    high, low = split_low(small[...] + small_other[...])
    for j in range(64):
        rows = slice(8 * j, 8 * j + 8)
        out_s[16 * j : 16 * j + 16, 1280:1408] = jnp.concatenate(
            [high[rows], low[rows]], axis=0
        ).astype(BF16)
    outs = []
    for i in range(CHUNKS):
        rows = slice(i * 128, (i + 1) * 128)
        first[i].wait()
        second[i].wait()
        out_s[rows, 0:1280] = (keep_s[rows].astype(F32) + other_s[rows].astype(F32)).astype(BF16)
        outs.append(pltpu.make_async_copy(out_s.at[rows], out.at[rows], sems.at[2, i]))
        outs[-1].start()
    for copy in outs:
        copy.wait()


def sum_attend(info, keep, other, mixer_total, out, keep_s, other_s, out_s, sems):
    first = chunk_copies(keep, keep_s, CHUNKS, sems.at[0])
    second = chunk_copies(other, other_s, CHUNKS, sems.at[1])
    high, low = split_low(mixer_total[0:8, :] + mixer_total[8:16, :])
    block = jnp.concatenate([high, low], axis=0).astype(BF16)
    outs = []
    for i in range(CHUNKS):
        rows = slice(i * 128, (i + 1) * 128)
        first[i].wait()
        second[i].wait()
        total = keep_s[rows].astype(F32) + other_s[rows].astype(F32)
        out_s[rows, 0:512] = total.astype(BF16)

        @pl.when(info[INFO_CORE] == 1)
        def _():
            high, low = split_low(total[:, 256:384] + total[:, 384:512])
            out_s[rows, 256:384] = high.astype(BF16)
            out_s[rows, 384:512] = low.astype(BF16)

        for j in range(8):
            out_s[i * 128 + 16 * j : i * 128 + 16 * j + 16, 512:640] = block
        outs.append(pltpu.make_async_copy(out_s.at[rows], out.at[rows], sems.at[2, i]))
        outs[-1].start()
    for copy in outs:
        copy.wait()


def sum_chips(info, terms, out, *rest):
    small = rest[0] if len(rest) == 3 else None
    terms_s, sems = rest[-2:]
    copies = chunk_copies(terms, terms_s, CHUNKS, sems)
    columns = out.shape[1]
    for c in range(CHUNKS):
        copies[c].wait()
        parts = [terms_s[8 * c + i, :, 0:columns].astype(F32) for i in range(8)]
        total = ((parts[0] + parts[1]) + (parts[2] + parts[3])) + (
            (parts[4] + parts[5]) + (parts[6] + parts[7])
        )
        if c == 0:
            out[...] = total
        else:
            out[...] += total
        if small is not None:
            for i in range(8 * c, 8 * c + 8):
                pair = terms_s[i, :, columns : columns + 128].astype(F32)
                small[8 * i : 8 * i + 8, :] = pair[0:8] + pair[8:16]


def finish(
    info,
    merge_logits,
    mixer_mine,
    mixer_theirs,
    mine,
    theirs,
    small,
    att_in,
    att_out,
    mix_in,
    mix_out,
    anorm,
    mnorm,
    fnorm,
    gnorm,
    taps,
    bias,
    slope,
    merge,
):
    core, branch = info[INFO_CORE], info[INFO_BRANCH]

    def rows(v):
        return jnp.where(core == 0, v[0:8], v[8:16])

    def halves(a, b):
        return jnp.where(core == 0, a, b), jnp.where(core == 0, b, a)

    low, high = halves(rows(mixer_mine), rows(mixer_theirs))
    first, second = halves(mine[...], theirs[...])
    att_in[0] = rows(first)[:, 0:256]
    att_in[1] = rows(first)[:, 256:512]
    att_in[2] = rows(second)[:, 0:256]
    mix_in[:, 0, :] = low[:, 0:768]
    mix_in[:, 1, :] = jnp.concatenate([low[:, 768:1280], high[:, 0:256]], axis=1)
    mix_out[...] = high[:, 256:1024]
    att_out[...] = high[:, 1024:1280]
    little = second[:, 256:384] + second[:, 384:512]
    for p in range(2):
        for j in range(4):
            anorm[p : p + 1, j * 128 : (j + 1) * 128] = little[p * 4 + j : p * 4 + j + 1]
    for r in range(4):
        slope[r] = jnp.where(
            branch == 0, jnp.sum(little[8 + r : 9 + r]), jnp.sum(little[12 + r : 13 + r])
        )
    for g in range(6):
        group = small[pl.ds(pl.multiple_of((branch * 6 + g) * 40, 8), 40), :]
        columns = slice(g * 128, (g + 1) * 128)
        taps[:, columns] = group[0:31]
        bias[:, columns] = group[31:32]
        gnorm[:, columns] = group[32:34]
    attend_sum, mixer_sum = 0.0, 0.0
    for j in range(4):
        columns = slice(j * 128, (j + 1) * 128)
        group = small[480 + 8 * j : 488 + 8 * j, :]
        fnorm[:, columns] = group[0:2]
        mnorm[:, columns] = group[4:6]
        attend_sum += jnp.sum(group[2:3], axis=1, keepdims=True)
        mixer_sum += jnp.sum(group[3:4], axis=1, keepdims=True)
    mix_attend, mix_mixer = merge_mix(merge_logits)
    average = mix_attend * attend_sum + mix_mixer * mixer_sum
    merge[0] = jnp.sum(mix_attend * (attend_sum - average))
    merge[1] = jnp.sum(mix_mixer * (mixer_sum - average))


def place_pair(info, own, other, out, own_s, other_s, out_s, sems):
    branch = info[INFO_BRANCH]
    loads = [
        start_all(
            [
                pltpu.make_async_copy(source.at[u], target.at[u], sems.at[p, u])
                for u in range(UTTS)
            ]
        )
        for p, (source, target) in enumerate(((own, own_s), (other, other_s)))
    ]
    stores = []
    for u in range(UTTS):
        for p, source in enumerate((own_s, other_s)):
            loads[p][u].wait()
            out_s[p, u] = source[u].astype(F32)
            at = branch if p == 0 else 1 - branch
            stores.append(
                pltpu.make_async_copy(out_s.at[p, u], out.at[u, at], sems.at[2 + p, u])
            )
            stores[-1].start()
    for copy in stores:
        copy.wait()


def whole(shape):
    return pl.BlockSpec(shape, lambda i, *_: (0,) * len(shape), pipeline_mode=pl.Buffered(1))


def per_utt(shape):
    return pl.BlockSpec((1,) + shape, lambda i, *_: (i,) + (0,) * len(shape))


ANY = pl.BlockSpec(memory_space=pl.ANY)
OWN_FRAMES = pl.BlockSpec((1, 1, SLOT, WIDTH), lambda i, info, *_: (i, info[0], 0, 0))


def scratch(*shape, dtype=F32):
    return pltpu.VMEM(shape, dtype)


def struct(*shape, dtype=F32):
    return jax.ShapeDtypeStruct(shape, dtype)


def call(kernel, name, info, operands, in_specs, outs, out_specs, scratches=(), grid=1, us=2, **extra):
    return pl.pallas_call(
        kernel,
        grid_spec=pltpu.PrefetchScalarGridSpec(
            num_scalar_prefetch=1,
            grid=(grid,),
            in_specs=in_specs,
            out_specs=out_specs,
            scratch_shapes=scratches,
        ),
        out_shape=outs,
        compiler_params=pltpu.CompilerParams(
            dimension_semantics=("arbitrary",), vmem_limit_bytes=VMEM_LIMIT
        ),
        cost_estimate=pl.CostEstimate(
            flops=us * 100000000, bytes_accessed=1 << 16, transcendentals=0
        ),
        name=name,
        **extra,
    )(info, *operands)


def run_pack(info, *operands):
    return call(
        pack_local,
        "pack_local",
        info,
        operands,
        [whole(a.shape) for a in operands],
        struct(8, 3328, dtype=BF16),
        whole((8, 3328)),
    )


def run_spread(info, local, other):
    return call(
        spread_block,
        "spread_block",
        info,
        (local, other),
        [whole((8, 3328))] * 2,
        struct(16, 16, 1664, dtype=BF16),
        whole((16, 16, 1664)),
    )


def run_attend_forward(info, frames, norm, own, other, pieces):
    return call(
        attend_forward,
        "attend_forward",
        info,
        (frames, norm, own, other, *pieces),
        [OWN_FRAMES, whole((2, WIDTH)), whole((35, 768)), whole((35, 768))] + [ANY] * 8,
        [
            struct(UTTS, HALF, SLOT, dtype=BF16),
            struct(UTTS, WIDTH, SLOT, dtype=BF16),
            struct(UTTS, HEADS, SLOT),
            struct(2, WIDTH, 768, dtype=BF16),
            struct(HEADS, 128),
        ],
        [
            per_utt((HALF, SLOT)),
            per_utt((WIDTH, SLOT)),
            per_utt((HEADS, SLOT)),
            whole((2, WIDTH, 768)),
            whole((HEADS, 128)),
        ],
        [scratch(HEADS, SLOT, SLOT), pltpu.SemaphoreType.DMA((16,))],
        grid=UTTS,
    )


def run_mixer(info, frames, cotangent, context, mnorm, fnorm, merge_logits, own, other, pieces):
    forward, inverse, tap_forward, tap_inverse = transform_tables()
    tables = (
        jnp.asarray(forward, BF16),
        jnp.asarray(inverse, BF16),
        jnp.asarray(tap_forward, BF16),
        jnp.asarray(tap_inverse, BF16),
    )
    return call(
        mixer_both,
        "mixer_both",
        info,
        (frames, cotangent, context, mnorm, fnorm, merge_logits, own, other, *tables, *pieces),
        [
            OWN_FRAMES,
            OWN_FRAMES,
            per_utt((WIDTH, SLOT)),
            whole((2, WIDTH)),
            whole((2, WIDTH)),
            whole((1, 2)),
            whole((35, 768)),
            whole((35, 768)),
            whole((SPEC, SLOT)),
            whole((SLOT, SPEC)),
            whole((SPEC, 96)),
            whole((32, SPEC)),
        ]
        + [ANY] * 8,
        [
            struct(UTTS, SLOT, WIDTH, dtype=BF16),
            struct(UTTS, SLOT, WIDTH),
            struct(UTTS, WIDTH, SLOT, dtype=BF16),
            struct(2, WIDTH, 1280, dtype=BF16),
            struct(2, WIDTH, 1280, dtype=BF16),
            struct(512, 128),
        ],
        [
            per_utt((SLOT, WIDTH)),
            per_utt((SLOT, WIDTH)),
            per_utt((WIDTH, SLOT)),
            ANY,
            ANY,
            whole((512, 128)),
        ],
        [
            scratch(2, WIDTH, 2560, dtype=BF16),
            scratch(2, 35, 768),
            scratch(40, HALF),
            scratch(8, WIDTH),
            scratch(SPEC, HALF),
            scratch(SLOT, HALF),
            scratch(SLOT, HALF),
            scratch(SLOT, HALF),
            scratch(SLOT, HALF),
            scratch(SLOT, HALF),
            scratch(SPEC, HALF),
            scratch(SPEC, HALF),
            scratch(SLOT, HALF),
            scratch(ROWS, HALF, dtype=BF16),
            scratch(ROWS, 2 * HALF, dtype=BF16),
            scratch(ROWS, WIDTH, dtype=BF16),
            scratch(ROWS, WIDTH, dtype=BF16),
            scratch(ROWS, WIDTH, dtype=BF16),
            scratch(WIDTH, ROWS, dtype=BF16),
            scratch(2, 2, WIDTH, 1280, dtype=BF16),
            pltpu.SemaphoreType.DMA((16,)),
        ],
        grid=UTTS,
    )


def run_attend_backward(
    info, frames, grad_mixed, triple, log_total, grad_context, norm, slopes, weights
):
    return call(
        attend_backward,
        "attend_backward",
        info,
        (frames, grad_mixed, triple, log_total, grad_context, norm, slopes, weights),
        [
            OWN_FRAMES,
            per_utt((SLOT, WIDTH)),
            per_utt((HALF, SLOT)),
            per_utt((HEADS, SLOT)),
            per_utt((WIDTH, SLOT)),
            whole((2, WIDTH)),
            whole((HEADS, 128)),
            whole((2, WIDTH, 768)),
        ],
        [
            struct(UTTS, SLOT, WIDTH, dtype=BF16),
            struct(2, WIDTH, 512, dtype=BF16),
            struct(2, WIDTH, 512, dtype=BF16),
        ],
        [per_utt((SLOT, WIDTH)), ANY, ANY],
        [
            scratch(SLOT, SLOT),
            scratch(ROWS, WIDTH, dtype=BF16),
            scratch(HALF, ROWS, dtype=BF16),
            scratch(16, 128),
            scratch(2, 2, WIDTH, 512, dtype=BF16),
            pltpu.SemaphoreType.DMA((4,)),
        ],
        grid=UTTS,
    )


def run_sum_mixer(info, keep, other, small, small_other):
    return call(
        sum_mixer,
        "sum_mixer",
        info,
        (keep.reshape(1024, 1280), other.reshape(1024, 1280), small, small_other),
        [ANY, ANY, whole((512, 128)), whole((512, 128))],
        struct(1024, 1408, dtype=BF16),
        ANY,
        [
            scratch(1024, 1280, dtype=BF16),
            scratch(1024, 1280, dtype=BF16),
            scratch(1024, 1408, dtype=BF16),
            pltpu.SemaphoreType.DMA((3, CHUNKS)),
        ],
    )


def run_sum_attend(info, keep, other, mixer_total):
    return call(
        sum_attend,
        "sum_attend",
        info,
        (keep.reshape(1024, 512), other.reshape(1024, 512), mixer_total),
        [ANY, ANY, pl.BlockSpec((16, 128), lambda i, *_: (0, 10))],
        struct(1024, 640, dtype=BF16),
        ANY,
        [
            scratch(1024, 512, dtype=BF16),
            scratch(1024, 512, dtype=BF16),
            scratch(1024, 640, dtype=BF16),
            pltpu.SemaphoreType.DMA((3, CHUNKS)),
        ],
    )


def run_sum_chips(info, terms, small):
    columns = terms.shape[2]
    outs = [struct(16, columns)] if not small else [struct(16, columns - 128), struct(512, 128)]
    return call(
        sum_chips,
        "sum_chips",
        info,
        (terms,),
        [ANY],
        outs,
        [whole(o.shape) for o in outs],
        [scratch(*terms.shape, dtype=BF16), pltpu.SemaphoreType.DMA((CHUNKS,))],
    )


def run_finish(info, *operands):
    shapes = [
        (3, 8, 256),
        (8, 256),
        (8, 2, 768),
        (8, 768),
        (2, WIDTH),
        (2, WIDTH),
        (2, WIDTH),
        (2, 768),
        (31, 768),
        (1, 768),
    ]
    scalars = pl.BlockSpec(memory_space=pltpu.SMEM)
    return call(
        finish,
        "finish",
        info,
        operands,
        [whole(a.shape) for a in operands],
        [struct(*s) for s in shapes] + [struct(4), struct(2)],
        [whole(s) for s in shapes] + [scalars, scalars],
    )


def run_place_pair(info, own, other):
    return call(
        place_pair,
        "place_pair",
        info,
        (own, other),
        [ANY, ANY],
        struct(UTTS, 2, SLOT, WIDTH),
        ANY,
        [
            scratch(UTTS, SLOT, WIDTH, dtype=BF16),
            scratch(UTTS, SLOT, WIDTH, dtype=BF16),
            scratch(2, UTTS, SLOT, WIDTH),
            pltpu.SemaphoreType.DMA((4, UTTS)),
        ],
    )


def swap(value, axis):
    return lax.ppermute(value, axis, [(0, 1), (1, 0)])


def along_x(block):
    return [block] + [
        lax.ppermute(block, "x", [(i, (i + s) % 4) for i in range(4)]) for s in SHIFTS[1:]
    ]


def with_partner(pieces):
    both = []
    for piece in pieces:
        both += [piece, swap(piece, "core")]
    return both


CHIPS = ("branch", "x", "z", "yh")


def exchange(blocks):
    return lax.all_to_all(blocks, CHIPS, 0, 0, tiled=True)


def shards(
    frames,
    attend_norm,
    attend_in,
    attend_out,
    position_slope,
    mixer_norm,
    mixer_in,
    gating_norm,
    kernel_taps,
    kernel_bias,
    mixer_out,
    merge_logits,
    final_norm,
    lengths,
    cotangent,
):
    branch = lax.axis_index("branch")
    core = lax.axis_index("core")
    own_lengths = lax.dynamic_slice_in_dim(lengths, branch, 1, 1)[:, 0]
    info = jnp.concatenate([jnp.stack([branch, core, lax.axis_index("x")]), own_lengths])
    merge_logits = merge_logits[None]
    local = run_pack(info, attend_in.transpose(1, 0, 2), attend_out, mixer_in, mixer_out)
    own = jnp.concatenate(
        [kernel_taps, kernel_bias[None], gating_norm, jnp.pad(position_slope, (0, 764))[None]]
    )
    other = swap(own, "branch")
    block = run_spread(info, local, swap(local, "core"))
    block, other = lax.optimization_barrier((block, other))
    plane = lax.all_to_all(block, ("branch", "z", "yh"), 0, 0, tiled=True).reshape(2, 128, 1664)
    attend_pieces = along_x(plane[:, :, 0:384])
    *attend_pieces, mixer_block = lax.optimization_barrier(
        (*attend_pieces, plane[:, :, 384:1664])
    )
    mixer_pieces = along_x(mixer_block)

    triple, context, log_total, attend_w, slopes = run_attend_forward(
        info, frames, attend_norm, own, other, with_partner(attend_pieces)
    )
    *mixer_pieces, context = lax.optimization_barrier((*mixer_pieces, context))
    layer, grad_mixed, grad_context, mixer_keep, mixer_send, small = run_mixer(
        info,
        frames,
        cotangent,
        context,
        mixer_norm,
        final_norm,
        merge_logits,
        own,
        other,
        with_partner(mixer_pieces),
    )
    mixer_other = swap(mixer_send, "core")
    small_other = swap(small, "core")
    layer_other = swap(layer, "branch")
    mixer_other, small_other, grad_context = lax.optimization_barrier(
        (mixer_other, small_other, grad_context)
    )
    mixer_terms = run_sum_mixer(info, mixer_keep, mixer_other, small, small_other)
    mixer_terms, grad_context, layer_other = lax.optimization_barrier(
        (mixer_terms, grad_context, layer_other)
    )
    mixer_terms = exchange(mixer_terms.reshape(64, 16, 1408))
    grads, attend_keep, attend_send = run_attend_backward(
        info,
        frames,
        grad_mixed,
        triple,
        log_total,
        grad_context,
        attend_norm,
        slopes,
        attend_w,
    )
    grads_other = swap(grads, "branch")
    mixer_total = run_sum_chips(info, mixer_terms, False)[0]
    attend_terms = run_sum_attend(info, attend_keep, swap(attend_send, "core"), mixer_total)
    attend_total, small = run_sum_chips(info, exchange(attend_terms.reshape(64, 16, 640)), True)
    (
        att_in,
        att_out,
        mix_in,
        mix_out,
        anorm,
        mnorm,
        fnorm,
        gnorm,
        taps,
        bias,
        slope,
        merge,
    ) = run_finish(
        info,
        merge_logits,
        mixer_total,
        swap(mixer_total, "core"),
        attend_total,
        swap(attend_total, "core"),
        small,
    )
    return (
        run_place_pair(info, layer, layer_other),
        run_place_pair(info, grads, grads_other),
        anorm,
        att_in.transpose(1, 0, 2),
        att_out,
        slope,
        mnorm,
        mix_in,
        gnorm,
        taps,
        bias[0],
        mix_out,
        merge,
        fnorm,
    )


def solution(mesh):
    fine = Mesh(mesh.devices.reshape(2, 4, 4, 2, 2), ("branch", "x", "z", "yh", "core"))
    dp = ("x", "z", "yh", "core")
    placed = (
        P(None, dp, None, None),
        P(),
        P(dp, None, "branch"),
        P(dp, "branch"),
        P("branch"),
        P(),
        P(dp, None, "branch"),
        P(None, "branch"),
        P(None, "branch"),
        P("branch"),
        P(dp, "branch"),
        P(),
        P(),
        P(None, dp),
        P(None, dp, None, None),
    )
    return jax.shard_map(
        shards,
        mesh=fine,
        in_specs=placed,
        out_specs=(
            P(None, dp, None, None),
            P(None, dp, None, None),
            P(),
            P(dp, None, "branch"),
            P(dp, "branch"),
            P("branch"),
            P(),
            P(dp, None, "branch"),
            P(None, "branch"),
            P(None, "branch"),
            P("branch"),
            P(dp, "branch"),
            P(),
            P(),
        ),
        check_vma=False,
    )
```

time: 2480 us -> 245 us (0.10)
  waiting for transfers between devices: 1340 us -> 77.8 us
  blocking collectives: 625 us -> 21.3 us
  other arithmetic: 233 us -> 2.83 us
  local copies, waits for them, and re-layouts: 128 us -> 10.2 us
  matrix products: 110 us -> 0 us
  Pallas kernels: 0 us -> 99.7 us
  starting transfers between devices: 0.58 us -> 30.3 us
  between operations: 25.8 us -> 0.99 us
    reduce_scatter x4 -> x0, waiting for transfers between devices: 806 us -> none  [the longest x1 329 us: shards(): lax.psum_scatter(weight_grads[0], 'dp', scatter_dimension=0, tiled=True)]
    psum x3 -> x0, waiting for transfers between devices: 534 us -> none  [the longest x1 359 us: shards(): small_total = lax.psum(small_sums, 'dp')]
    psum x3 -> x0, blocking collectives: 340 us -> none  [the longest x1 323 us: shards(): small_total = lax.psum(small_sums, 'dp')]
    all_gather x3 -> x0, blocking collectives: 284 us -> none  [the longest x1 96.1 us: shards(): lax.all_gather(attend_out, 'dp', axis=0, tiled=True)]
    dot_general x54 -> x0, matrix products: 110 us -> none  [the longest x3 23.2 us: shards(): jnp.einsum('td,dc->tc', mixer_grad_low, full_mix_out, preferred_element_t...]
    pallas_call x0 -> x12, Pallas kernels: none -> 99.7 us  [call(): pl.pallas_call(kernel, grid_spec=pltpu.PrefetchScalarGridSpec(num_scalar_...]
    reduce_sum x38 -> x0, other arithmetic: 87.5 us -> none  [the longest x6 16.4 us: norm_rows(): return centered * lax.rsqrt(variance + EPSILON) * params[0] + params[1]]
    mul x8 -> x0, other arithmetic: 56 us -> none  [the longest x4 50.7 us: depthwise(): result = result + kernel_taps[tap] * padded[:, tap:tap + slot_len]]
  transfers between devices with their start and end apart: 8 -> 25, of which waited for: 6 -> 17; matrix products, arithmetic and copies ran while one was open for 6% -> 0% of each run, Pallas kernels for 0% -> 22%
where the time goes in v2:
time: 245 us; the launch traced here: 243 us
  Pallas kernels  99.7 us (41%)
  waiting for transfers between devices  77.8 us (32%)
  starting transfers between devices  30.3 us (12%)
  blocking collectives  21.3 us (9%)
  local copies, waits for them, and re-layouts  10.2 us (4%)
  other arithmetic  2.83 us (1%)
    pallas_call x12, Pallas kernels, call(): pl.pallas_call(kernel, grid_spec=pltpu.PrefetchScalarGridSpec(num_scalar_...  99.7 us
    all_to_all x2, waiting for transfers between devices, exchange(): return lax.all_to_all(blocks, CHIPS, 0, 0, tiled=True)  36.9 us
    ppermute x17, waiting for transfers between devices, swap(): return lax.ppermute(value, axis, [(0, 1), (1, 0)])  25 us
    all_to_all x1, blocking collectives, shards(): lax.all_to_all(block, ('branch', 'z', 'yh'), 0, 0, tiled=True)  21.3 us
    ppermute x6, waiting for transfers between devices, along_x(): lax.ppermute(block, 'x', [(i, (i + s) % 4) for i in range(4)])  16 us
    all_to_all x2, starting transfers between devices, exchange(): return lax.all_to_all(blocks, CHIPS, 0, 0, tiled=True)  14.6 us
    ppermute x6, starting transfers between devices, along_x(): lax.ppermute(block, 'x', [(i, (i + s) % 4) for i in range(4)])  9.62 us
    unnamed x58, local copies, waits for them, and re-layouts  8.82 us
  transfers between devices with their start and end apart: 25, of which 17 were waited for; matrix products, arithmetic and copies ran while one was open for 0% of the time, Pallas kernels for 22%

profile of v2, /device:TPU:16, one launch (start us, length us, event | category | flops | bytes accessed | tf_op | source)
XLA Modules:
  0.0 243.3 jit_solution(16369506536435197044)
XLA Ops:
  0.7 0.7 broadcast_in_dim.9
  1.4 0.7 pad.4
  2.0 0.9 pad_maximum_fusion.own
  3.0 1.4 collective-permute-start.1
  4.3 0.6 pad_add_fusion.info
  5.0 2.1 pack_local.1.local
  7.1 1.4 collective-permute-done.other
  8.5 0.6 copy-done.26
  9.1 2.5 %spread_block.1 = bf16[16,16,1664]{2,1,0:T(8,128)(2,1)} custom-call(s32[6]{0:T(128)} %pad_add_fusion.info, bf16[8,3328]{1,0:T(8,128)(2,1)} %pack_local.1.local, bf16[8,3328]{1,0:T(8,128)(2,1)} %copy-done.26), custom_call_target="tpu_custom_call" | custom-call | flops 200000000 | bytes 65536 | tf_op jit(solution)/shard_map/spread_block/pallas_call | solution.py:752
  11.6 21.3 %all_to_all.15 = bf16[16,16,1664]{2,1,0:T(8,128)(2,1)S(1)} all-to-all(bf16[16,16,1664]{2,1,0:T(8,128)(2,1)} %spread_block.1), channel_id=1, replica_groups=mesh['branch'=2,'x'=4,'z'=4,'yh'=2,'core'=2] {'branch','z','yh'}, dimensions={0} | all-to-all | bytes 1703936 | tf_op jit(solution)/shard_map/all_to_all | solution.py:1077
  33.0 3.1 %collective-permute-start.4 = (bf16[2,128,384]{2,1,0:T(8,128)(2,1)S(1)}, bf16[2,128,384]{2,1,0:T(8,128)(2,1)S(1)}, u32[]{:S(2)}, u32[]{:S(2)}) collective-permute-start(bf16[2,128,384]{2,1,0:T(8,128)(2,1)S(1)} %slice.8.rest_0_), channel_id=1, source_target_pairs={{0,32},{16,48},{32,0},{48,16},{1,33},{17,49},{33,1},{49,17},{2,34}... | collective-permute-start | bytes 589832 | tf_op jit(solution)/shard_map/ppermute | solution.py:1030
  36.1 1.1 collective-permute-start.3
  37.2 0.9 collective-permute-start.2
  38.2 4.2 %collective-permute-done.4.rest_6_ = bf16[2,128,384]{2,1,0:T(8,128)(2,1)S(1)} collective-permute-done((bf16[2,128,384]{2,1,0:T(8,128)(2,1)S(1)}, bf16[2,128,384]{2,1,0:T(8,128)(2,1)S(1)}, u32[]{:S(2)}, u32[]{:S(2)}) %collective-permute-start.4) | collective-permute-done | bytes 196640 | tf_op jit(solution)/shard_map/ppermute | solution.py:1030
  42.4 2.3 collective-permute-done.3.rest_4_
  44.7 0.5 collective-permute-done.2.rest_2_
  45.2 2.5 %collective-permute-start.7 = (bf16[2,128,1280]{2,1,0:T(8,128)(2,1)S(1)}, bf16[2,128,1280]{2,1,0:T(8,128)(2,1)S(1)}, u32[]{:S(2)}, u32[]{:S(2)}) collective-permute-start(bf16[2,128,1280]{2,1,0:T(8,128)(2,1)S(1)} %slice.9.rest_0_), channel_id=1, source_target_pairs={{0,32},{16,48},{32,0},{48,16},{1,33},{17,49},{33,1},{49,17},{2,34}... | collective-permute-start | bytes 1966088 | tf_op jit(solution)/shard_map/ppermute | solution.py:1030
  47.6 1.2 collective-permute-start.6
  48.9 0.8 collective-permute-start.5
  49.7 0.5 collective-permute-start.9
  50.2 0.9 collective-permute-done.8.rest_1_
  51.1 0.1 collective-permute-start.10
  51.2 0.1 collective-permute-done.9.rest_3_
  51.4 0.2 collective-permute-start.11
  51.6 0.9 collective-permute-done.10.rest_5_
  52.5 0.7 copy-done.25
  53.3 14.2 %attend_forward.1 = (bf16[3,1536,256]{2,1,0:T(8,128)(2,1)}, bf16[3,512,256]{2,1,0:T(8,128)(2,1)}, f32[3,8,256]{2,1,0:T(8,128)}, bf16[2,512,768]{2,1,0:T(8,128)(2,1)}, f32[8,128]{1,0:T(8,128)}) custom-call(s32[6]{0:T(128)} %pad_add_fusion.info, f32[3,2,256,512]{3,2,1,0:T(8,128)} %frames.5, f32[2,512]{1,0:T(2,128)} %norm.3, f32[35,768]{1,0:T(8,128)} %copy-done.5, ...), custom_call_target="tpu_custom_call" | custom-call | flops 200000000 | bytes 65536 | tf_op jit(solution)/shard_map/attend_forward/pallas_call | solution.py:752
  67.6 9.0 %collective-permute-done.6.rest_4_ = bf16[2,128,1280]{2,1,0:T(8,128)(2,1)S(1)} collective-permute-done((bf16[2,128,1280]{2,1,0:T(8,128)(2,1)S(1)}, bf16[2,128,1280]{2,1,0:T(8,128)(2,1)S(1)}, u32[]{:S(2)}, u32[]{:S(2)}) %collective-permute-start.6) | collective-permute-done | bytes 655392 | tf_op jit(solution)/shard_map/ppermute | solution.py:1030
  76.7 0.5 collective-permute-start.13
  77.2 0.1 collective-permute-start.14
  77.3 0.4 collective-permute-start.15
  77.7 1.1 collective-permute-done.12.rest_1_
  78.8 0.9 collective-permute-done.13.rest_3_
  79.7 0.9 collective-permute-done.14.rest_5_
  80.7 0.9 collective-permute-done.15.rest_7_
  81.6 0.9 copy-done.16
  82.5 38.6 %mixer_both.1 = (bf16[3,256,512]{2,1,0:T(8,128)(2,1)}, f32[3,256,512]{2,1,0:T(8,128)}, bf16[3,512,256]{2,1,0:T(8,128)(2,1)}, bf16[2,512,1280]{2,1,0:T(8,128)(2,1...) custom-call(s32[6]{0:T(128)} %pad_add_fusion.info, f32[3,2,256,512]{3,2,1,0:T(8,128)} %frames.5, ...), custom_call_target="tpu_custom_call" | custom-call | flops 200000000 | bytes 65536 | tf_op jit(solution)/shard_map/mixer_both/pallas_call | solution.py:752
  121.1 0.4 collective-permute-start.16
  121.5 0.7 collective-permute-start.18
  122.3 4.6 %collective-permute-done.17.small_other = f32[512,128]{1,0:T(8,128)S(1)} collective-permute-done((f32[512,128]{1,0:T(8,128)}, f32[512,128]{1,0:T(8,128)S(1)}, u32[]{:S(2)}, u32[]{:S(2)}) %collective-permute-start.17) | collective-permute-done | bytes 262176 | tf_op jit(solution)/shard_map/ppermute | solution.py:1025
  126.9 0.7 copy-done.19
  127.6 0.8 copy-done.4
  128.5 5.3 %sum_mixer.1 = bf16[1024,1408]{1,0:T(8,128)(2,1)} custom-call(s32[6]{0:T(128)} %pad_add_fusion.info, bf16[1024,1280]{1,0:T(8,128)(2,1)} %bitcast.19, bf16[1024,1280]{1,0:T(8,128)(2,1)} %bitcast.20, f32[512,128]{1,0:T(8,128)} %get-tuple-element.76.small, f32[512,128]{1,0:T(8,128)} %copy-done.19), custom_call_target="tpu_custom_call" | custom-call | flops 200000000 | bytes 65536 | tf_op jit(solution)/shard_map/sum_mixer/pallas_call | solution.py:752
  133.8 7.8 %collective-permute-done.18.other = bf16[3,256,512]{2,1,0:T(8,128)(2,1)S(1)} collective-permute-done((bf16[3,256,512]{2,1,0:T(8,128)(2,1)}, bf16[3,256,512]{2,1,0:T(8,128)(2,1)S(1)}, u32[]{:S(2)}, u32[]{:S(2)}) %collective-permute-start.18) | collective-permute-done | bytes 786464 | tf_op jit(solution)/shard_map/ppermute | solution.py:1025
  141.6 0.9 copy-done.7
  142.5 7.5 %all-to-all-start.1 = ((bf16[64,16,1408]{2,1,0:T(8,128)(2,1)}), bf16[64,16,1408]{2,1,0:T(8,128)(2,1)S(1)}, u32[]{:S(2)}, u32[]{:S(2)}) async-start(bf16[64,16,1408]{2,1,0:T(8,128)(2,1)} %bitcast.15), calls=%async_computation.1 | async-start | bytes 5767168 | tf_op jit(solution)/shard_map/all_to_all | solution.py:1045
  150.0 17.1 %attend_backward.1 = (bf16[3,256,512]{2,1,0:T(8,128)(2,1)}, bf16[2,512,512]{2,1,0:T(8,128)(2,1)}, bf16[2,512,512]{2,1,0:T(8,128)(2,1)}) custom-call(s32[6]{0:T(128)} %pad_add_fusion.info, f32[3,2,256,512]{3,2,1,0:T(8,128)} %frames.5, f32[3,256,512]{2,1,0:T(8,128)} %get-tuple-element.82.grad_mixed, bf16[3,1536,256]{2,1,0:T(8,128)(2,1)} %get-tuple-element.83.triple, ...), custom_call_target="tpu_custom_call" | custom-call | flops 200000000 | bytes 65536 | tf_op jit(solution)/shard_map/attend_backward/pallas_call | solution.py:752
  167.1 0.1 collective-permute-start.21
  167.2 19.5 %all-to-all-done.1.terms = bf16[64,16,1408]{2,1,0:T(8,128)(2,1)S(1)} async-done(((bf16[64,16,1408]{2,1,0:T(8,128)(2,1)}), bf16[64,16,1408]{2,1,0:T(8,128)(2,1)S(1)}, u32[]{:S(2)}, u32[]{:S(2)}) %all-to-all-start.1) | async-done | bytes 2883616 | tf_op jit(solution)/shard_map/all_to_all | solution.py:1045
  186.7 1.6 copy-done.1
  188.2 3.2 %sum_chips.2.mixer_total.mixer_mine = f32[16,1408]{1,0:T(8,128)} custom-call(s32[6]{0:T(128)} %pad_add_fusion.info, bf16[64,16,1408]{2,1,0:T(8,128)(2,1)} %copy-done.1), custom_call_target="tpu_custom_call" | custom-call | flops 200000000 | bytes 65536 | tf_op jit(solution)/shard_map/sum_chips/pallas_call | solution.py:752
  191.4 4.1 %sum_attend.1 = bf16[1024,640]{1,0:T(8,128)(2,1)} custom-call(s32[6]{0:T(128)} %pad_add_fusion.info, bf16[1024,512]{1,0:T(8,128)(2,1)} %bitcast.21, bf16[1024,512]{1,0:T(8,128)(2,1)} %bitcast.11.other, f32[16,1408]{1,0:T(8,128)} %sum_chips.2.mixer_total.mixer_mine), custom_call_target="tpu_custom_call" | custom-call | flops 200000000 | bytes 65536 | tf_op jit(solution)/shard_map/sum_attend/pallas_call | solution.py:752
  195.6 7.1 %all-to-all-start.2 = ((bf16[64,16,640]{2,1,0:T(8,128)(2,1)}), bf16[64,16,640]{2,1,0:T(8,128)(2,1)S(1)}, u32[]{:S(2)}, u32[]{:S(2)}) async-start(bf16[64,16,640]{2,1,0:T(8,128)(2,1)} %bitcast.16), calls=%async_computation.2 | async-start | bytes 2621440 | tf_op jit(solution)/shard_map/all_to_all | solution.py:1045
  202.7 1.4 collective-permute-start.19
  204.1 17.4 %all-to-all-done.2.terms = bf16[64,16,640]{2,1,0:T(8,128)(2,1)S(1)} async-done(((bf16[64,16,640]{2,1,0:T(8,128)(2,1)}), bf16[64,16,640]{2,1,0:T(8,128)(2,1)S(1)}, u32[]{:S(2)}, u32[]{:S(2)}) %all-to-all-start.2) | async-done | bytes 1310752 | tf_op jit(solution)/shard_map/all_to_all | solution.py:1045
  221.4 1.1 copy-done.2
  222.5 2.9 %sum_chips.3 = (f32[16,512]{1,0:T(8,128)}, f32[512,128]{1,0:T(8,128)}) custom-call(s32[6]{0:T(128)} %pad_add_fusion.info, bf16[64,16,640]{2,1,0:T(8,128)(2,1)} %copy-done.2), custom_call_target="tpu_custom_call" | custom-call | flops 200000000 | bytes 65536 | tf_op jit(solution)/shard_map/sum_chips/pallas_call | solution.py:752
  225.4 3.5 %place_pair.2 = f32[3,2,256,512]{3,2,1,0:T(8,128)} custom-call(s32[6]{0:T(128)} %pad_add_fusion.info, bf16[3,256,512]{2,1,0:T(8,128)(2,1)} %get-tuple-element.73.own, bf16[3,256,512]{2,1,0:T(8,128)(2,1)} %copy-done.7), custom_call_target="tpu_custom_call" | custom-call | flops 200000000 | bytes 65536 | tf_op jit(solution)/shard_map/place_pair/pallas_call | solution.py:752
  228.9 5.2 %collective-permute-done.19.other = bf16[3,256,512]{2,1,0:T(8,128)(2,1)S(1)} collective-permute-done((bf16[3,256,512]{2,1,0:T(8,128)(2,1)S(1)}, bf16[3,256,512]{2,1,0:T(8,128)(2,1)S(1)}, u32[]{:S(2)}, u32[]{:S(2)}) %collective-permute-start.19) | collective-permute-done | bytes 786464 | tf_op jit(solution)/shard_map/ppermute | solution.py:1025
  234.2 0.9 copy-done.9
  235.0 3.5 %place_pair.3 = f32[3,2,256,512]{3,2,1,0:T(8,128)} custom-call(s32[6]{0:T(128)} %pad_add_fusion.info, bf16[3,256,512]{2,1,0:T(8,128)(2,1)} %get-tuple-element.88.own, bf16[3,256,512]{2,1,0:T(8,128)(2,1)} %copy-done.9), custom_call_target="tpu_custom_call" | custom-call | flops 200000000 | bytes 65536 | tf_op jit(solution)/shard_map/place_pair/pallas_call | solution.py:752
  238.6 0.6 copy-done.27
  239.2 2.8 %finish.1 = (f32[3,8,256]{2,1,0:T(8,128)}, f32[8,256]{1,0:T(8,128)}, f32[8,2,768]{2,1,0:T(2,128)}, f32[8,768]{1,0:T(8,128)}, f32[2,512]{1,0:T(2,128)}, /*index=5...) custom-call(s32[6]{0:T(128)} %pad_add_fusion.info, ...), custom_call_target="tpu_custom_call" | custom-call | flops 200000000 | bytes 65536 | tf_op jit(solution)/shard_map/finish/pallas_call | solution.py:752
  242.0 1.3 reduce
  (66 shorter events, 0.5 us)
Async XLA Ops:
  0.6 3.7 %copy-start = (s32[3,2]{0,1:T(2,128)S(1)}, s32[3,2]{0,1:T(2,128)}, u32[]{:S(2)}) copy-start(s32[3,2]{0,1:T(2,128)} %param.32) | copy-start | bytes 76
  3.0 50.3 %copy-start.5 = (f32[35,768]{1,0:T(8,128)}, f32[35,768]{1,0:T(8,128)S(1)}, u32[]{:S(2)}) copy-start(f32[35,768]{1,0:T(8,128)S(1)} %pad_maximum_fusion.own) | copy-start | bytes 322564
  3.0 8.6 %collective-permute-start.1 = (f32[35,768]{1,0:T(8,128)S(1)}, f32[35,768]{1,0:T(8,128)S(1)}, u32[]{:S(2)}, u32[]{:S(2)}) collective-permute-start(f32[35,768]{1,0:T(8,128)S(1)} %pad_maximum_fusion.own), channel_id=1, source_target_pairs={{0,64},{64,0},{1,65},{65,1},{2,66},{66,2},{3,67},{67,3},{4,68},{68... | collective-permute-start | bytes 322568 | tf_op jit(solution)/shard_map/ppermute | solution.py:1025
  7.1 1.4 collective-permute-start
  8.5 0.6 copy-start.26
  11.6 41.6 %copy-start.17 = (f32[35,768]{1,0:T(8,128)}, f32[35,768]{1,0:T(8,128)S(1)}, u32[]{:S(2)}) copy-start(f32[35,768]{1,0:T(8,128)S(1)} %collective-permute-done.1.other) | copy-start | bytes 322564
  33.0 20.3 %copy-start.6 = (bf16[2,128,384]{2,1,0:T(8,128)(2,1)}, bf16[2,128,384]{2,1,0:T(8,128)(2,1)S(1)}, u32[]{:S(2)}) copy-start(bf16[2,128,384]{2,1,0:T(8,128)(2,1)S(1)} %slice.8.rest_0_) | copy-start | bytes 589828
  33.0 9.4 %collective-permute-start.4 = (bf16[2,128,384]{2,1,0:T(8,128)(2,1)S(1)}, bf16[2,128,384]{2,1,0:T(8,128)(2,1)S(1)}, u32[]{:S(2)}, u32[]{:S(2)}) collective-permute-start(bf16[2,128,384]{2,1,0:T(8,128)(2,1)S(1)} %slice.8.rest_0_), channel_id=1, source_target_pairs={{0,32},{16,48},{32,0},{48,16},{1,33},{17,49},{33,1},{49,17},{2,34}... | collective-permute-start | bytes 589832 | tf_op jit(solution)/shard_map/ppermute | solution.py:1030
  36.1 8.6 %collective-permute-start.3 = (bf16[2,128,384]{2,1,0:T(8,128)(2,1)S(1)}, bf16[2,128,384]{2,1,0:T(8,128)(2,1)S(1)}, u32[]{:S(2)}, u32[]{:S(2)}) collective-permute-start(bf16[2,128,384]{2,1,0:T(8,128)(2,1)S(1)} %slice.8.rest_0_), channel_id=1, source_target_pairs={{0,48},{16,0},{32,16},{48,32},{1,49},{17,1},{33,17},{49,33},{2,50}... | collective-permute-start | bytes 589832 | tf_op jit(solution)/shard_map/ppermute | solution.py:1030
  37.2 7.9 %collective-permute-start.2 = (bf16[2,128,384]{2,1,0:T(8,128)(2,1)S(1)}, bf16[2,128,384]{2,1,0:T(8,128)(2,1)S(1)}, u32[]{:S(2)}, u32[]{:S(2)}) collective-permute-start(bf16[2,128,384]{2,1,0:T(8,128)(2,1)S(1)} %slice.8.rest_0_), channel_id=1, source_target_pairs={{0,16},{16,32},{32,48},{48,0},{1,17},{17,33},{33,49},{49,1},{2,18}... | collective-permute-start | bytes 589832 | tf_op jit(solution)/shard_map/ppermute | solution.py:1030
  38.2 44.3 %copy-start.3 = (bf16[2,128,1280]{2,1,0:T(8,128)(2,1)}, bf16[2,128,1280]{2,1,0:T(8,128)(2,1)S(1)}, u32[]{:S(2)}) copy-start(bf16[2,128,1280]{2,1,0:T(8,128)(2,1)S(1)} %slice.9.rest_0_) | copy-start | bytes 1966084
  42.4 10.8 %copy-start.20 = (bf16[2,128,384]{2,1,0:T(8,128)(2,1)}, bf16[2,128,384]{2,1,0:T(8,128)(2,1)S(1)}, u32[]{:S(2)}) copy-start(bf16[2,128,384]{2,1,0:T(8,128)(2,1)S(1)} %collective-permute-done.4.rest_6_) | copy-start | bytes 589828
  44.7 8.6 %copy-start.21 = (bf16[2,128,384]{2,1,0:T(8,128)(2,1)}, bf16[2,128,384]{2,1,0:T(8,128)(2,1)S(1)}, u32[]{:S(2)}) copy-start(bf16[2,128,384]{2,1,0:T(8,128)(2,1)S(1)} %collective-permute-done.3.rest_4_) | copy-start | bytes 589828
  45.2 8.1 %copy-start.22 = (bf16[2,128,384]{2,1,0:T(8,128)(2,1)}, bf16[2,128,384]{2,1,0:T(8,128)(2,1)S(1)}, u32[]{:S(2)}) copy-start(bf16[2,128,384]{2,1,0:T(8,128)(2,1)S(1)} %collective-permute-done.2.rest_2_) | copy-start | bytes 589828
  45.2 22.4 %collective-permute-start.7 = (bf16[2,128,1280]{2,1,0:T(8,128)(2,1)S(1)}, bf16[2,128,1280]{2,1,0:T(8,128)(2,1)S(1)}, u32[]{:S(2)}, u32[]{:S(2)}) collective-permute-start(bf16[2,128,1280]{2,1,0:T(8,128)(2,1)S(1)} %slice.9.rest_0_), channel_id=1, source_target_pairs={{0,32},{16,48},{32,0},{48,16},{1,33},{17,49},{33,1},{49,17},{2,34}... | collective-permute-start | bytes 1966088 | tf_op jit(solution)/shard_map/ppermute | solution.py:1030
  47.6 29.0 %collective-permute-start.6 = (bf16[2,128,1280]{2,1,0:T(8,128)(2,1)S(1)}, bf16[2,128,1280]{2,1,0:T(8,128)(2,1)S(1)}, u32[]{:S(2)}, u32[]{:S(2)}) collective-permute-start(bf16[2,128,1280]{2,1,0:T(8,128)(2,1)S(1)} %slice.9.rest_0_), channel_id=1, source_target_pairs={{0,48},{16,0},{32,16},{48,32},{1,49},{17,1},{33,17},{49,33},{2,50}... | collective-permute-start | bytes 1966088 | tf_op jit(solution)/shard_map/ppermute | solution.py:1030
  48.9 27.8 %collective-permute-start.5 = (bf16[2,128,1280]{2,1,0:T(8,128)(2,1)S(1)}, bf16[2,128,1280]{2,1,0:T(8,128)(2,1)S(1)}, u32[]{:S(2)}, u32[]{:S(2)}) collective-permute-start(bf16[2,128,1280]{2,1,0:T(8,128)(2,1)S(1)} %slice.9.rest_0_), channel_id=1, source_target_pairs={{0,16},{16,32},{32,48},{48,0},{1,17},{17,33},{33,49},{49,1},{2,18}... | collective-permute-start | bytes 1966088 | tf_op jit(solution)/shard_map/ppermute | solution.py:1030
  49.7 1.4 collective-permute-start.8
  49.7 1.7 collective-permute-start.9
  51.1 2.2 copy-start.23
  51.1 1.4 collective-permute-start.10
  51.4 1.9 copy-start.24
  51.4 1.9 collective-permute-start.11
  52.5 0.7 copy-start.25
  67.6 14.9 %copy-start.10 = (bf16[2,128,1280]{2,1,0:T(8,128)(2,1)}, bf16[2,128,1280]{2,1,0:T(8,128)(2,1)S(1)}, u32[]{:S(2)}) copy-start(bf16[2,128,1280]{2,1,0:T(8,128)(2,1)S(1)} %collective-permute-done.7.rest_6_) | copy-start | bytes 1966084
  76.6 5.9 %copy-start.11 = (bf16[2,128,1280]{2,1,0:T(8,128)(2,1)}, bf16[2,128,1280]{2,1,0:T(8,128)(2,1)S(1)}, u32[]{:S(2)}) copy-start(bf16[2,128,1280]{2,1,0:T(8,128)(2,1)S(1)} %collective-permute-done.6.rest_4_) | copy-start | bytes 1966084
  76.6 5.9 %copy-start.12 = (bf16[2,128,1280]{2,1,0:T(8,128)(2,1)}, bf16[2,128,1280]{2,1,0:T(8,128)(2,1)S(1)}, u32[]{:S(2)}) copy-start(bf16[2,128,1280]{2,1,0:T(8,128)(2,1)S(1)} %collective-permute-done.5.rest_2_) | copy-start | bytes 1966084
  76.6 2.2 collective-permute-start.12
  76.7 3.0 %collective-permute-start.13 = (bf16[2,128,1280]{2,1,0:T(8,128)(2,1)S(1)}, bf16[2,128,1280]{2,1,0:T(8,128)(2,1)S(1)}, u32[]{:S(2)}, u32[]{:S(2)}) collective-permute-start(bf16[2,128,1280]{2,1,0:T(8,128)(2,1)S(1)} %collective-permute-done.5.rest_2_), channel_id=1, source_target_pairs={{0,1},{1,0},{2,3},{3,2},{4,5},{5,4},{6,7},{7,6},{8,9},{9,8},{10,11... | collective-permute-start | bytes 1966088 | tf_op jit(solution)/shard_map/ppermute | solution.py:1025
  77.2 3.5 %collective-permute-start.14 = (bf16[2,128,1280]{2,1,0:T(8,128)(2,1)S(1)}, bf16[2,128,1280]{2,1,0:T(8,128)(2,1)S(1)}, u32[]{:S(2)}, u32[]{:S(2)}) collective-permute-start(bf16[2,128,1280]{2,1,0:T(8,128)(2,1)S(1)} %collective-permute-done.6.rest_4_), channel_id=1, source_target_pairs={{0,1},{1,0},{2,3},{3,2},{4,5},{5,4},{6,7},{7,6},{8,9},{9,8},{10,11... | collective-permute-start | bytes 1966088 | tf_op jit(solution)/shard_map/ppermute | solution.py:1025
  77.3 4.3 %collective-permute-start.15 = (bf16[2,128,1280]{2,1,0:T(8,128)(2,1)S(1)}, bf16[2,128,1280]{2,1,0:T(8,128)(2,1)S(1)}, u32[]{:S(2)}, u32[]{:S(2)}) collective-permute-start(bf16[2,128,1280]{2,1,0:T(8,128)(2,1)S(1)} %collective-permute-done.7.rest_6_), channel_id=1, source_target_pairs={{0,1},{1,0},{2,3},{3,2},{4,5},{5,4},{6,7},{7,6},{8,9},{9,8},{10,11... | collective-permute-start | bytes 1966088 | tf_op jit(solution)/shard_map/ppermute | solution.py:1025
  78.8 3.7 %copy-start.13 = (bf16[2,128,1280]{2,1,0:T(8,128)(2,1)}, bf16[2,128,1280]{2,1,0:T(8,128)(2,1)S(1)}, u32[]{:S(2)}) copy-start(bf16[2,128,1280]{2,1,0:T(8,128)(2,1)S(1)} %collective-permute-done.12.rest_1_) | copy-start | bytes 1966084
  79.7 1.9 copy-start.14
  80.7 0.9 copy-start.15
  81.6 0.9 copy-start.16
  121.1 5.8 %collective-permute-start.16 = (bf16[2,512,1280]{2,1,0:T(8,128)(2,1)}, bf16[2,512,1280]{2,1,0:T(8,128)(2,1)S(1)}, u32[]{:S(2)}, u32[]{:S(2)}) collective-permute-start(bf16[2,512,1280]{2,1,0:T(8,128)(2,1)} %get-tuple-element.75), channel_id=1, source_target_pairs={{0,1},{1,0},{2,3},{3,2},{4,5},{5,4},{6,7},{7,6},{8,9},{9,8},{10,11... | collective-permute-start | bytes 7864328 | tf_op jit(solution)/shard_map/ppermute | solution.py:1025
  121.5 20.0 %collective-permute-start.18 = (bf16[3,256,512]{2,1,0:T(8,128)(2,1)}, bf16[3,256,512]{2,1,0:T(8,128)(2,1)S(1)}, u32[]{:S(2)}, u32[]{:S(2)}) collective-permute-start(bf16[3,256,512]{2,1,0:T(8,128)(2,1)} %get-tuple-element.73.own), channel_id=1, source_target_pairs={{0,64},{64,0},{1,65},{65,1},{2,66},{66,2},{3,67},{67,3},{4,68},{68... | collective-permute-start | bytes 2359304 | tf_op jit(solution)/shard_map/ppermute | solution.py:1025
  122.2 4.7 %collective-permute-start.17 = (f32[512,128]{1,0:T(8,128)}, f32[512,128]{1,0:T(8,128)S(1)}, u32[]{:S(2)}, u32[]{:S(2)}) collective-permute-start(f32[512,128]{1,0:T(8,128)} %get-tuple-element.76.small), channel_id=1, source_target_pairs={{0,1},{1,0},{2,3},{3,2},{4,5},{5,4},{6,7},{7,6},{8,9},{9,8},{10,11... | collective-permute-start | bytes 786440 | tf_op jit(solution)/shard_map/ppermute | solution.py:1025
  126.9 0.7 copy-start.19
  126.9 1.6 copy-start.4
  141.6 0.9 copy-start.7
  142.5 44.2 %all-to-all-start.1 = ((bf16[64,16,1408]{2,1,0:T(8,128)(2,1)}), bf16[64,16,1408]{2,1,0:T(8,128)(2,1)S(1)}, u32[]{:S(2)}, u32[]{:S(2)}) async-start(bf16[64,16,1408]{2,1,0:T(8,128)(2,1)} %bitcast.15), calls=%async_computation.1 | async-start | bytes 5767168 | tf_op jit(solution)/shard_map/all_to_all | solution.py:1045
  167.1 24.3 %collective-permute-start.21 = (bf16[2,512,512]{2,1,0:T(8,128)(2,1)}, bf16[2,512,512]{2,1,0:T(8,128)(2,1)}, u32[]{:S(2)}, u32[]{:S(2)}) collective-permute-start(bf16[2,512,512]{2,1,0:T(8,128)(2,1)} %get-tuple-element.91), channel_id=1, source_target_pairs={{0,1},{1,0},{2,3},{3,2},{4,5},{5,4},{6,7},{7,6},{8,9},{9,8},{10,11... | collective-permute-start | bytes 3145736 | tf_op jit(solution)/shard_map/ppermute | solution.py:1025
  186.7 1.6 copy-start.1
  191.4 11.3 %copy-start.8 = (bf16[3,256,512]{2,1,0:T(8,128)(2,1)S(1)}, bf16[3,256,512]{2,1,0:T(8,128)(2,1)}, u32[]{:S(2)}) copy-start(bf16[3,256,512]{2,1,0:T(8,128)(2,1)} %get-tuple-element.88.own) | copy-start | bytes 2359300
  191.4 12.6 %copy-start.18 = (f32[16,1408]{1,0:T(8,128)S(1)}, f32[16,1408]{1,0:T(8,128)}, u32[]{:S(2)}) copy-start(f32[16,1408]{1,0:T(8,128)} %sum_chips.2.mixer_total.mixer_mine) | copy-start | bytes 270340
  195.6 25.9 %all-to-all-start.2 = ((bf16[64,16,640]{2,1,0:T(8,128)(2,1)}), bf16[64,16,640]{2,1,0:T(8,128)(2,1)S(1)}, u32[]{:S(2)}, u32[]{:S(2)}) async-start(bf16[64,16,640]{2,1,0:T(8,128)(2,1)} %bitcast.16), calls=%async_computation.2 | async-start | bytes 2621440 | tf_op jit(solution)/shard_map/all_to_all | solution.py:1045
  202.7 31.4 %collective-permute-start.19 = (bf16[3,256,512]{2,1,0:T(8,128)(2,1)S(1)}, bf16[3,256,512]{2,1,0:T(8,128)(2,1)S(1)}, u32[]{:S(2)}, u32[]{:S(2)}) collective-permute-start(bf16[3,256,512]{2,1,0:T(8,128)(2,1)S(1)} %copy-done.8), channel_id=1, source_target_pairs={{0,64},{64,0},{1,65},{65,1},{2,66},{66,2},{3,67},{67,3},{4,68},{68... | collective-permute-start | bytes 2359304 | tf_op jit(solution)/shard_map/ppermute | solution.py:1025
  204.1 34.4 %collective-permute-start.20 = (f32[16,1408]{1,0:T(8,128)S(1)}, f32[16,1408]{1,0:T(8,128)S(1)}, u32[]{:S(2)}, u32[]{:S(2)}) collective-permute-start(f32[16,1408]{1,0:T(8,128)S(1)} %copy-done.18), channel_id=1, source_target_pairs={{0,1},{1,0},{2,3},{3,2},{4,5},{5,4},{6,7},{7,6},{8,9},{9,8},{10,11... | collective-permute-start | bytes 270344 | tf_op jit(solution)/shard_map/ppermute | solution.py:1025
  221.4 1.1 copy-start.2
  225.4 13.2 %collective-permute-start.22 = (f32[16,512]{1,0:T(8,128)}, f32[16,512]{1,0:T(8,128)S(1)}, u32[]{:S(2)}, u32[]{:S(2)}) collective-permute-start(f32[16,512]{1,0:T(8,128)} %get-tuple-element.92.mine), channel_id=1, source_target_pairs={{0,1},{1,0},{2,3},{3,2},{4,5},{5,4},{6,7},{7,6},{8,9},{9,8},{10,11... | collective-permute-start | bytes 98312 | tf_op jit(solution)/shard_map/ppermute | solution.py:1025
  234.2 0.9 copy-start.9
  238.5 0.6 copy-start.27
  238.5 0.6 copy-start.28

commit v3 on v2

--- a/solution.py
+++ b/solution.py
@@ -31,7 +31,12 @@
 GELU_A = 0.7978845608028654
 GELU_B = GELU_A * 0.044715
 HEAD_UNROLL = 8
-VMEM_LIMIT = 60 * 1024 * 1024
+VMEM_LIMIT = 64 * 1024 * 1024 - 65536
+
+
+def three_terms(table):
+    high = np.asarray(table.astype(BF16)).astype(np.float64)
+    return np.concatenate([high, high, table - high], 1)
 
 
 def transform_tables():
@@ -43,11 +48,9 @@
     inverse = np.concatenate([np.cos(angle) * weight, -np.sin(angle) * weight], 0).T
     tap_forward = np.concatenate([np.cos(lag_angle), -np.sin(lag_angle)], 0)
     tap_inverse = np.concatenate([np.cos(lag_angle) * weight, -np.sin(lag_angle) * weight], 0).T
-    tap_forward = np.pad(tap_forward, ((0, 0), (0, 1)))
-    tap_high = np.asarray(tap_forward.astype(BF16)).astype(np.float64)
-    tap_forward = np.concatenate([tap_high, tap_high, tap_forward - tap_high], 1)
+    tap_forward = three_terms(np.pad(tap_forward, ((0, 0), (0, 1))))
     tap_inverse = np.pad(tap_inverse, ((0, 1), (0, 0)))
-    return forward, inverse, tap_forward, tap_inverse
+    return three_terms(forward), inverse, three_terms(inverse), tap_forward, tap_inverse
 
 
 def dot_nn(a, b):
@@ -88,52 +91,76 @@
     return mixing[:, 0:1], mixing[:, 1:2]
 
 
-INFO_BRANCH, INFO_CORE, INFO_X, INFO_LENGTH = 0, 1, 2, 3
+INFO_BRANCH, INFO_CORE, INFO_X, INFO_Y, INFO_Z, INFO_LENGTH = 0, 1, 2, 3, 4, 5
 SHIFTS = (0, 1, 3, 2)
 
 
-def piece_copies(info, pieces, target, sems):
+def piece_copies(info, pieces, target, sems, along="x"):
     core = info[INFO_CORE]
-    half = pieces[0].shape[2]
+    columns_in = pieces[0].shape[3]
     copies = []
     for i, piece in enumerate(pieces):
-        at = lax.rem(info[INFO_X] + (4 - SHIFTS[i // 2]), 4)
+        at = lax.rem(info[INFO_X if along == "x" else INFO_Z] + (4 - SHIFTS[i // 2]), 4)
         side = core if i % 2 == 0 else 1 - core
-        rows = pl.ds(pl.multiple_of(at * 128, 128), 128)
-        columns = pl.ds(pl.multiple_of(side * half, 128), half)
+        columns = pl.ds(pl.multiple_of(side * columns_in, 128), columns_in)
         for b in range(2):
-            copies.append(
-                pltpu.make_async_copy(
-                    piece.at[b], target.at[b, rows, columns], sems.at[2 * i + b]
-                )
-            )
+            if along == "x":
+                goal = target.at[b, at, :, :, columns]
+            else:
+                goal = target.at[b, :, at, :, columns]
+            copies.append(pltpu.make_async_copy(piece.at[b], goal, sems.at[2 * i + b]))
     return copies
 
 
-def pack_local(info, att_in, att_out, mix_in, mix_out, out):
+def weight(weights, b, first, last):
+    return weights[b, :, :, :, first:last].reshape(WIDTH, last - first)
+
+
+def pack_local(info, slopes, att_in, att_out, mix_in, mix_out, taps, bias, gnorm, out, own):
     for i in range(3):
         out[:, i * 256 : (i + 1) * 256] = att_in[i]
     for i in range(2):
         out[:, 768 + i * 768 : 768 + (i + 1) * 768] = mix_in[:, i, :]
     out[:, 2304:3072] = mix_out[...]
     out[:, 3072:3328] = att_out[...]
-
-
-def spread_block(info, local, other, out):
+    own[0:31, :] = taps[...]
+    own[31, :] = bias[...]
+    own[32:34, :] = gnorm[...]
+    lane = lax.broadcasted_iota(jnp.int32, (1, 768), 1)
+    row = jnp.zeros((1, 768), F32)
+    for r in range(4):
+        row = jnp.where(lane == r, slopes[r], row)
+    own[34:35, :] = row
+
+
+def pair_rows(info, local, other, out):
     core = info[INFO_CORE]
     mine, theirs = local[...].astype(F32), other[...].astype(F32)
     rows = jnp.concatenate(
         [jnp.where(core == 0, mine, theirs), jnp.where(core == 0, theirs, mine)], axis=0
     )
-    block = jnp.concatenate(
-        [
-            jnp.where(core == 0, rows[:, 0:384], rows[:, 384:768]),
-            jnp.where(core == 0, rows[:, 768:2048], rows[:, 2048:3328]),
-        ],
-        axis=1,
-    ).astype(BF16)
-    for j in range(16):
-        out[j] = block
+    out[:, 0:384] = jnp.where(core == 0, rows[:, 0:384], rows[:, 384:768]).astype(BF16)
+    out[:, 384:1664] = jnp.where(core == 0, rows[:, 768:2048], rows[:, 2048:3328]).astype(BF16)
+
+
+def join_y(info, *rest):
+    pieces, (first, second) = rest[:4], rest[4:]
+    for piece, s in zip(pieces, SHIFTS):
+        y = lax.rem(info[INFO_Y] + (4 - s), 4)
+        at = lax.rem(y, 2) * 2 + y // 2
+        first[at] = piece[:, 0:384]
+        second[at] = piece[:, 384:1664]
+
+
+def join_planes(info, *rest):
+    over_z, over_x, (attend, mixer) = rest[:4], rest[4:8], rest[8:]
+    for i, s in enumerate(SHIFTS):
+        z = lax.rem(info[INFO_Z] + (4 - s), 4)
+        x = lax.rem(info[INFO_X] + (4 - s), 4)
+        for b in range(2):
+            here = slice(b * 2, b * 2 + 2)
+            attend[b, pl.ds(z * 2, 2)] = over_z[i][here]
+            mixer[b, pl.ds(x * 2, 2)] = over_x[i][here]
 
 
 def fill_distance(distance):
@@ -175,9 +202,9 @@
     normed, _ = standardize(frames[0, 0])
     low = (normed * norm[0:1] + norm[1:2]).astype(BF16)
     for b in range(2):
-        part = dot_tt(weights[b, :, 0:256], low) * (HEAD**-0.5)
+        part = dot_tt(weight(weights, b, 0, 256), low) * (HEAD**-0.5)
         triple[0, b * 768 : b * 768 + 256, :] = part.astype(BF16)
-        part = dot_tt(weights[b, :, 256:768], low)
+        part = dot_tt(weight(weights, b, 256, 768), low)
         triple[0, b * 768 + 256 : (b + 1) * 768, :] = part.astype(BF16)
     is_key = lax.broadcasted_iota(jnp.int32, (SLOT, SLOT), 0) < info[INFO_LENGTH + step]
 
@@ -210,6 +237,7 @@
     other,
     forward,
     inverse,
+    inverse_three,
     tap_forward,
     tap_inverse,
     *rest,
@@ -247,7 +275,7 @@
     step = pl.program_id(0)
     branch, core = info[INFO_BRANCH], info[INFO_CORE]
     here = pl.ds(pl.multiple_of(step * SLOT, SLOT), SLOT)
-    copies = piece_copies(info, pieces, weights, sems)
+    copies = piece_copies(info, pieces, weights, sems, "z")
 
     @pl.when(step == 0)
     def _():
@@ -256,9 +284,9 @@
         params_s[branch] = own[...]
         params_s[1 - branch] = other[...]
         for b in range(2):
-            high, low = split_low(params_s[b, 0:32, :])
-            stacked = jnp.concatenate([high, low, high], axis=0).astype(BF16)
-            tap_spec[:, b * 768 : (b + 1) * 768] = dot_nn(tap_forward[...], stacked)
+            tap_spec[:, b * 768 : (b + 1) * 768] = dot_nn(
+                tap_forward[...], stack_terms(params_s[b, 0:32, :])
+            )
         cross_s[...] = jnp.zeros_like(cross_s)
         small_wide[...] = jnp.zeros_like(small_wide)
         small_narrow[...] = jnp.zeros_like(small_narrow)
@@ -279,8 +307,8 @@
         for k in range(BLOCKS)
     ]
 
-    def weight(b, kind, off):
-        return weights[b, :, kind * 768 + off.start : kind * 768 + off.stop]
+    def part(b, kind, off):
+        return weight(weights, b, kind * 768 + off.start, kind * 768 + off.stop)
 
     def fold(v):
         return v[:, 0:128] + v[:, 128:256]
@@ -290,7 +318,7 @@
 
     total = jnp.zeros((SLOT, 128), F32)
     for b, off, wide in places:
-        active, slope = gelu_pair(dot_nn(low, weight(b, 1, off)))
+        active, slope = gelu_pair(dot_nn(low, part(b, 1, off)))
         second_s[:, wide] = active
         second_slope[:, wide] = slope
         total += fold(active)
@@ -304,26 +332,26 @@
     for b, off, wide in places:
         standard = (second_s[:, wide] - average) * gate_rstd
         gate_in = (standard * params_s[b, 32:33, off] + params_s[b, 33:34, off]) * valid
-        spec = dot_nn(forward[...], gate_in.astype(BF16))
+        spec = dot_nn(forward[...], stack_terms(gate_in))
         spec_s[:, wide] = spec
         real, imag = spec[0:BINS], spec[BINS:SPEC]
         tap_real, tap_imag = tap_spec[0:BINS, wide], tap_spec[BINS:SPEC, wide]
         product = jnp.concatenate(
             [real * tap_real + imag * tap_imag, imag * tap_real - real * tap_imag], axis=0
         )
-        conved = dot_nn(inverse[...], product.astype(BF16)) + params_s[b, 31:32, off]
+        conved = dot_nn(inverse_three[...], stack_terms(product)) + params_s[b, 31:32, off]
         conv_s[:, wide] = conved
-        active, slope = gelu_pair(dot_nn(low, weight(b, 0, off)))
+        active, slope = gelu_pair(dot_nn(low, part(b, 0, off)))
         first_s[:, wide] = active
         first_slope[:, wide] = slope
         gated_s[here, wide] = (active * conved).astype(BF16)
 
-    mixer_part = dot_nt(gated_s[here, 0:768], weights[0, :, 1536:2304]) + dot_nt(
-        gated_s[here, 768:1536], weights[1, :, 1536:2304]
+    mixer_part = dot_nt(gated_s[here, 0:768], weight(weights, 0, 1536, 2304)) + dot_nt(
+        gated_s[here, 768:1536], weight(weights, 1, 1536, 2304)
     )
     context_s[:, here] = context[0]
-    attend_part = dot_tt(context[0, 0:256, :], weights[0, :, 2304:2560]) + dot_tt(
-        context[0, 256:512, :], weights[1, :, 2304:2560]
+    attend_part = dot_tt(context[0, 0:256, :], weight(weights, 0, 2304, 2560)) + dot_tt(
+        context[0, 256:512, :], weight(weights, 1, 2304, 2560)
     )
     merged = rows_in + mix_attend * attend_part + mix_mixer * mixer_part
     merged_normed, merged_rstd = standardize(merged)
@@ -345,16 +373,16 @@
     attend_s[here, :] = grad_attend
     for b in range(2):
         grad_context[0, b * 256 : (b + 1) * 256, :] = dot_tt(
-            weights[b, :, 2304:2560], grad_attend
+            weight(weights, b, 2304, 2560), grad_attend
         ).astype(BF16)
 
     total, cross_total = jnp.zeros((SLOT, 128), F32), jnp.zeros((SLOT, 128), F32)
     for b, off, wide in places:
-        grad_gated = dot_nn(grad_mixer, weight(b, 2, off))
+        grad_gated = dot_nn(grad_mixer, part(b, 2, off))
         grad_conved = grad_gated * first_s[:, wide]
         hidden_s[here, wide] = (first_slope[:, wide] * (grad_gated * conv_s[:, wide])).astype(BF16)
         small_wide[31:32, wide] += jnp.sum(grad_conved, axis=0, keepdims=True)
-        grad_spec = dot_nn(forward[...], grad_conved.astype(BF16))
+        grad_spec = dot_nn(forward[:, 0:SLOT], grad_conved.astype(BF16))
         grad_real, grad_imag = grad_spec[0:BINS], grad_spec[BINS:SPEC]
         real, imag = spec_s[0:BINS, wide], spec_s[BINS:SPEC, wide]
         cross_s[0:BINS, wide] += grad_real * real + grad_imag * imag
@@ -385,11 +413,11 @@
             second_slope[:, wide] * grad_second
         ).astype(BF16)
     grad_low = (
-        dot_nt(hidden_s[here, 0:768], weights[0, :, 0:768])
-        + dot_nt(hidden_s[here, 768:1536], weights[1, :, 0:768])
+        dot_nt(hidden_s[here, 0:768], weight(weights, 0, 0, 768))
+        + dot_nt(hidden_s[here, 768:1536], weight(weights, 1, 0, 768))
     ) + (
-        dot_nt(hidden_s[here, 1536:2304], weights[0, :, 768:1536])
-        + dot_nt(hidden_s[here, 2304:3072], weights[1, :, 768:1536])
+        dot_nt(hidden_s[here, 1536:2304], weight(weights, 0, 768, 1536))
+        + dot_nt(hidden_s[here, 2304:3072], weight(weights, 1, 768, 1536))
     )
     small_narrow[4:5] += jnp.sum(grad_low * normed, axis=0, keepdims=True)
     small_narrow[5:6] += jnp.sum(grad_low, axis=0, keepdims=True)
@@ -403,39 +431,45 @@
     @pl.when(step == UTTS - 1)
     def _():
         outs = []
-        for half in range(2):
-            for b in range(2):
-                if half == 0:
-                    parts = [
-                        dot_tn(low_s[...], hidden_s[:, b * 768 : (b + 1) * 768]),
-                        dot_tn(low_s[...], hidden_s[:, HALF + b * 768 : HALF + b * 768 + 512]),
-                    ]
-                else:
-                    parts = [
-                        dot_tn(
-                            low_s[...], hidden_s[:, HALF + b * 768 + 512 : HALF + (b + 1) * 768]
-                        ),
-                        dot_tn(grad_s[...], gated_s[:, b * 768 : (b + 1) * 768]),
-                        dot_tt(attend_s[...], context_s[b * 256 : (b + 1) * 256, :]),
-                    ]
-                column = 0
-                for part in parts:
-                    grads_s[half, b, :, column : column + part.shape[1]] = part.astype(BF16)
-                    column += part.shape[1]
-                for i, target in enumerate((keep, send)):
-                    copy = pltpu.make_async_copy(
-                        grads_s.at[half, b], target.at[b], sems.at[half * 2 + b]
+        for b in range(2):
+            first, second = b * 768, HALF + b * 768
+            pairs = [
+                (dot_tn(low_s[...], hidden_s[:, first : first + 256]),
+                 dot_tn(low_s[...], hidden_s[:, second + 512 : second + 768])),
+                (dot_tn(low_s[...], hidden_s[:, first + 256 : first + 512]),
+                 dot_tn(grad_s[...], gated_s[:, first : first + 256])),
+                (dot_tn(low_s[...], hidden_s[:, first + 512 : first + 768]),
+                 dot_tn(grad_s[...], gated_s[:, first + 256 : first + 512])),
+                (dot_tn(low_s[...], hidden_s[:, second : second + 256]),
+                 dot_tn(grad_s[...], gated_s[:, first + 512 : first + 768])),
+                (dot_tn(low_s[...], hidden_s[:, second + 256 : second + 512]),
+                 dot_tt(attend_s[...], context_s[b * 256 : (b + 1) * 256, :])),
+            ]
+            for i, (upper, lower) in enumerate(pairs):
+                upper, lower = upper.reshape(32, 2, 8, 256), lower.reshape(32, 2, 8, 256)
+                for p in range(2):
+                    grads_s[p, b * 32 : (b + 1) * 32, :, i * 256 : (i + 1) * 256] = (
+                        jnp.concatenate([upper[:, p], lower[:, p]], axis=1).astype(BF16)
                     )
-                    outs.append((core == half if i == 0 else core != half, copy))
-                    pl.when(outs[-1][0])(copy.start)
+            chips = pl.ds(b * 32, 32)
+            outs += start_all(
+                [
+                    pltpu.make_async_copy(
+                        grads_s.at[core, chips], keep.at[chips], sems.at[2 * b]
+                    ),
+                    pltpu.make_async_copy(
+                        grads_s.at[1 - core, chips], send.at[chips], sems.at[2 * b + 1]
+                    ),
+                ]
+            )
         tap_grad = dot_nn(tap_inverse[...], cross_s[...].astype(BF16))
         small_wide[0:31, :] = tap_grad[0:31]
         for g in range(12):
             small[g * 40 : (g + 1) * 40, :] = small_wide[:, g * 128 : (g + 1) * 128]
         for j in range(4):
             small[480 + 8 * j : 488 + 8 * j, :] = small_narrow[:, j * 128 : (j + 1) * 128]
-        for wanted, copy in outs:
-            pl.when(wanted)(copy.wait)
+        for copy in outs:
+            copy.wait()
 
 
 def attend_backward(
@@ -455,12 +489,11 @@
     low_s,
     triple_t,
     small,
-    grads_s,
+    terms,
     sems,
 ):
     step = pl.program_id(0)
     here = pl.ds(pl.multiple_of(step * SLOT, SLOT), SLOT)
-    core = info[INFO_CORE]
 
     @pl.when(step == 0)
     def _():
@@ -495,8 +528,8 @@
         return carry
 
     lax.fori_loop(0, HEADS, head, 0, unroll=HEAD_UNROLL)
-    grad_low = dot_tt(triple_t[0:768, here], weights[0]) + dot_tt(
-        triple_t[768:1536, here], weights[1]
+    grad_low = dot_tt(triple_t[0:768, here], weight(weights, 0, 0, 768)) + dot_tt(
+        triple_t[768:1536, here], weight(weights, 1, 0, 768)
     )
     gain_row = jnp.sum(grad_low * normed, axis=0, keepdims=True)
     bias_row = jnp.sum(grad_low, axis=0, keepdims=True)
@@ -516,30 +549,35 @@
 
     @pl.when(step == UTTS - 1)
     def _():
-        high, low = split_low(small[...])
-        pair = jnp.concatenate([high, low], axis=1).astype(BF16)
-        outs = []
-        for half in range(2):
-            for b in range(2):
-                rows = b * 768 + half * 512
-                if half == 0:
-                    grads_s[half, b] = dot_tt(low_s[...], triple_t[rows : rows + 512, :]).astype(
-                        BF16
-                    )
-                else:
-                    grads_s[half, b, :, 0:256] = dot_tt(
-                        low_s[...], triple_t[rows : rows + 256, :]
-                    ).astype(BF16)
-                    for m in range(32):
-                        grads_s[half, b, 16 * m : 16 * m + 16, 256:512] = pair
-                for i, target in enumerate((keep, send)):
-                    copy = pltpu.make_async_copy(
-                        grads_s.at[half, b], target.at[b], sems.at[half * 2 + b]
-                    )
-                    outs.append((core == half if i == 0 else core != half, copy))
-                    pl.when(outs[-1][0])(copy.start)
-        for wanted, copy in outs:
-            pl.when(wanted)(copy.wait)
+        high, low = split_low(jnp.sum(small[8:16, :], axis=1, keepdims=True))
+        block = jnp.concatenate([small[0:8, :], slope_rows(high, low)], axis=0).astype(BF16)
+        for b in range(2):
+            grads = dot_tt(low_s[...], triple_t[b * 768 : (b + 1) * 768, :]).reshape(32, 2, 8, 768)
+            for p in range(2):
+                terms[p, b * 32 : (b + 1) * 32, :, 0:384] = jnp.concatenate(
+                    [grads[:, p, :, 0:384], grads[:, p, :, 384:768]], axis=1
+                ).astype(BF16)
+                for m in range(32):
+                    terms[p, b * 32 + m, :, 384:512] = block
+        core = info[INFO_CORE]
+        outs = start_all(
+            [
+                pltpu.make_async_copy(terms.at[core], keep, sems.at[0]),
+                pltpu.make_async_copy(terms.at[1 - core], send, sems.at[1]),
+            ]
+        )
+        for copy in outs:
+            copy.wait()
+
+
+def stack_terms(value):
+    high, low = split_low(value)
+    return jnp.concatenate([high, low, high], axis=0).astype(BF16)
+
+
+def slope_rows(high, low):
+    lane = lax.broadcasted_iota(jnp.int32, (8, 128), 1)
+    return jnp.where(lane == 0, high, jnp.where(lane == 1, low, 0.0))
 
 
 def split_low(value):
@@ -568,83 +606,130 @@
 CHUNKS = 8
 
 
-def sum_mixer(info, keep, other, small, small_other, out, keep_s, other_s, out_s, sems):
-    first = chunk_copies(keep, keep_s, CHUNKS, sems.at[0])
-    second = chunk_copies(other, other_s, CHUNKS, sems.at[1])
+def sum_pairs(info, keep, other, pieces, keep_s, other_s, out_s, sems):
+    loads = []
+    for i, s in enumerate(SHIFTS):
+        x = lax.rem(info[INFO_X] + s, 4)
+        for b in range(2):
+            chips = pl.ds(b * 32 + x * 8, 8)
+            here = pl.ds(b * 8, 8)
+            loads.append(
+                start_all(
+                    [
+                        pltpu.make_async_copy(
+                            source.at[chips], target.at[i, here], sems.at[p, 2 * i + b]
+                        )
+                        for p, (source, target) in enumerate(((keep, keep_s), (other, other_s)))
+                    ]
+                )
+            )
+    stores = []
+    columns = keep.shape[2]
+    for i in (1, 2, 3, 0):
+        for b in range(2):
+            for copy in loads[2 * i + b]:
+                copy.wait()
+            here = slice(b * 8, b * 8 + 8)
+            out_s[i, here, :, 0:columns] = (
+                keep_s[i, here].astype(F32) + other_s[i, here].astype(F32)
+            ).astype(BF16)
+        yield i
+        stores.append(pltpu.make_async_copy(out_s.at[i], pieces[i], sems.at[2, i]))
+        stores[-1].start()
+    for copy in stores:
+        copy.wait()
+
+
+def spread_small(small, small_other, out):
     high, low = split_low(small[...] + small_other[...])
-    for j in range(64):
-        rows = slice(8 * j, 8 * j + 8)
-        out_s[16 * j : 16 * j + 16, 1280:1408] = jnp.concatenate(
-            [high[rows], low[rows]], axis=0
-        ).astype(BF16)
-    outs = []
-    for i in range(CHUNKS):
-        rows = slice(i * 128, (i + 1) * 128)
-        first[i].wait()
-        second[i].wait()
-        out_s[rows, 0:1280] = (keep_s[rows].astype(F32) + other_s[rows].astype(F32)).astype(BF16)
-        outs.append(pltpu.make_async_copy(out_s.at[rows], out.at[rows], sems.at[2, i]))
-        outs[-1].start()
-    for copy in outs:
-        copy.wait()
-
-
-def sum_attend(info, keep, other, mixer_total, out, keep_s, other_s, out_s, sems):
-    first = chunk_copies(keep, keep_s, CHUNKS, sems.at[0])
-    second = chunk_copies(other, other_s, CHUNKS, sems.at[1])
-    high, low = split_low(mixer_total[0:8, :] + mixer_total[8:16, :])
-    block = jnp.concatenate([high, low], axis=0).astype(BF16)
-    outs = []
-    for i in range(CHUNKS):
-        rows = slice(i * 128, (i + 1) * 128)
-        first[i].wait()
-        second[i].wait()
-        total = keep_s[rows].astype(F32) + other_s[rows].astype(F32)
-        out_s[rows, 0:512] = total.astype(BF16)
-
-        @pl.when(info[INFO_CORE] == 1)
-        def _():
-            high, low = split_low(total[:, 256:384] + total[:, 384:512])
-            out_s[rows, 256:384] = high.astype(BF16)
-            out_s[rows, 384:512] = low.astype(BF16)
-
-        for j in range(8):
-            out_s[i * 128 + 16 * j : i * 128 + 16 * j + 16, 512:640] = block
-        outs.append(pltpu.make_async_copy(out_s.at[rows], out.at[rows], sems.at[2, i]))
-        outs[-1].start()
-    for copy in outs:
-        copy.wait()
-
-
-def sum_chips(info, terms, out, *rest):
-    small = rest[0] if len(rest) == 3 else None
-    terms_s, sems = rest[-2:]
-    copies = chunk_copies(terms, terms_s, CHUNKS, sems)
-    columns = out.shape[1]
-    for c in range(CHUNKS):
-        copies[c].wait()
-        parts = [terms_s[8 * c + i, :, 0:columns].astype(F32) for i in range(8)]
-        total = ((parts[0] + parts[1]) + (parts[2] + parts[3])) + (
-            (parts[4] + parts[5]) + (parts[6] + parts[7])
+    for j in range(16):
+        for x in range(4):
+            chip = (j // 8 * 4 + x) * 8 + j % 8
+            rows = slice(8 * chip, 8 * chip + 8)
+            out[j, 16 * x : 16 * x + 16, :] = jnp.concatenate(
+                [high[rows], low[rows]], axis=0
+            ).astype(BF16)
+
+
+def sum_mixer(info, keep, other, small, small_other, *rest):
+    pieces, (small_out, keep_s, other_s, out_s, sems) = rest[:4], rest[4:]
+    sums = sum_pairs(info, keep, other, pieces, keep_s, other_s, out_s, sems)
+    next(sums)
+    spread_small(small, small_other, small_out)
+    for _ in sums:
+        pass
+
+
+def sum_attend(info, keep, other, small_terms, *rest):
+    pieces, (keep_s, other_s, out_s, sems) = rest[:4], rest[4:]
+    total = (small_terms[0].astype(F32) + small_terms[1].astype(F32)) + (
+        small_terms[2].astype(F32) + small_terms[3].astype(F32)
+    )
+    for i in range(4, 16):
+        total += small_terms[i].astype(F32)
+    chunks = []
+    for x in range(4):
+        high, low = split_low(total[16 * x : 16 * x + 8] + total[16 * x + 8 : 16 * x + 16])
+        chunks.append(jnp.concatenate([high, low], axis=0))
+    chunks = jnp.concatenate(chunks, axis=1).astype(BF16)
+    for i in sum_pairs(info, keep, other, pieces, keep_s, other_s, out_s, sems):
+        total = keep_s[i, 0, :, 384:512].astype(F32) + other_s[i, 0, :, 384:512].astype(F32)
+        high, low = split_low(total[8:16, 0:1] + total[8:16, 1:2])
+        block = jnp.concatenate([total[0:8], slope_rows(high, low)], axis=0).astype(BF16)
+        for j in range(16):
+            out_s[i, j, :, 384:512] = block
+        out_s[i, 16] = chunks
+
+
+def sum_four(info, *rest):
+    terms, (out, terms_s, sems) = rest[:4], rest[4:]
+    loads = [
+        start_all(
+            [
+                pltpu.make_async_copy(
+                    terms[i].at[pl.ds(c * 4, 4)], terms_s.at[i, pl.ds(c * 4, 4)], sems.at[i, c]
+                )
+                for i in range(4)
+            ]
         )
-        if c == 0:
-            out[...] = total
-        else:
-            out[...] += total
-        if small is not None:
-            for i in range(8 * c, 8 * c + 8):
-                pair = terms_s[i, :, columns : columns + 128].astype(F32)
-                small[8 * i : 8 * i + 8, :] = pair[0:8] + pair[8:16]
+        for c in range(4)
+    ]
+    for c in range(4):
+        for copy in loads[c]:
+            copy.wait()
+        here = slice(c * 4, c * 4 + 4)
+        total = (terms_s[0, here].astype(F32) + terms_s[1, here].astype(F32)) + (
+            terms_s[2, here].astype(F32) + terms_s[3, here].astype(F32)
+        )
+        out[here] = total.astype(BF16)
+
+
+def join_terms(info, mixer, *rest):
+    terms, out = rest[0:4], rest[4]
+    for j in range(16):
+        out[j, :, 0:1280] = mixer[j]
+        total = (terms[0][j].astype(F32) + terms[1][j].astype(F32)) + (
+            terms[2][j].astype(F32) + terms[3][j].astype(F32)
+        )
+        out[j, :, 1280:1664] = total[:, 0:384].astype(BF16)
+        if j == 0:
+            little = total[:, 384:512]
+            high, low = split_low(little[8:16, 0:1] + little[8:16, 1:2])
+            block = jnp.concatenate([little[0:8], slope_rows(high, low)], axis=0).astype(BF16)
+        out[j, :, 1664:1792] = block
+    total = (terms[0][16].astype(F32) + terms[1][16].astype(F32)) + (
+        terms[2][16].astype(F32) + terms[3][16].astype(F32)
+    )
+    high, low = split_low(total[0:8] + total[8:16])
+    chunks = jnp.concatenate([high, low], axis=0).astype(BF16)
+    for j in range(16):
+        out[j, :, 1792:2304] = chunks
 
 
 def finish(
     info,
     merge_logits,
-    mixer_mine,
-    mixer_theirs,
-    mine,
-    theirs,
-    small,
+    terms,
     att_in,
     att_out,
     mix_in,
@@ -657,37 +742,32 @@
     bias,
     slope,
     merge,
+    terms_s,
+    small,
+    sems,
 ):
-    core, branch = info[INFO_CORE], info[INFO_BRANCH]
-
-    def rows(v):
-        return jnp.where(core == 0, v[0:8], v[8:16])
-
-    def halves(a, b):
-        return jnp.where(core == 0, a, b), jnp.where(core == 0, b, a)
-
-    low, high = halves(rows(mixer_mine), rows(mixer_theirs))
-    first, second = halves(mine[...], theirs[...])
-    att_in[0] = rows(first)[:, 0:256]
-    att_in[1] = rows(first)[:, 256:512]
-    att_in[2] = rows(second)[:, 0:256]
-    mix_in[:, 0, :] = low[:, 0:768]
-    mix_in[:, 1, :] = jnp.concatenate([low[:, 768:1280], high[:, 0:256]], axis=1)
-    mix_out[...] = high[:, 256:1024]
-    att_out[...] = high[:, 1024:1280]
-    little = second[:, 256:384] + second[:, 384:512]
-    for p in range(2):
-        for j in range(4):
-            anorm[p : p + 1, j * 128 : (j + 1) * 128] = little[p * 4 + j : p * 4 + j + 1]
-    for r in range(4):
-        slope[r] = jnp.where(
-            branch == 0, jnp.sum(little[8 + r : 9 + r]), jnp.sum(little[12 + r : 13 + r])
-        )
+    branch = info[INFO_BRANCH]
+    copies = chunk_copies(terms, terms_s, CHUNKS, sems)
+    total = jnp.zeros((16, 1792), F32)
+    for c in range(CHUNKS):
+        copies[c].wait()
+        for i in range(c * 2, c * 2 + 2):
+            total += terms_s[i, :, 0:1792].astype(F32)
+            for x in range(4):
+                pair = terms_s[i, :, 1792 + x * 128 : 1920 + x * 128].astype(F32)
+                chip = (i // 8 * 4 + x) * 8 + i % 8
+                small[8 * chip : 8 * chip + 8, :] = pair[0:8] + pair[8:16]
+    upper, lower = total[0:8], total[8:16]
+    mix_in[:, 0, :] = upper[:, 0:768]
+    mix_in[:, 1, :] = jnp.concatenate([upper[:, 768:1280], lower[:, 0:256]], axis=1)
+    mix_out[...] = lower[:, 256:1024]
+    att_out[...] = lower[:, 1024:1280]
+    total = total[:, 1280:1792]
     for g in range(6):
         group = small[pl.ds(pl.multiple_of((branch * 6 + g) * 40, 8), 40), :]
         columns = slice(g * 128, (g + 1) * 128)
         taps[:, columns] = group[0:31]
-        bias[:, columns] = group[31:32]
+        bias[columns] = group[31]
         gnorm[:, columns] = group[32:34]
     attend_sum, mixer_sum = 0.0, 0.0
     for j in range(4):
@@ -701,6 +781,18 @@
     average = mix_attend * attend_sum + mix_mixer * mixer_sum
     merge[0] = jnp.sum(mix_attend * (attend_sum - average))
     merge[1] = jnp.sum(mix_mixer * (mixer_sum - average))
+    att_in[0] = total[0:8, 0:256]
+    att_in[1] = jnp.concatenate([total[0:8, 256:384], total[8:16, 0:128]], axis=1)
+    att_in[2] = total[8:16, 128:384]
+    for p in range(2):
+        for j in range(4):
+            r = p * 4 + j
+            anorm[p : p + 1, j * 128 : (j + 1) * 128] = total[r : r + 1, 384:512]
+    slopes = total[8:16, 384:385] + total[8:16, 385:386]
+    for r in range(4):
+        slope[r] = jnp.where(
+            branch == 0, jnp.sum(slopes[r : r + 1]), jnp.sum(slopes[4 + r : 5 + r])
+        )
 
 
 def place_pair(info, own, other, out, own_s, other_s, out_s, sems):
@@ -770,27 +862,53 @@
     )(info, *operands)
 
 
-def run_pack(info, *operands):
+def run_pack(info, slopes, *operands):
     return call(
         pack_local,
         "pack_local",
         info,
-        operands,
-        [whole(a.shape) for a in operands],
-        struct(8, 3328, dtype=BF16),
-        whole((8, 3328)),
-    )
-
-
-def run_spread(info, local, other):
+        (slopes, *operands),
+        [pl.BlockSpec(memory_space=pltpu.SMEM)] + [whole(a.shape) for a in operands],
+        [struct(8, 3328, dtype=BF16), struct(35, 768)],
+        [whole((8, 3328)), whole((35, 768))],
+    )
+
+
+def run_pair(info, local, other):
     return call(
-        spread_block,
-        "spread_block",
+        pair_rows,
+        "pair_rows",
         info,
         (local, other),
         [whole((8, 3328))] * 2,
-        struct(16, 16, 1664, dtype=BF16),
-        whole((16, 16, 1664)),
+        struct(16, 1664, dtype=BF16),
+        whole((16, 1664)),
+    )
+
+
+def run_join_y(info, pieces):
+    shapes = [(4, 16, 384), (4, 16, 1280)]
+    return call(
+        join_y,
+        "join_y",
+        info,
+        pieces,
+        [whole((16, 1664))] * 4,
+        [struct(*s, dtype=BF16) for s in shapes],
+        [whole(s) for s in shapes],
+    )
+
+
+def run_join_planes(info, over_z, over_x):
+    shapes = [(2, 8, 16, 384), (2, 8, 16, 1280)]
+    return call(
+        join_planes,
+        "join_planes",
+        info,
+        (*over_z, *over_x),
+        [whole((4, 16, 384))] * 4 + [whole((4, 16, 1280))] * 4,
+        [struct(*s, dtype=BF16) for s in shapes],
+        [whole(s) for s in shapes],
     )
 
 
@@ -805,14 +923,14 @@
             struct(UTTS, HALF, SLOT, dtype=BF16),
             struct(UTTS, WIDTH, SLOT, dtype=BF16),
             struct(UTTS, HEADS, SLOT),
-            struct(2, WIDTH, 768, dtype=BF16),
+            struct(2, 4, 4, 32, 768, dtype=BF16),
             struct(HEADS, 128),
         ],
         [
             per_utt((HALF, SLOT)),
             per_utt((WIDTH, SLOT)),
             per_utt((HEADS, SLOT)),
-            whole((2, WIDTH, 768)),
+            whole((2, 4, 4, 32, 768)),
             whole((HEADS, 128)),
         ],
         [scratch(HEADS, SLOT, SLOT), pltpu.SemaphoreType.DMA((16,))],
@@ -821,10 +939,11 @@
 
 
 def run_mixer(info, frames, cotangent, context, mnorm, fnorm, merge_logits, own, other, pieces):
-    forward, inverse, tap_forward, tap_inverse = transform_tables()
+    forward, inverse, inverse_three, tap_forward, tap_inverse = transform_tables()
     tables = (
         jnp.asarray(forward, BF16),
         jnp.asarray(inverse, BF16),
+        jnp.asarray(inverse_three, BF16),
         jnp.asarray(tap_forward, BF16),
         jnp.asarray(tap_inverse, BF16),
     )
@@ -842,8 +961,9 @@
             whole((1, 2)),
             whole((35, 768)),
             whole((35, 768)),
-            whole((SPEC, SLOT)),
+            whole((SPEC, 3 * SLOT)),
             whole((SLOT, SPEC)),
+            whole((SLOT, 3 * SPEC)),
             whole((SPEC, 96)),
             whole((32, SPEC)),
         ]
@@ -852,8 +972,8 @@
             struct(UTTS, SLOT, WIDTH, dtype=BF16),
             struct(UTTS, SLOT, WIDTH),
             struct(UTTS, WIDTH, SLOT, dtype=BF16),
-            struct(2, WIDTH, 1280, dtype=BF16),
-            struct(2, WIDTH, 1280, dtype=BF16),
+            struct(64, 16, 1280, dtype=BF16),
+            struct(64, 16, 1280, dtype=BF16),
             struct(512, 128),
         ],
         [
@@ -865,7 +985,7 @@
             whole((512, 128)),
         ],
         [
-            scratch(2, WIDTH, 2560, dtype=BF16),
+            scratch(2, 4, 4, 32, 2560, dtype=BF16),
             scratch(2, 35, 768),
             scratch(40, HALF),
             scratch(8, WIDTH),
@@ -884,7 +1004,7 @@
             scratch(ROWS, WIDTH, dtype=BF16),
             scratch(ROWS, WIDTH, dtype=BF16),
             scratch(WIDTH, ROWS, dtype=BF16),
-            scratch(2, 2, WIDTH, 1280, dtype=BF16),
+            scratch(2, 64, 16, 1280, dtype=BF16),
             pltpu.SemaphoreType.DMA((16,)),
         ],
         grid=UTTS,
@@ -907,12 +1027,12 @@
             per_utt((WIDTH, SLOT)),
             whole((2, WIDTH)),
             whole((HEADS, 128)),
-            whole((2, WIDTH, 768)),
+            whole((2, 4, 4, 32, 768)),
         ],
         [
             struct(UTTS, SLOT, WIDTH, dtype=BF16),
-            struct(2, WIDTH, 512, dtype=BF16),
-            struct(2, WIDTH, 512, dtype=BF16),
+            struct(64, 16, 512, dtype=BF16),
+            struct(64, 16, 512, dtype=BF16),
         ],
         [per_utt((SLOT, WIDTH)), ANY, ANY],
         [
@@ -920,61 +1040,65 @@
             scratch(ROWS, WIDTH, dtype=BF16),
             scratch(HALF, ROWS, dtype=BF16),
             scratch(16, 128),
-            scratch(2, 2, WIDTH, 512, dtype=BF16),
-            pltpu.SemaphoreType.DMA((4,)),
+            scratch(2, 64, 16, 512, dtype=BF16),
+            pltpu.SemaphoreType.DMA((2,)),
         ],
         grid=UTTS,
     )
 
 
 def run_sum_mixer(info, keep, other, small, small_other):
+    piece = (16, 16, 1280)
     return call(
         sum_mixer,
         "sum_mixer",
         info,
-        (keep.reshape(1024, 1280), other.reshape(1024, 1280), small, small_other),
+        (keep, other, small, small_other),
         [ANY, ANY, whole((512, 128)), whole((512, 128))],
-        struct(1024, 1408, dtype=BF16),
-        ANY,
-        [
-            scratch(1024, 1280, dtype=BF16),
-            scratch(1024, 1280, dtype=BF16),
-            scratch(1024, 1408, dtype=BF16),
-            pltpu.SemaphoreType.DMA((3, CHUNKS)),
-        ],
-    )
-
-
-def run_sum_attend(info, keep, other, mixer_total):
+        [struct(*piece, dtype=BF16)] * 4 + [struct(16, 64, 128, dtype=BF16)],
+        [ANY] * 4 + [whole((16, 64, 128))],
+        [scratch(4, *piece, dtype=BF16)] * 3 + [pltpu.SemaphoreType.DMA((3, 8))],
+    )
+
+
+def run_sum_attend(info, keep, other, small_terms):
+    piece, wider = (16, 16, 512), (17, 16, 512)
     return call(
         sum_attend,
         "sum_attend",
         info,
-        (keep.reshape(1024, 512), other.reshape(1024, 512), mixer_total),
-        [ANY, ANY, pl.BlockSpec((16, 128), lambda i, *_: (0, 10))],
-        struct(1024, 640, dtype=BF16),
-        ANY,
-        [
-            scratch(1024, 512, dtype=BF16),
-            scratch(1024, 512, dtype=BF16),
-            scratch(1024, 640, dtype=BF16),
-            pltpu.SemaphoreType.DMA((3, CHUNKS)),
-        ],
-    )
-
-
-def run_sum_chips(info, terms, small):
-    columns = terms.shape[2]
-    outs = [struct(16, columns)] if not small else [struct(16, columns - 128), struct(512, 128)]
+        (keep, other, small_terms),
+        [ANY, ANY, whole((16, 64, 128))],
+        [struct(*wider, dtype=BF16)] * 4,
+        [ANY] * 4,
+        [scratch(4, *piece, dtype=BF16)] * 2
+        + [scratch(4, *wider, dtype=BF16), pltpu.SemaphoreType.DMA((3, 8))],
+    )
+
+
+def run_sum_four(info, terms):
+    piece = terms[0].shape
     return call(
-        sum_chips,
-        "sum_chips",
-        info,
-        (terms,),
-        [ANY],
-        outs,
-        [whole(o.shape) for o in outs],
-        [scratch(*terms.shape, dtype=BF16), pltpu.SemaphoreType.DMA((CHUNKS,))],
+        sum_four,
+        "sum_four",
+        info,
+        terms,
+        [ANY] * 4,
+        struct(*piece, dtype=BF16),
+        whole(piece),
+        [scratch(4, *piece, dtype=BF16), pltpu.SemaphoreType.DMA((4, 4))],
+    )
+
+
+def run_join(info, mixer, terms):
+    return call(
+        join_terms,
+        "join_terms",
+        info,
+        (mixer, *terms),
+        [whole(mixer.shape)] + [whole(terms[0].shape)] * 4,
+        struct(16, 16, 2304, dtype=BF16),
+        whole((16, 16, 2304)),
     )
 
 
@@ -989,7 +1113,7 @@
         (2, WIDTH),
         (2, 768),
         (31, 768),
-        (1, 768),
+        (768,),
     ]
     scalars = pl.BlockSpec(memory_space=pltpu.SMEM)
     return call(
@@ -997,9 +1121,14 @@
         "finish",
         info,
         operands,
-        [whole(a.shape) for a in operands],
+        [whole(a.shape) for a in operands[:-1]] + [ANY],
         [struct(*s) for s in shapes] + [struct(4), struct(2)],
         [whole(s) for s in shapes] + [scalars, scalars],
+        [
+            scratch(*operands[-1].shape, dtype=BF16),
+            scratch(512, 128),
+            pltpu.SemaphoreType.DMA((CHUNKS,)),
+        ],
     )
 
 
@@ -1025,10 +1154,25 @@
     return lax.ppermute(value, axis, [(0, 1), (1, 0)])
 
 
-def along_x(block):
-    return [block] + [
-        lax.ppermute(block, "x", [(i, (i + s) % 4) for i in range(4)]) for s in SHIFTS[1:]
-    ]
+def move_x(block, distance):
+    return lax.ppermute(block, "x", [(i, (i + distance) % 4) for i in range(4)])
+
+
+def move_y(block, distance):
+    def joint(y):
+        return (y % 2) * 2 + y // 2
+
+    return lax.ppermute(
+        block, ("branch", "yh"), [(joint(y), joint((y + distance) % 4)) for y in range(4)]
+    )
+
+
+def move(block, axis, distance):
+    return lax.ppermute(block, axis, [(i, (i + distance) % 4) for i in range(4)])
+
+
+def along(block, axis):
+    return [block] + [move(block, axis, s) for s in SHIFTS[1:]]
 
 
 def with_partner(pieces):
@@ -1038,11 +1182,16 @@
     return both
 
 
+def exchange_x(pieces):
+    return [pieces[0]] + [move(p, "x", s) for p, s in zip(pieces[1:], SHIFTS[1:])]
+
+
 CHIPS = ("branch", "x", "z", "yh")
-
-
-def exchange(blocks):
-    return lax.all_to_all(blocks, CHIPS, 0, 0, tiled=True)
+PLANE = ("branch", "z", "yh")
+
+
+def exchange(blocks, axes):
+    return lax.all_to_all(blocks, axes, 0, 0, tiled=True)
 
 
 def shards(
@@ -1065,21 +1214,27 @@
     branch = lax.axis_index("branch")
     core = lax.axis_index("core")
     own_lengths = lax.dynamic_slice_in_dim(lengths, branch, 1, 1)[:, 0]
-    info = jnp.concatenate([jnp.stack([branch, core, lax.axis_index("x")]), own_lengths])
+    x, yh, z = (lax.axis_index(axis) for axis in ("x", "yh", "z"))
+    info = jnp.concatenate([jnp.stack([branch, core, x, 2 * yh + branch, z]), own_lengths])
     merge_logits = merge_logits[None]
-    local = run_pack(info, attend_in.transpose(1, 0, 2), attend_out, mixer_in, mixer_out)
-    own = jnp.concatenate(
-        [kernel_taps, kernel_bias[None], gating_norm, jnp.pad(position_slope, (0, 764))[None]]
+    local, own = run_pack(
+        info,
+        position_slope,
+        attend_in.transpose(1, 0, 2),
+        attend_out,
+        mixer_in,
+        mixer_out,
+        kernel_taps,
+        kernel_bias,
+        gating_norm,
     )
     other = swap(own, "branch")
-    block = run_spread(info, local, swap(local, "core"))
-    block, other = lax.optimization_barrier((block, other))
-    plane = lax.all_to_all(block, ("branch", "z", "yh"), 0, 0, tiled=True).reshape(2, 128, 1664)
-    attend_pieces = along_x(plane[:, :, 0:384])
-    *attend_pieces, mixer_block = lax.optimization_barrier(
-        (*attend_pieces, plane[:, :, 384:1664])
-    )
-    mixer_pieces = along_x(mixer_block)
+    block = run_pair(info, local, swap(local, "core"))
+    first, second = run_join_y(info, [block] + [move_y(block, s) for s in SHIFTS[1:]])
+    first, second, other = lax.optimization_barrier((first, second, other))
+    attend_block, mixer_block = run_join_planes(info, along(first, "z"), along(second, "x"))
+    attend_pieces = along(attend_block.reshape(2, 4, 32, 384), "x")
+    mixer_pieces = along(mixer_block.reshape(2, 4, 32, 1280), "z")
 
     triple, context, log_total, attend_w, slopes = run_attend_forward(
         info, frames, attend_norm, own, other, with_partner(attend_pieces)
@@ -1097,17 +1252,14 @@
         other,
         with_partner(mixer_pieces),
     )
+    small_other = swap(small, "core")
     mixer_other = swap(mixer_send, "core")
-    small_other = swap(small, "core")
     layer_other = swap(layer, "branch")
-    mixer_other, small_other, grad_context = lax.optimization_barrier(
-        (mixer_other, small_other, grad_context)
-    )
-    mixer_terms = run_sum_mixer(info, mixer_keep, mixer_other, small, small_other)
-    mixer_terms, grad_context, layer_other = lax.optimization_barrier(
-        (mixer_terms, grad_context, layer_other)
-    )
-    mixer_terms = exchange(mixer_terms.reshape(64, 16, 1408))
+    *mixer_sent, small_sent = run_sum_mixer(info, mixer_keep, mixer_other, small, small_other)
+    mixer_terms = exchange_x(mixer_sent)
+    small_sent, _, grad_context = lax.optimization_barrier(
+        (small_sent, mixer_sent[0], grad_context)
+    )
     grads, attend_keep, attend_send = run_attend_backward(
         info,
         frames,
@@ -1119,10 +1271,24 @@
         slopes,
         attend_w,
     )
+    small_sent, grads = lax.optimization_barrier((small_sent, grads))
+    small_terms = exchange(small_sent, PLANE)
+    grads, attend_keep, attend_send, layer_other, small_terms, *mixer_terms = (
+        lax.optimization_barrier(
+            (grads, attend_keep, attend_send, layer_other, small_terms, *mixer_terms)
+        )
+    )
     grads_other = swap(grads, "branch")
-    mixer_total = run_sum_chips(info, mixer_terms, False)[0]
-    attend_terms = run_sum_attend(info, attend_keep, swap(attend_send, "core"), mixer_total)
-    attend_total, small = run_sum_chips(info, exchange(attend_terms.reshape(64, 16, 640)), True)
+    attend_terms = exchange_x(
+        run_sum_attend(info, attend_keep, swap(attend_send, "core"), small_terms)
+    )
+    mixer_total = run_sum_four(info, mixer_terms)
+    layer_out = run_place_pair(info, layer, layer_other)
+    *attend_terms, mixer_total, grads_other, layer_out = lax.optimization_barrier(
+        (*attend_terms, mixer_total, grads_other, layer_out)
+    )
+    terms = exchange(run_join(info, mixer_total, attend_terms), PLANE)
+    frames_out = run_place_pair(info, grads, grads_other)
     (
         att_in,
         att_out,
@@ -1139,15 +1305,11 @@
     ) = run_finish(
         info,
         merge_logits,
-        mixer_total,
-        swap(mixer_total, "core"),
-        attend_total,
-        swap(attend_total, "core"),
-        small,
+        terms,
     )
     return (
-        run_place_pair(info, layer, layer_other),
-        run_place_pair(info, grads, grads_other),
+        layer_out,
+        frames_out,
         anorm,
         att_in.transpose(1, 0, 2),
         att_out,
@@ -1156,7 +1318,7 @@
         mix_in,
         gnorm,
         taps,
-        bias[0],
+        bias,
         mix_out,
         merge,
         fnorm,

time: 245 us -> 224 us (0.914)
  waiting for transfers between devices: 77.8 us -> 53.1 us
  starting transfers between devices: 30.3 us -> 52.3 us
  blocking collectives: 21.3 us -> 0 us
  Pallas kernels: 99.7 us -> 114 us
  local copies, waits for them, and re-layouts: 10.2 us -> 2.39 us
  other arithmetic: 2.83 us -> 0 us
    ppermute x6 -> x21, starting transfers between devices: 9.62 us -> 31.7 us  [the longest x18 29 us: move(): lax.ppermute(block, axis, [(i, (i + distance) % 4) for i in range(4)])]
    all_to_all x1 -> x0, blocking collectives: 21.3 us -> none  [shards(): lax.all_to_all(block, ('branch', 'z', 'yh'), 0, 0, tiled=True)]
    all_to_all x2, waiting for transfers between devices: 36.9 us -> 21.6 us  [exchange(): return lax.all_to_all(blocks, axes, 0, 0, tiled=True)]
    pallas_call x12 -> x14, Pallas kernels: 99.7 us -> 114 us  [call(): pl.pallas_call(kernel, grid_spec=pltpu.PrefetchScalarGridSpec(num_scalar_...]
    ppermute x17 -> x15, waiting for transfers between devices: 25 us -> 11.1 us  [swap(): return lax.ppermute(value, axis, [(0, 1), (1, 0)])]
    unnamed x58 -> x12, local copies, waits for them, and re-layouts: 8.82 us -> 1.09 us
    ppermute x6 -> x21, waiting for transfers between devices: 16 us -> 20.5 us  [the longest x18 16 us: move(): lax.ppermute(block, axis, [(i, (i + distance) % 4) for i in range(4)])]
    ppermute x17 -> x15, starting transfers between devices: 6.07 us -> 6.65 us  [swap(): return lax.ppermute(value, axis, [(0, 1), (1, 0)])]
  transfers between devices with their start and end apart: 25 -> 38, of which waited for: 17 -> 22; matrix products, arithmetic and copies ran while one was open for 0% -> 0% of each run, Pallas kernels for 22% -> 26%
where the time goes in v3:
time: 224 us; the launch traced here: 223 us
  Pallas kernels  114 us (51%)
  waiting for transfers between devices  53.1 us (24%)
  starting transfers between devices  52.3 us (23%)
  local copies, waits for them, and re-layouts  2.39 us (1%)
    pallas_call x14, Pallas kernels, call(): pl.pallas_call(kernel, grid_spec=pltpu.PrefetchScalarGridSpec(num_scalar_...  114 us
    ppermute x18, starting transfers between devices, move(): lax.ppermute(block, axis, [(i, (i + distance) % 4) for i in range(4)])  29 us
    all_to_all x2, waiting for transfers between devices, exchange(): return lax.all_to_all(blocks, axes, 0, 0, tiled=True)  21.6 us
    ppermute x18, waiting for transfers between devices, move(): lax.ppermute(block, axis, [(i, (i + distance) % 4) for i in range(4)])  16 us
    all_to_all x2, starting transfers between devices, exchange(): return lax.all_to_all(blocks, axes, 0, 0, tiled=True)  13.9 us
    ppermute x15, waiting for transfers between devices, swap(): return lax.ppermute(value, axis, [(0, 1), (1, 0)])  11.1 us
    ppermute x15, starting transfers between devices, swap(): return lax.ppermute(value, axis, [(0, 1), (1, 0)])  6.65 us
  transfers between devices with their start and end apart: 38, of which 22 were waited for; matrix products, arithmetic and copies ran while one was open for 0% of the time, Pallas kernels for 26%

profile of v3, /device:TPU:16, one launch (start us, length us, event | category | flops | bytes accessed | tf_op | source)
XLA Modules:
  0.0 223.2 jit_solution(16878417780380907234)
XLA Ops:
  0.7 0.7 dynamic-slice_bitcast_fusion
  1.3 0.6 concatenate.3.info
  2.0 2.4 %pack_local.1 = (bf16[8,3328]{1,0:T(8,128)(2,1)}, f32[35,768]{1,0:T(8,128)}) custom-call(s32[8]{0:T(128)} %concatenate.3.info, f32[4]{0:T(128)} %slopes.1, bf16[3,8,256]{2,1,0:T(8,128)(2,1)} %bitcast.25, bf16[8,256]{1,0:T(8,128)(2,1)} %att_out.1, bf16[8,2,768]{2,1,0:T(2,128)(2,1)} %mix_in.1, bf16[8,768]{1,0:T(8,128)(2,1)} %mix_out.1, f32[31,768]{1,0:T(8,128)} %taps.1, ...), custom_call_target="tpu_custom_call" | custom-call | flops 200000000 | bytes 65536 | tf_op jit(solution)/shard_map/pack_local/pallas_call | solution.py:844
  4.3 1.3 collective-permute-start.4
  5.6 0.3 collective-permute-done.other
  5.9 2.1 pair_rows.1.rest_0_
  8.0 0.3 collective-permute-start.3
  8.4 2.4 %collective-permute-start.2 = (bf16[16,1664]{1,0:T(8,128)(2,1)}, bf16[16,1664]{1,0:T(8,128)(2,1)}, u32[]{:S(2)}, u32[]{:S(2)}) collective-permute-start(bf16[16,1664]{1,0:T(8,128)(2,1)} %pair_rows.1.rest_0_), channel_id=1, source_target_pairs={{0,66},{64,0},{2,64},{66,2},{1,67},{65,1},{3,65},{67,3},{4,70},{68... | collective-permute-start | bytes 159752 | tf_op jit(solution)/shard_map/ppermute | solution.py:1165
  10.8 3.3 %collective-permute-done.3.rest_3_ = bf16[16,1664]{1,0:T(8,128)(2,1)} collective-permute-done((bf16[16,1664]{1,0:T(8,128)(2,1)}, bf16[16,1664]{1,0:T(8,128)(2,1)}, u32[]{:S(2)}, u32[]{:S(2)}) %collective-permute-start.3) | collective-permute-done | bytes 53280 | tf_op jit(solution)/shard_map/ppermute | solution.py:1165
  14.1 1.1 collective-permute-done.1.rest_1_
  15.2 2.3 %join_y.1 = (bf16[4,16,384]{2,1,0:T(8,128)(2,1)}, bf16[4,16,1280]{2,1,0:T(8,128)(2,1)}) custom-call(s32[8]{0:T(128)} %concatenate.3.info, bf16[16,1664]{1,0:T(8,128)(2,1)} %pair_rows.1.rest_0_, bf16[16,1664]{1,0:T(8,128)(2,1)} %collective-permute-done.1.rest_1_, bf16[16,1664]{1,0:T(8,128)(2,1)} %collective-permute-done.2.rest_2_, ...), custom_call_target="tpu_custom_call" | custom-call | flops 200000000 | bytes 65536 | tf_op jit(solution)/shard_map/join_y/pallas_call | solution.py:844
  17.5 3.0 %collective-permute-start.10 = (bf16[4,16,1280]{2,1,0:T(8,128)(2,1)}, bf16[4,16,1280]{2,1,0:T(8,128)(2,1)}, u32[]{:S(2)}, u32[]{:S(2)}) collective-permute-start(bf16[4,16,1280]{2,1,0:T(8,128)(2,1)} %get-tuple-element.88.rest_4_), channel_id=1, source_target_pairs={{0,32},{16,48},{32,0},{48,16},{1,33},{17,49},{33,1},{49,17},{2,34}... | collective-permute-start | bytes 491528 | tf_op jit(solution)/shard_map/ppermute | solution.py:1171
  20.5 1.1 collective-permute-start.9
  21.7 0.9 collective-permute-start.8
  22.6 3.9 %collective-permute-start.7 = (bf16[4,16,384]{2,1,0:T(8,128)(2,1)}, bf16[4,16,384]{2,1,0:T(8,128)(2,1)}, u32[]{:S(2)}, u32[]{:S(2)}) collective-permute-start(bf16[4,16,384]{2,1,0:T(8,128)(2,1)} %get-tuple-element.87.rest_0_), channel_id=1, source_target_pairs={{0,8},{4,12},{8,0},{12,4},{1,9},{5,13},{9,1},{13,5},{2,10},{6,14},... | collective-permute-start | bytes 147464 | tf_op jit(solution)/shard_map/ppermute | solution.py:1171
  26.4 0.7 collective-permute-start.6
  27.2 1.7 collective-permute-done.7.rest_3_
  28.8 1.6 collective-permute-start.5
  30.4 0.5 collective-permute-done.6.rest_2_
  30.8 4.1 %collective-permute-done.5.rest_1_ = bf16[4,16,384]{2,1,0:T(8,128)(2,1)} collective-permute-done((bf16[4,16,384]{2,1,0:T(8,128)(2,1)}, bf16[4,16,384]{2,1,0:T(8,128)(2,1)}, u32[]{:S(2)}, u32[]{:S(2)}) %collective-permute-start.5) | collective-permute-done | bytes 49184 | tf_op jit(solution)/shard_map/ppermute | solution.py:1171
  34.9 2.9 %join_planes.1 = (bf16[2,8,16,384]{3,2,1,0:T(8,128)(2,1)}, bf16[2,8,16,1280]{3,2,1,0:T(8,128)(2,1)}) custom-call(s32[8]{0:T(128)} %concatenate.3.info, bf16[4,16,384]{2,1,0:T(8,128)(2,1)} %get-tuple-element.87.rest_0_, bf16[4,16,384]{2,1,0:T(8,128)(2,1)} %collective-permute-done.5.rest_1_, bf16[4,16,384]{2,1,0:T(8,128)(2,1)} %collective-permute-done.6.rest_2_, ...), custom_call_target="tpu_custom_call" | custom-call | flops 200000000 | bytes 65536 | tf_op jit(solution)/shard_map/join_planes/pallas_call | solution.py:844
  37.8 0.6 collective-permute-start.19
  38.4 1.8 collective-permute-start.13
  40.3 0.7 collective-permute-start.12
  41.0 1.3 collective-permute-start.11
  42.3 2.8 %collective-permute-start.17 = (bf16[2,4,32,384]{3,2,1,0:T(8,128)(2,1)}, bf16[2,4,32,384]{3,2,1,0:T(8,128)(2,1)S(1)}, u32[]{:S(2)}, u32[]{:S(2)}) collective-permute-start(bf16[2,4,32,384]{3,2,1,0:T(8,128)(2,1)} %bitcast.18), channel_id=1, source_target_pairs={{0,48},{16,0},{32,16},{48,32},{1,49},{17,1},{33,17},{49,33},{2,50}... | collective-permute-start | bytes 589832 | tf_op jit(solution)/shard_map/ppermute | solution.py:1171
  45.3 1.5 collective-permute-start.15
  46.8 2.2 collective-permute-done.17.rest_4_
  49.0 3.4 %collective-permute-done.15.rest_2_ = bf16[2,4,32,384]{3,2,1,0:T(8,128)(2,1)S(1)} collective-permute-done((bf16[2,4,32,384]{3,2,1,0:T(8,128)(2,1)}, bf16[2,4,32,384]{3,2,1,0:T(8,128)(2,1)S(1)}, u32[]{:S(2)}, u32[]{:S(2)}) %collective-permute-start.15) | collective-permute-done | bytes 196640 | tf_op jit(solution)/shard_map/ppermute | solution.py:1171
  52.4 0.5 collective-permute-start.18
  52.9 0.9 collective-permute-done.20.rest_7_
  54.1 0.4 copy-done.4
  54.5 0.7 copy-done.5
  55.4 14.2 %attend_forward.1 = (bf16[3,1536,256]{2,1,0:T(8,128)(2,1)}, bf16[3,512,256]{2,1,0:T(8,128)(2,1)}, f32[3,8,256]{2,1,0:T(8,128)}, bf16[2,4,4,32,768]{4,3,2,1,0:T(8,128)(2,1)}, f32[8,128]{1,0:T(8,128)}) custom-call(s32[8]{0:T(128)} %concatenate.3.info, f32[3,2,256,512]{3,2,1,0:T(8,128)} %frames.5, f32[2,512]{1,0:T(2,128)} %norm.3, ...), custom_call_target="tpu_custom_call" | custom-call | flops 200000000 | bytes 65536 | tf_op jit(solution)/shard_map/attend_forward/pallas_call | solution.py:844
  69.9 0.4 collective-permute-start.22
  70.4 0.4 collective-permute-start.24
  70.8 1.4 collective-permute-done.21.rest_1_
  72.2 0.9 collective-permute-done.22.rest_3_
  73.1 0.9 collective-permute-done.23.rest_5_
  74.1 0.9 collective-permute-done.24.rest_7_
  75.0 44.8 %mixer_both.1 = (bf16[3,256,512]{2,1,0:T(8,128)(2,1)}, f32[3,256,512]{2,1,0:T(8,128)}, bf16[3,512,256]{2,1,0:T(8,128)(2,1)}, bf16[64,16,1280]{2,1,0:T(8,128)(2,1...) custom-call(s32[8]{0:T(128)} %concatenate.3.info, f32[3,2,256,512]{3,2,1,0:T(8,128)} %frames.5, ...), custom_call_target="tpu_custom_call" | custom-call | flops 200000000 | bytes 65536 | tf_op jit(solution)/shard_map/mixer_both/pallas_call | solution.py:844
  120.0 0.4 collective-permute-start.26
  120.4 1.3 collective-permute-start.27
  121.7 3.8 %collective-permute-done.26.small_other = f32[512,128]{1,0:T(8,128)} collective-permute-done((f32[512,128]{1,0:T(8,128)}, f32[512,128]{1,0:T(8,128)}, u32[]{:S(2)}, u32[]{:S(2)}) %collective-permute-start.26) | collective-permute-done | bytes 262176 | tf_op jit(solution)/shard_map/ppermute | solution.py:1154
  125.5 6.2 %sum_mixer.1 = (bf16[16,16,1280]{2,1,0:T(8,128)(2,1)}, bf16[16,16,1280]{2,1,0:T(8,128)(2,1)}, bf16[16,16,1280]{2,1,0:T(8,128)(2,1)}, bf16[16,16,1280]{2,1,0:T(8,128)(2,1)}, bf16[16,64,128]{2,1,0:T(8,128)(2,1)}) custom-call(s32[8]{0:T(128)} %concatenate.3.info, bf16[64,16,1280]{2,1,0:T(8,128)(2,1)} %get-tuple-element.98.keep, ...), custom_call_target="tpu_custom_call" | custom-call | flops 200000000 | bytes 65536 | tf_op jit(solution)/shard_map/sum_mixer/pallas_call | solution.py:844
  131.7 0.4 collective-permute-start.28
  132.1 2.9 %collective-permute-start.29 = (bf16[16,16,1280]{2,1,0:T(8,128)(2,1)}, bf16[16,16,1280]{2,1,0:T(8,128)(2,1)}, u32[]{:S(2)}, u32[]{:S(2)}) collective-permute-start(bf16[16,16,1280]{2,1,0:T(8,128)(2,1)} %get-tuple-element.118), channel_id=1, source_target_pairs={{0,48},{16,0},{32,16},{48,32},{1,49},{17,1},{33,17},{49,33},{2,50}... | collective-permute-start | bytes 1966088 | tf_op jit(solution)/shard_map/ppermute | solution.py:1171
  135.0 17.5 %attend_backward.1 = (bf16[3,256,512]{2,1,0:T(8,128)(2,1)}, bf16[64,16,512]{2,1,0:T(8,128)(2,1)}, bf16[64,16,512]{2,1,0:T(8,128)(2,1)}) custom-call(s32[8]{0:T(128)} %concatenate.3.info, f32[3,2,256,512]{3,2,1,0:T(8,128)} %frames.5, f32[3,256,512]{2,1,0:T(8,128)} %get-tuple-element.105.grad_mixed, bf16[3,1536,256]{2,1,0:T(8,128)(2,1)} %get-tuple-element.106.triple, ...), custom_call_target="tpu_custom_call" | custom-call | flops 200000000 | bytes 65536 | tf_op jit(solution)/shard_map/attend_backward/pallas_call | solution.py:844
  152.5 7.5 %all-to-all-start = ((bf16[16,64,128]{2,1,0:T(8,128)(2,1)}), bf16[16,64,128]{2,1,0:T(8,128)(2,1)}, u32[]{:S(2)}, u32[]{:S(2)}) async-start(bf16[16,64,128]{2,1,0:T(8,128)(2,1)} %get-tuple-element.116), calls=%async_computation | async-start | bytes 524288 | tf_op jit(solution)/shard_map/all_to_all | solution.py:1194
  160.1 6.6 %all-to-all-done.small_terms = bf16[16,64,128]{2,1,0:T(8,128)(2,1)} async-done(((bf16[16,64,128]{2,1,0:T(8,128)(2,1)}), bf16[16,64,128]{2,1,0:T(8,128)(2,1)}, u32[]{:S(2)}, u32[]{:S(2)}) %all-to-all-start) | async-done | bytes 262176 | tf_op jit(solution)/shard_map/all_to_all | solution.py:1194
  166.8 1.6 collective-permute-start.35
  168.5 1.3 collective-permute-done.31.other
  169.8 4.5 %sum_attend.1 = (bf16[17,16,512]{2,1,0:T(8,128)(2,1)}, bf16[17,16,512]{2,1,0:T(8,128)(2,1)}, bf16[17,16,512]{2,1,0:T(8,128)(2,1)}, bf16[17,16,512]{2,1,0:T(8,128)(2,1)}) custom-call(s32[8]{0:T(128)} %concatenate.3.info, bf16[64,16,512]{2,1,0:T(8,128)(2,1)} %get-tuple-element.120.keep, bf16[64,16,512]{2,1,0:T(8,128)(2,1)} %collective-permute-done.31.other, ...), custom_call_target="tpu_custom_call" | custom-call | flops 200000000 | bytes 65536 | tf_op jit(solution)/shard_map/sum_attend/pallas_call | solution.py:844
  174.4 0.9 collective-permute-start.32
  175.3 2.4 %collective-permute-start.33 = (bf16[17,16,512]{2,1,0:T(8,128)(2,1)}, bf16[17,16,512]{2,1,0:T(8,128)(2,1)}, u32[]{:S(2)}, u32[]{:S(2)}) collective-permute-start(bf16[17,16,512]{2,1,0:T(8,128)(2,1)} %get-tuple-element.125), channel_id=1, source_target_pairs={{0,48},{16,0},{32,16},{48,32},{1,49},{17,1},{33,17},{49,33},{2,50}... | collective-permute-start | bytes 835592 | tf_op jit(solution)/shard_map/ppermute | solution.py:1171
  177.7 2.3 %collective-permute-start.34 = (bf16[17,16,512]{2,1,0:T(8,128)(2,1)}, bf16[17,16,512]{2,1,0:T(8,128)(2,1)}, u32[]{:S(2)}, u32[]{:S(2)}) collective-permute-start(bf16[17,16,512]{2,1,0:T(8,128)(2,1)} %get-tuple-element.126), channel_id=1, source_target_pairs={{0,32},{16,48},{32,0},{48,16},{1,33},{17,49},{33,1},{49,17},{2,34}... | collective-permute-start | bytes 835592 | tf_op jit(solution)/shard_map/ppermute | solution.py:1171
  180.0 3.5 %place_pair.2 = f32[3,2,256,512]{3,2,1,0:T(8,128)} custom-call(s32[8]{0:T(128)} %concatenate.3.info, bf16[3,256,512]{2,1,0:T(8,128)(2,1)} %get-tuple-element.115.own, bf16[3,256,512]{2,1,0:T(8,128)(2,1)} %collective-permute-done.27.other), custom_call_target="tpu_custom_call" | custom-call | flops 200000000 | bytes 65536 | tf_op jit(solution)/shard_map/place_pair/pallas_call | solution.py:844
  183.4 3.5 %sum_four.1.mixer = bf16[16,16,1280]{2,1,0:T(8,128)(2,1)} custom-call(s32[8]{0:T(128)} %concatenate.3.info, bf16[16,16,1280]{2,1,0:T(8,128)(2,1)} %get-tuple-element.127.rest_0_, bf16[16,16,1280]{2,1,0:T(8,128)(2,1)} %collective-permute-done.28.rest_1_, bf16[16,16,1280]{2,1,0:T(8,128)(2,1)} %collective-permute-done.29.rest_2_, ...), custom_call_target="tpu_custom_call" | custom-call | flops 200000000 | bytes 65536 | tf_op jit(solution)/shard_map/sum_four/pallas_call | solution.py:844
  187.1 4.1 %collective-permute-done.34.rest_3_ = bf16[17,16,512]{2,1,0:T(8,128)(2,1)} collective-permute-done((bf16[17,16,512]{2,1,0:T(8,128)(2,1)}, bf16[17,16,512]{2,1,0:T(8,128)(2,1)}, u32[]{:S(2)}, u32[]{:S(2)}) %collective-permute-start.34) | collective-permute-done | bytes 278560 | tf_op jit(solution)/shard_map/ppermute | solution.py:1171
  191.2 3.3 %join_terms.1 = bf16[16,16,2304]{2,1,0:T(8,128)(2,1)} custom-call(s32[8]{0:T(128)} %concatenate.3.info, bf16[16,16,1280]{2,1,0:T(8,128)(2,1)} %sum_four.1.mixer, bf16[17,16,512]{2,1,0:T(8,128)(2,1)} %get-tuple-element.136.rest_0_, bf16[17,16,512]{2,1,0:T(8,128)(2,1)} %collective-permute-done.32.rest_1_, ...), custom_call_target="tpu_custom_call" | custom-call | flops 200000000 | bytes 65536 | tf_op jit(solution)/shard_map/join_terms/pallas_call | solution.py:844
  194.5 6.3 %all-to-all-start.1 = ((bf16[16,16,2304]{2,1,0:T(8,128)(2,1)}), bf16[16,16,2304]{2,1,0:T(8,128)(2,1)}, u32[]{:S(2)}, u32[]{:S(2)}) async-start(bf16[16,16,2304]{2,1,0:T(8,128)(2,1)} %join_terms.1), calls=%async_computation.1 | async-start | bytes 2359296 | tf_op jit(solution)/shard_map/all_to_all | solution.py:1194
  200.9 3.5 %place_pair.3 = f32[3,2,256,512]{3,2,1,0:T(8,128)} custom-call(s32[8]{0:T(128)} %concatenate.3.info, bf16[3,256,512]{2,1,0:T(8,128)(2,1)} %get-tuple-element.131.own, bf16[3,256,512]{2,1,0:T(8,128)(2,1)} %collective-permute-done.35.other), custom_call_target="tpu_custom_call" | custom-call | flops 200000000 | bytes 65536 | tf_op jit(solution)/shard_map/place_pair/pallas_call | solution.py:844
  204.4 14.9 %all-to-all-done.1.terms = bf16[16,16,2304]{2,1,0:T(8,128)(2,1)} async-done(((bf16[16,16,2304]{2,1,0:T(8,128)(2,1)}), bf16[16,16,2304]{2,1,0:T(8,128)(2,1)}, u32[]{:S(2)}, u32[]{:S(2)}) %all-to-all-start.1) | async-done | bytes 1179680 | tf_op jit(solution)/shard_map/all_to_all | solution.py:1194
  219.3 3.7 %finish.1 = (f32[3,8,256]{2,1,0:T(8,128)}, f32[8,256]{1,0:T(8,128)}, f32[8,2,768]{2,1,0:T(2,128)}, f32[8,768]{1,0:T(8,128)}, f32[2,512]{1,0:T(2,128)}, /*index=5...) custom-call(s32[8]{0:T(128)} %concatenate.3.info, ...), custom_call_target="tpu_custom_call" | custom-call | flops 200000000 | bytes 65536 | tf_op jit(solution)/shard_map/finish/pallas_call | solution.py:844
  (40 shorter events, 1.5 us)
Async XLA Ops:
  4.3 1.6 collective-permute-start
  4.3 13.2 %collective-permute-start.4 = (f32[35,768]{1,0:T(8,128)}, f32[35,768]{1,0:T(8,128)}, u32[]{:S(2)}, u32[]{:S(2)}) collective-permute-start(f32[35,768]{1,0:T(8,128)} %get-tuple-element.86.own), channel_id=1, source_target_pairs={{0,64},{64,0},{1,65},{65,1},{2,66},{66,2},{3,67},{67,3},{4,68},{68... | collective-permute-start | bytes 322568 | tf_op jit(solution)/shard_map/ppermute | solution.py:1154
  8.0 6.1 %collective-permute-start.3 = (bf16[16,1664]{1,0:T(8,128)(2,1)}, bf16[16,1664]{1,0:T(8,128)(2,1)}, u32[]{:S(2)}, u32[]{:S(2)}) collective-permute-start(bf16[16,1664]{1,0:T(8,128)(2,1)} %pair_rows.1.rest_0_), channel_id=1, source_target_pairs={{0,2},{64,66},{2,0},{66,64},{1,3},{65,67},{3,1},{67,65},{4,6},{68,... | collective-permute-start | bytes 159752 | tf_op jit(solution)/shard_map/ppermute | solution.py:1165
  8.4 5.7 %collective-permute-start.2 = (bf16[16,1664]{1,0:T(8,128)(2,1)}, bf16[16,1664]{1,0:T(8,128)(2,1)}, u32[]{:S(2)}, u32[]{:S(2)}) collective-permute-start(bf16[16,1664]{1,0:T(8,128)(2,1)} %pair_rows.1.rest_0_), channel_id=1, source_target_pairs={{0,66},{64,0},{2,64},{66,2},{1,67},{65,1},{3,65},{67,3},{4,70},{68... | collective-permute-start | bytes 159752 | tf_op jit(solution)/shard_map/ppermute | solution.py:1165
  10.8 4.5 %collective-permute-start.1 = (bf16[16,1664]{1,0:T(8,128)(2,1)}, bf16[16,1664]{1,0:T(8,128)(2,1)}, u32[]{:S(2)}, u32[]{:S(2)}) collective-permute-start(bf16[16,1664]{1,0:T(8,128)(2,1)} %pair_rows.1.rest_0_), channel_id=1, source_target_pairs={{0,64},{64,2},{2,66},{66,0},{1,65},{65,3},{3,67},{67,1},{4,68},{68... | collective-permute-start | bytes 159752 | tf_op jit(solution)/shard_map/ppermute | solution.py:1165
  17.5 17.4 %collective-permute-start.10 = (bf16[4,16,1280]{2,1,0:T(8,128)(2,1)}, bf16[4,16,1280]{2,1,0:T(8,128)(2,1)}, u32[]{:S(2)}, u32[]{:S(2)}) collective-permute-start(bf16[4,16,1280]{2,1,0:T(8,128)(2,1)} %get-tuple-element.88.rest_4_), channel_id=1, source_target_pairs={{0,32},{16,48},{32,0},{48,16},{1,33},{17,49},{33,1},{49,17},{2,34}... | collective-permute-start | bytes 491528 | tf_op jit(solution)/shard_map/ppermute | solution.py:1171
  20.5 14.4 %collective-permute-start.9 = (bf16[4,16,1280]{2,1,0:T(8,128)(2,1)}, bf16[4,16,1280]{2,1,0:T(8,128)(2,1)}, u32[]{:S(2)}, u32[]{:S(2)}) collective-permute-start(bf16[4,16,1280]{2,1,0:T(8,128)(2,1)} %get-tuple-element.88.rest_4_), channel_id=1, source_target_pairs={{0,48},{16,0},{32,16},{48,32},{1,49},{17,1},{33,17},{49,33},{2,50}... | collective-permute-start | bytes 491528 | tf_op jit(solution)/shard_map/ppermute | solution.py:1171
  21.7 13.3 %collective-permute-start.8 = (bf16[4,16,1280]{2,1,0:T(8,128)(2,1)}, bf16[4,16,1280]{2,1,0:T(8,128)(2,1)}, u32[]{:S(2)}, u32[]{:S(2)}) collective-permute-start(bf16[4,16,1280]{2,1,0:T(8,128)(2,1)} %get-tuple-element.88.rest_4_), channel_id=1, source_target_pairs={{0,16},{16,32},{32,48},{48,0},{1,17},{17,33},{33,49},{49,1},{2,18}... | collective-permute-start | bytes 491528 | tf_op jit(solution)/shard_map/ppermute | solution.py:1171
  22.6 6.3 %collective-permute-start.7 = (bf16[4,16,384]{2,1,0:T(8,128)(2,1)}, bf16[4,16,384]{2,1,0:T(8,128)(2,1)}, u32[]{:S(2)}, u32[]{:S(2)}) collective-permute-start(bf16[4,16,384]{2,1,0:T(8,128)(2,1)} %get-tuple-element.87.rest_0_), channel_id=1, source_target_pairs={{0,8},{4,12},{8,0},{12,4},{1,9},{5,13},{9,1},{13,5},{2,10},{6,14},... | collective-permute-start | bytes 147464 | tf_op jit(solution)/shard_map/ppermute | solution.py:1171
  26.4 4.4 %collective-permute-start.6 = (bf16[4,16,384]{2,1,0:T(8,128)(2,1)}, bf16[4,16,384]{2,1,0:T(8,128)(2,1)}, u32[]{:S(2)}, u32[]{:S(2)}) collective-permute-start(bf16[4,16,384]{2,1,0:T(8,128)(2,1)} %get-tuple-element.87.rest_0_), channel_id=1, source_target_pairs={{0,12},{4,0},{8,4},{12,8},{1,13},{5,1},{9,5},{13,9},{2,14},{6,2},{... | collective-permute-start | bytes 147464 | tf_op jit(solution)/shard_map/ppermute | solution.py:1171
  28.8 6.1 %collective-permute-start.5 = (bf16[4,16,384]{2,1,0:T(8,128)(2,1)}, bf16[4,16,384]{2,1,0:T(8,128)(2,1)}, u32[]{:S(2)}, u32[]{:S(2)}) collective-permute-start(bf16[4,16,384]{2,1,0:T(8,128)(2,1)} %get-tuple-element.87.rest_0_), channel_id=1, source_target_pairs={{0,4},{4,8},{8,12},{12,0},{1,5},{5,9},{9,13},{13,1},{2,6},{6,10},{... | collective-permute-start | bytes 147464 | tf_op jit(solution)/shard_map/ppermute | solution.py:1171
  37.8 7.5 %collective-permute-start.19 = (bf16[2,4,32,384]{3,2,1,0:T(8,128)(2,1)}, bf16[2,4,32,384]{3,2,1,0:T(8,128)(2,1)S(1)}, u32[]{:S(2)}, u32[]{:S(2)}) collective-permute-start(bf16[2,4,32,384]{3,2,1,0:T(8,128)(2,1)} %bitcast.17), channel_id=1, source_target_pairs={{0,32},{16,48},{32,0},{48,16},{1,33},{17,49},{33,1},{49,17},{2,34}... | collective-permute-start | bytes 589832 | tf_op jit(solution)/shard_map/ppermute | solution.py:1171
  38.4 31.2 %collective-permute-start.13 = (bf16[2,4,32,1280]{3,2,1,0:T(8,128)(2,1)}, bf16[2,4,32,1280]{3,2,1,0:T(8,128)(2,1)}, u32[]{:S(2)}, u32[]{:S(2)}) collective-permute-start(bf16[2,4,32,1280]{3,2,1,0:T(8,128)(2,1)} %bitcast.12), channel_id=1, source_target_pairs={{0,8},{4,12},{8,0},{12,4},{1,9},{5,13},{9,1},{13,5},{2,10},{6,14},... | collective-permute-start | bytes 1966088 | tf_op jit(solution)/shard_map/ppermute | solution.py:1171
  40.3 29.4 %collective-permute-start.12 = (bf16[2,4,32,1280]{3,2,1,0:T(8,128)(2,1)}, bf16[2,4,32,1280]{3,2,1,0:T(8,128)(2,1)}, u32[]{:S(2)}, u32[]{:S(2)}) collective-permute-start(bf16[2,4,32,1280]{3,2,1,0:T(8,128)(2,1)} %bitcast.13), channel_id=1, source_target_pairs={{0,12},{4,0},{8,4},{12,8},{1,13},{5,1},{9,5},{13,9},{2,14},{6,2},{... | collective-permute-start | bytes 1966088 | tf_op jit(solution)/shard_map/ppermute | solution.py:1171
  41.0 28.7 %collective-permute-start.11 = (bf16[2,4,32,1280]{3,2,1,0:T(8,128)(2,1)}, bf16[2,4,32,1280]{3,2,1,0:T(8,128)(2,1)}, u32[]{:S(2)}, u32[]{:S(2)}) collective-permute-start(bf16[2,4,32,1280]{3,2,1,0:T(8,128)(2,1)} %bitcast.14), channel_id=1, source_target_pairs={{0,4},{4,8},{8,12},{12,0},{1,5},{5,9},{9,13},{13,1},{2,6},{6,10},{... | collective-permute-start | bytes 1966088 | tf_op jit(solution)/shard_map/ppermute | solution.py:1171
  42.3 6.6 %collective-permute-start.17 = (bf16[2,4,32,384]{3,2,1,0:T(8,128)(2,1)}, bf16[2,4,32,384]{3,2,1,0:T(8,128)(2,1)S(1)}, u32[]{:S(2)}, u32[]{:S(2)}) collective-permute-start(bf16[2,4,32,384]{3,2,1,0:T(8,128)(2,1)} %bitcast.18), channel_id=1, source_target_pairs={{0,48},{16,0},{32,16},{48,32},{1,49},{17,1},{33,17},{49,33},{2,50}... | collective-permute-start | bytes 589832 | tf_op jit(solution)/shard_map/ppermute | solution.py:1171
  45.3 7.1 %copy-start = (bf16[2,4,32,384]{3,2,1,0:T(8,128)(2,1)}, bf16[2,4,32,384]{3,2,1,0:T(8,128)(2,1)S(1)}, u32[]{:S(2)}) copy-start(bf16[2,4,32,384]{3,2,1,0:T(8,128)(2,1)S(1)} %collective-permute-done.19.rest_6_) | copy-start | bytes 589828
  45.3 7.1 %collective-permute-start.15 = (bf16[2,4,32,384]{3,2,1,0:T(8,128)(2,1)}, bf16[2,4,32,384]{3,2,1,0:T(8,128)(2,1)S(1)}, u32[]{:S(2)}, u32[]{:S(2)}) collective-permute-start(bf16[2,4,32,384]{3,2,1,0:T(8,128)(2,1)} %bitcast.19), channel_id=1, source_target_pairs={{0,16},{16,32},{32,48},{48,0},{1,17},{17,33},{33,49},{49,1},{2,18}... | collective-permute-start | bytes 589832 | tf_op jit(solution)/shard_map/ppermute | solution.py:1171
  48.9 4.9 %copy-start.1 = (bf16[2,4,32,384]{3,2,1,0:T(8,128)(2,1)}, bf16[2,4,32,384]{3,2,1,0:T(8,128)(2,1)S(1)}, u32[]{:S(2)}) copy-start(bf16[2,4,32,384]{3,2,1,0:T(8,128)(2,1)S(1)} %collective-permute-done.17.rest_4_) | copy-start | bytes 589828
  48.9 3.4 %collective-permute-start.14 = (bf16[2,4,32,384]{3,2,1,0:T(8,128)(2,1)}, bf16[2,4,32,384]{3,2,1,0:T(8,128)(2,1)S(1)}, u32[]{:S(2)}, u32[]{:S(2)}) collective-permute-start(bf16[2,4,32,384]{3,2,1,0:T(8,128)(2,1)} %bitcast.20), channel_id=1, source_target_pairs={{0,1},{1,0},{2,3},{3,2},{4,5},{5,4},{6,7},{7,6},{8,9},{9,8},{10,11... | collective-permute-start | bytes 589832 | tf_op jit(solution)/shard_map/ppermute | solution.py:1154
  52.4 1.7 copy-start.2
  52.4 1.4 collective-permute-start.20
  52.4 1.7 copy-start.3
  52.4 1.7 collective-permute-start.18
  53.8 0.7 copy-start.4
  53.8 1.6 collective-permute-start.16
  54.5 0.7 copy-start.5
  69.7 2.5 %collective-permute-start.21 = (bf16[2,4,32,1280]{3,2,1,0:T(8,128)(2,1)}, bf16[2,4,32,1280]{3,2,1,0:T(8,128)(2,1)}, u32[]{:S(2)}, u32[]{:S(2)}) collective-permute-start(bf16[2,4,32,1280]{3,2,1,0:T(8,128)(2,1)} %bitcast.15), channel_id=1, source_target_pairs={{0,1},{1,0},{2,3},{3,2},{4,5},{5,4},{6,7},{7,6},{8,9},{9,8},{10,11... | collective-permute-start | bytes 1966088 | tf_op jit(solution)/shard_map/ppermute | solution.py:1154
  69.9 3.2 %collective-permute-start.22 = (bf16[2,4,32,1280]{3,2,1,0:T(8,128)(2,1)}, bf16[2,4,32,1280]{3,2,1,0:T(8,128)(2,1)}, u32[]{:S(2)}, u32[]{:S(2)}) collective-permute-start(bf16[2,4,32,1280]{3,2,1,0:T(8,128)(2,1)} %collective-permute-done.11.rest_2_), channel_id=1, source_target_pairs={{0,1},{1,0},{2,3},{3,2},{4,5},{5,4},{6,7},{7,6},{8,9},{9,8},{10,11... | collective-permute-start | bytes 1966088 | tf_op jit(solution)/shard_map/ppermute | solution.py:1154
  70.3 3.8 %collective-permute-start.23 = (bf16[2,4,32,1280]{3,2,1,0:T(8,128)(2,1)}, bf16[2,4,32,1280]{3,2,1,0:T(8,128)(2,1)}, u32[]{:S(2)}, u32[]{:S(2)}) collective-permute-start(bf16[2,4,32,1280]{3,2,1,0:T(8,128)(2,1)} %collective-permute-done.12.rest_4_), channel_id=1, source_target_pairs={{0,1},{1,0},{2,3},{3,2},{4,5},{5,4},{6,7},{7,6},{8,9},{9,8},{10,11... | collective-permute-start | bytes 1966088 | tf_op jit(solution)/shard_map/ppermute | solution.py:1154
  70.4 4.6 %collective-permute-start.24 = (bf16[2,4,32,1280]{3,2,1,0:T(8,128)(2,1)}, bf16[2,4,32,1280]{3,2,1,0:T(8,128)(2,1)}, u32[]{:S(2)}, u32[]{:S(2)}) collective-permute-start(bf16[2,4,32,1280]{3,2,1,0:T(8,128)(2,1)} %collective-permute-done.13.rest_6_), channel_id=1, source_target_pairs={{0,1},{1,0},{2,3},{3,2},{4,5},{5,4},{6,7},{7,6},{8,9},{9,8},{10,11... | collective-permute-start | bytes 1966088 | tf_op jit(solution)/shard_map/ppermute | solution.py:1154
  119.8 5.7 %collective-permute-start.25 = (bf16[64,16,1280]{2,1,0:T(8,128)(2,1)}, bf16[64,16,1280]{2,1,0:T(8,128)(2,1)}, u32[]{:S(2)}, u32[]{:S(2)}) collective-permute-start(bf16[64,16,1280]{2,1,0:T(8,128)(2,1)} %get-tuple-element.99), channel_id=1, source_target_pairs={{0,1},{1,0},{2,3},{3,2},{4,5},{5,4},{6,7},{7,6},{8,9},{9,8},{10,11... | collective-permute-start | bytes 7864328 | tf_op jit(solution)/shard_map/ppermute | solution.py:1154
  120.0 5.5 %collective-permute-start.26 = (f32[512,128]{1,0:T(8,128)}, f32[512,128]{1,0:T(8,128)}, u32[]{:S(2)}, u32[]{:S(2)}) collective-permute-start(f32[512,128]{1,0:T(8,128)} %get-tuple-element.100.small), channel_id=1, source_target_pairs={{0,1},{1,0},{2,3},{3,2},{4,5},{5,4},{6,7},{7,6},{8,9},{9,8},{10,11... | collective-permute-start | bytes 786440 | tf_op jit(solution)/shard_map/ppermute | solution.py:1154
  120.4 39.7 %collective-permute-start.27 = (bf16[3,256,512]{2,1,0:T(8,128)(2,1)}, bf16[3,256,512]{2,1,0:T(8,128)(2,1)}, u32[]{:S(2)}, u32[]{:S(2)}) collective-permute-start(bf16[3,256,512]{2,1,0:T(8,128)(2,1)} %get-tuple-element.115.own), channel_id=1, source_target_pairs={{0,64},{64,0},{1,65},{65,1},{2,66},{66,2},{3,67},{67,3},{4,68},{68... | collective-permute-start | bytes 2359304 | tf_op jit(solution)/shard_map/ppermute | solution.py:1154
  131.7 35.0 %collective-permute-start.28 = (bf16[16,16,1280]{2,1,0:T(8,128)(2,1)}, bf16[16,16,1280]{2,1,0:T(8,128)(2,1)}, u32[]{:S(2)}, u32[]{:S(2)}) collective-permute-start(bf16[16,16,1280]{2,1,0:T(8,128)(2,1)} %get-tuple-element.117), channel_id=1, source_target_pairs={{0,16},{16,32},{32,48},{48,0},{1,17},{17,33},{33,49},{49,1},{2,18}... | collective-permute-start | bytes 1966088 | tf_op jit(solution)/shard_map/ppermute | solution.py:1171
  132.1 34.6 %collective-permute-start.29 = (bf16[16,16,1280]{2,1,0:T(8,128)(2,1)}, bf16[16,16,1280]{2,1,0:T(8,128)(2,1)}, u32[]{:S(2)}, u32[]{:S(2)}) collective-permute-start(bf16[16,16,1280]{2,1,0:T(8,128)(2,1)} %get-tuple-element.118), channel_id=1, source_target_pairs={{0,48},{16,0},{32,16},{48,32},{1,49},{17,1},{33,17},{49,33},{2,50}... | collective-permute-start | bytes 1966088 | tf_op jit(solution)/shard_map/ppermute | solution.py:1171
  135.0 31.7 %collective-permute-start.30 = (bf16[16,16,1280]{2,1,0:T(8,128)(2,1)}, bf16[16,16,1280]{2,1,0:T(8,128)(2,1)}, u32[]{:S(2)}, u32[]{:S(2)}) collective-permute-start(bf16[16,16,1280]{2,1,0:T(8,128)(2,1)} %get-tuple-element.119), channel_id=1, source_target_pairs={{0,32},{16,48},{32,0},{48,16},{1,33},{17,49},{33,1},{49,17},{2,34}... | collective-permute-start | bytes 1966088 | tf_op jit(solution)/shard_map/ppermute | solution.py:1171
  152.5 14.2 %all-to-all-start = ((bf16[16,64,128]{2,1,0:T(8,128)(2,1)}), bf16[16,64,128]{2,1,0:T(8,128)(2,1)}, u32[]{:S(2)}, u32[]{:S(2)}) async-start(bf16[16,64,128]{2,1,0:T(8,128)(2,1)} %get-tuple-element.116), calls=%async_computation | async-start | bytes 524288 | tf_op jit(solution)/shard_map/all_to_all | solution.py:1194
  166.7 3.1 %collective-permute-start.31 = (bf16[64,16,512]{2,1,0:T(8,128)(2,1)}, bf16[64,16,512]{2,1,0:T(8,128)(2,1)}, u32[]{:S(2)}, u32[]{:S(2)}) collective-permute-start(bf16[64,16,512]{2,1,0:T(8,128)(2,1)} %get-tuple-element.121), channel_id=1, source_target_pairs={{0,1},{1,0},{2,3},{3,2},{4,5},{5,4},{6,7},{7,6},{8,9},{9,8},{10,11... | collective-permute-start | bytes 3145736 | tf_op jit(solution)/shard_map/ppermute | solution.py:1154
  166.8 20.3 %collective-permute-start.35 = (bf16[3,256,512]{2,1,0:T(8,128)(2,1)}, bf16[3,256,512]{2,1,0:T(8,128)(2,1)}, u32[]{:S(2)}, u32[]{:S(2)}) collective-permute-start(bf16[3,256,512]{2,1,0:T(8,128)(2,1)} %get-tuple-element.131.own), channel_id=1, source_target_pairs={{0,64},{64,0},{1,65},{65,1},{2,66},{66,2},{3,67},{67,3},{4,68},{68... | collective-permute-start | bytes 2359304 | tf_op jit(solution)/shard_map/ppermute | solution.py:1154
  174.4 12.7 %collective-permute-start.32 = (bf16[17,16,512]{2,1,0:T(8,128)(2,1)}, bf16[17,16,512]{2,1,0:T(8,128)(2,1)}, u32[]{:S(2)}, u32[]{:S(2)}) collective-permute-start(bf16[17,16,512]{2,1,0:T(8,128)(2,1)} %get-tuple-element.124), channel_id=1, source_target_pairs={{0,16},{16,32},{32,48},{48,0},{1,17},{17,33},{33,49},{49,1},{2,18}... | collective-permute-start | bytes 835592 | tf_op jit(solution)/shard_map/ppermute | solution.py:1171
  175.3 11.8 %collective-permute-start.33 = (bf16[17,16,512]{2,1,0:T(8,128)(2,1)}, bf16[17,16,512]{2,1,0:T(8,128)(2,1)}, u32[]{:S(2)}, u32[]{:S(2)}) collective-permute-start(bf16[17,16,512]{2,1,0:T(8,128)(2,1)} %get-tuple-element.125), channel_id=1, source_target_pairs={{0,48},{16,0},{32,16},{48,32},{1,49},{17,1},{33,17},{49,33},{2,50}... | collective-permute-start | bytes 835592 | tf_op jit(solution)/shard_map/ppermute | solution.py:1171
  177.7 13.5 %collective-permute-start.34 = (bf16[17,16,512]{2,1,0:T(8,128)(2,1)}, bf16[17,16,512]{2,1,0:T(8,128)(2,1)}, u32[]{:S(2)}, u32[]{:S(2)}) collective-permute-start(bf16[17,16,512]{2,1,0:T(8,128)(2,1)} %get-tuple-element.126), channel_id=1, source_target_pairs={{0,32},{16,48},{32,0},{48,16},{1,33},{17,49},{33,1},{49,17},{2,34}... | collective-permute-start | bytes 835592 | tf_op jit(solution)/shard_map/ppermute | solution.py:1171
  194.5 24.8 %all-to-all-start.1 = ((bf16[16,16,2304]{2,1,0:T(8,128)(2,1)}), bf16[16,16,2304]{2,1,0:T(8,128)(2,1)}, u32[]{:S(2)}, u32[]{:S(2)}) async-start(bf16[16,16,2304]{2,1,0:T(8,128)(2,1)} %join_terms.1), calls=%async_computation.1 | async-start | bytes 2359296 | tf_op jit(solution)/shard_map/all_to_all | solution.py:1194

commit v4 on v3

--- a/solution.py
+++ b/solution.py
@@ -25,7 +25,7 @@
 PERIOD = SLOT + REACH
 BINS = (PERIOD + 1) // 2
 SPEC = 2 * BINS
-BLOCK = 256
+BLOCK = 768
 BLOCKS = HALF // BLOCK
 PER_BRANCH = 768 // BLOCK
 GELU_A = 0.7978845608028654
@@ -290,14 +290,18 @@
         cross_s[...] = jnp.zeros_like(cross_s)
         small_wide[...] = jnp.zeros_like(small_wide)
         small_narrow[...] = jnp.zeros_like(small_narrow)
-        for copy in copies:
-            copy.wait()
 
     mix_attend, mix_mixer = merge_mix(merge_logits)
     rows_in = frames[0, 0]
     normed, rstd = standardize(rows_in)
     low = (normed * mixer_norm[0:1] + mixer_norm[1:2]).astype(BF16)
     low_s[here, :] = low
+
+    @pl.when(step == 0)
+    def _():
+        for copy in copies:
+            copy.wait()
+
     length = info[INFO_LENGTH + step]
     valid = (lax.broadcasted_iota(jnp.int32, (SLOT, 1), 0) < length).astype(F32)
 
@@ -311,7 +315,10 @@
         return weight(weights, b, kind * 768 + off.start, kind * 768 + off.stop)
 
     def fold(v):
-        return v[:, 0:128] + v[:, 128:256]
+        total = v[:, 0:128]
+        for at in range(128, BLOCK, 128):
+            total = total + v[:, at : at + 128]
+        return total
 
     def lane_sum(v):
         return jnp.sum(v, axis=-1, keepdims=True)
@@ -862,11 +869,11 @@
     )(info, *operands)
 
 
-def run_pack(info, slopes, *operands):
+def run_pack(slopes, *operands):
     return call(
         pack_local,
         "pack_local",
-        info,
+        np.zeros((8,), np.int32),
         (slopes, *operands),
         [pl.BlockSpec(memory_space=pltpu.SMEM)] + [whole(a.shape) for a in operands],
         [struct(8, 3328, dtype=BF16), struct(35, 768)],
@@ -1218,7 +1225,6 @@
     info = jnp.concatenate([jnp.stack([branch, core, x, 2 * yh + branch, z]), own_lengths])
     merge_logits = merge_logits[None]
     local, own = run_pack(
-        info,
         position_slope,
         attend_in.transpose(1, 0, 2),
         attend_out,

time: 224 us -> 217 us (0.969)
  Pallas kernels: 114 us -> 108 us
    pallas_call x14, Pallas kernels: 114 us -> 108 us  [call(): pl.pallas_call(kernel, grid_spec=pltpu.PrefetchScalarGridSpec(num_scalar_...]
  transfers between devices with their start and end apart: 38 -> 38, of which waited for: 22 -> 21; matrix products, arithmetic and copies ran while one was open for 0% -> 1% of each run, Pallas kernels for 26% -> 27%
where the time goes in v4:
time: 217 us; the launch traced here: 216 us
  Pallas kernels  108 us (50%)
  waiting for transfers between devices  53.1 us (24%)
  starting transfers between devices  51.1 us (24%)
  local copies, waits for them, and re-layouts  2.9 us (1%)
    pallas_call x14, Pallas kernels, call(): pl.pallas_call(kernel, grid_spec=pltpu.PrefetchScalarGridSpec(num_scalar_...  108 us
    ppermute x18, starting transfers between devices, move(): lax.ppermute(block, axis, [(i, (i + distance) % 4) for i in range(4)])  29.6 us
    all_to_all x2, waiting for transfers between devices, exchange(): return lax.all_to_all(blocks, axes, 0, 0, tiled=True)  21.5 us
    ppermute x18, waiting for transfers between devices, move(): lax.ppermute(block, axis, [(i, (i + distance) % 4) for i in range(4)])  16 us
    all_to_all x2, starting transfers between devices, exchange(): return lax.all_to_all(blocks, axes, 0, 0, tiled=True)  12.7 us
    ppermute x15, waiting for transfers between devices, swap(): return lax.ppermute(value, axis, [(0, 1), (1, 0)])  11.4 us
    ppermute x15, starting transfers between devices, swap(): return lax.ppermute(value, axis, [(0, 1), (1, 0)])  6.15 us
  transfers between devices with their start and end apart: 38, of which 21 were waited for; matrix products, arithmetic and copies ran while one was open for 1% of the time, Pallas kernels for 27%

profile of v4, /device:TPU:16, one launch (start us, length us, event | category | flops | bytes accessed | tf_op | source)
XLA Modules:
  0.0 215.8 jit_solution(421435519922424629)
XLA Ops:
  0.6 0.5 call_exported.0.info
  1.2 2.4 %pack_local.1 = (bf16[8,3328]{1,0:T(8,128)(2,1)}, f32[35,768]{1,0:T(8,128)}) custom-call(s32[8]{0:T(128)} %call_exported.0.info, f32[4]{0:T(128)} %slopes.1, bf16[3,8,256]{2,1,0:T(8,128)(2,1)} %bitcast.25, bf16[8,256]{1,0:T(8,128)(2,1)} %att_out.1, bf16[8,2,768]{2,1,0:T(2,128)(2,1)} %mix_in.1, bf16[8,768]{1,0:T(8,128)(2,1)} %mix_out.1, f32[31,768]{1,0:T(8,128)} %taps.1, ...), custom_call_target="tpu_custom_call" | custom-call | flops 200000000 | bytes 65536 | tf_op jit(solution)/shard_map/pack_local/pallas_call | solution.py:851
  3.5 1.3 collective-permute-start.4
  4.8 0.7 dynamic-slice_bitcast_fusion
  5.5 0.6 concatenate.3.info
  6.1 2.1 pair_rows.1.rest_0_
  8.3 0.6 collective-permute-start.3
  8.9 1.6 collective-permute-start.2
  10.5 0.5 collective-permute-start.1
  10.9 3.4 %collective-permute-done.3.rest_3_ = bf16[16,1664]{1,0:T(8,128)(2,1)} collective-permute-done((bf16[16,1664]{1,0:T(8,128)(2,1)}, bf16[16,1664]{1,0:T(8,128)(2,1)}, u32[]{:S(2)}, u32[]{:S(2)}) %collective-permute-start.3) | collective-permute-done | bytes 53280 | tf_op jit(solution)/shard_map/ppermute | solution.py:1172
  14.3 0.9 collective-permute-done.1.rest_1_
  15.2 2.3 %join_y.1 = (bf16[4,16,384]{2,1,0:T(8,128)(2,1)}, bf16[4,16,1280]{2,1,0:T(8,128)(2,1)}) custom-call(s32[8]{0:T(128)} %concatenate.3.info, bf16[16,1664]{1,0:T(8,128)(2,1)} %pair_rows.1.rest_0_, bf16[16,1664]{1,0:T(8,128)(2,1)} %collective-permute-done.1.rest_1_, bf16[16,1664]{1,0:T(8,128)(2,1)} %collective-permute-done.2.rest_2_, ...), custom_call_target="tpu_custom_call" | custom-call | flops 200000000 | bytes 65536 | tf_op jit(solution)/shard_map/join_y/pallas_call | solution.py:851
  17.4 3.0 %collective-permute-start.10 = (bf16[4,16,1280]{2,1,0:T(8,128)(2,1)}, bf16[4,16,1280]{2,1,0:T(8,128)(2,1)}, u32[]{:S(2)}, u32[]{:S(2)}) collective-permute-start(bf16[4,16,1280]{2,1,0:T(8,128)(2,1)} %get-tuple-element.88.rest_4_), channel_id=1, source_target_pairs={{0,32},{16,48},{32,0},{48,16},{1,33},{17,49},{33,1},{49,17},{2,34}... | collective-permute-start | bytes 491528 | tf_op jit(solution)/shard_map/ppermute | solution.py:1178
  20.5 1.1 collective-permute-start.9
  21.6 0.9 collective-permute-start.8
  22.5 3.9 %collective-permute-start.7 = (bf16[4,16,384]{2,1,0:T(8,128)(2,1)}, bf16[4,16,384]{2,1,0:T(8,128)(2,1)}, u32[]{:S(2)}, u32[]{:S(2)}) collective-permute-start(bf16[4,16,384]{2,1,0:T(8,128)(2,1)} %get-tuple-element.87.rest_0_), channel_id=1, source_target_pairs={{0,8},{4,12},{8,0},{12,4},{1,9},{5,13},{9,1},{13,5},{2,10},{6,14},... | collective-permute-start | bytes 147464 | tf_op jit(solution)/shard_map/ppermute | solution.py:1178
  26.4 0.7 collective-permute-start.6
  27.1 1.7 collective-permute-done.7.rest_3_
  28.8 1.6 collective-permute-start.5
  30.3 0.5 collective-permute-done.6.rest_2_
  30.8 4.1 %collective-permute-done.5.rest_1_ = bf16[4,16,384]{2,1,0:T(8,128)(2,1)} collective-permute-done((bf16[4,16,384]{2,1,0:T(8,128)(2,1)}, bf16[4,16,384]{2,1,0:T(8,128)(2,1)}, u32[]{:S(2)}, u32[]{:S(2)}) %collective-permute-start.5) | collective-permute-done | bytes 49184 | tf_op jit(solution)/shard_map/ppermute | solution.py:1178
  34.9 2.9 %join_planes.1 = (bf16[2,8,16,384]{3,2,1,0:T(8,128)(2,1)}, bf16[2,8,16,1280]{3,2,1,0:T(8,128)(2,1)}) custom-call(s32[8]{0:T(128)} %concatenate.3.info, bf16[4,16,384]{2,1,0:T(8,128)(2,1)} %get-tuple-element.87.rest_0_, bf16[4,16,384]{2,1,0:T(8,128)(2,1)} %collective-permute-done.5.rest_1_, bf16[4,16,384]{2,1,0:T(8,128)(2,1)} %collective-permute-done.6.rest_2_, ...), custom_call_target="tpu_custom_call" | custom-call | flops 200000000 | bytes 65536 | tf_op jit(solution)/shard_map/join_planes/pallas_call | solution.py:851
  37.7 0.6 collective-permute-start.19
  38.4 1.8 collective-permute-start.13
  40.2 0.7 collective-permute-start.12
  40.9 1.3 collective-permute-start.11
  42.2 2.6 %collective-permute-start.17 = (bf16[2,4,32,384]{3,2,1,0:T(8,128)(2,1)}, bf16[2,4,32,384]{3,2,1,0:T(8,128)(2,1)S(1)}, u32[]{:S(2)}, u32[]{:S(2)}) collective-permute-start(bf16[2,4,32,384]{3,2,1,0:T(8,128)(2,1)} %bitcast.18), channel_id=1, source_target_pairs={{0,48},{16,0},{32,16},{48,32},{1,49},{17,1},{33,17},{49,33},{2,50}... | collective-permute-start | bytes 589832 | tf_op jit(solution)/shard_map/ppermute | solution.py:1178
  45.1 2.3 %collective-permute-start.15 = (bf16[2,4,32,384]{3,2,1,0:T(8,128)(2,1)}, bf16[2,4,32,384]{3,2,1,0:T(8,128)(2,1)S(1)}, u32[]{:S(2)}, u32[]{:S(2)}) collective-permute-start(bf16[2,4,32,384]{3,2,1,0:T(8,128)(2,1)} %bitcast.19), channel_id=1, source_target_pairs={{0,16},{16,32},{32,48},{48,0},{1,17},{17,33},{33,49},{49,1},{2,18}... | collective-permute-start | bytes 589832 | tf_op jit(solution)/shard_map/ppermute | solution.py:1178
  47.4 1.3 collective-permute-done.17.rest_4_
  48.7 4.3 %collective-permute-done.15.rest_2_ = bf16[2,4,32,384]{3,2,1,0:T(8,128)(2,1)S(1)} collective-permute-done((bf16[2,4,32,384]{3,2,1,0:T(8,128)(2,1)}, bf16[2,4,32,384]{3,2,1,0:T(8,128)(2,1)S(1)}, u32[]{:S(2)}, u32[]{:S(2)}) %collective-permute-start.15) | collective-permute-done | bytes 196640 | tf_op jit(solution)/shard_map/ppermute | solution.py:1178
  53.0 0.5 collective-permute-start.18
  53.5 0.9 collective-permute-done.20.rest_7_
  54.7 0.4 copy-done.4
  55.1 0.7 copy-done.5
  56.0 14.3 %attend_forward.1 = (bf16[3,1536,256]{2,1,0:T(8,128)(2,1)}, bf16[3,512,256]{2,1,0:T(8,128)(2,1)}, f32[3,8,256]{2,1,0:T(8,128)}, bf16[2,4,4,32,768]{4,3,2,1,0:T(8,128)(2,1)}, f32[8,128]{1,0:T(8,128)}) custom-call(s32[8]{0:T(128)} %concatenate.3.info, f32[3,2,256,512]{3,2,1,0:T(8,128)} %frames.5, f32[2,512]{1,0:T(2,128)} %norm.3, ...), custom_call_target="tpu_custom_call" | custom-call | flops 200000000 | bytes 65536 | tf_op jit(solution)/shard_map/attend_forward/pallas_call | solution.py:851
  70.5 0.4 collective-permute-start.22
  71.0 0.4 collective-permute-start.24
  71.4 1.4 collective-permute-done.21.rest_1_
  72.8 0.9 collective-permute-done.22.rest_3_
  73.7 0.9 collective-permute-done.23.rest_5_
  74.6 0.9 collective-permute-done.24.rest_7_
  75.6 38.0 %mixer_both.1 = (bf16[3,256,512]{2,1,0:T(8,128)(2,1)}, f32[3,256,512]{2,1,0:T(8,128)}, bf16[3,512,256]{2,1,0:T(8,128)(2,1)}, bf16[64,16,1280]{2,1,0:T(8,128)(2,1...) custom-call(s32[8]{0:T(128)} %concatenate.3.info, f32[3,2,256,512]{3,2,1,0:T(8,128)} %frames.5, ...), custom_call_target="tpu_custom_call" | custom-call | flops 200000000 | bytes 65536 | tf_op jit(solution)/shard_map/mixer_both/pallas_call | solution.py:851
  114.2 0.8 collective-permute-start.27
  115.0 4.3 %collective-permute-done.26.small_other = f32[512,128]{1,0:T(8,128)} collective-permute-done((f32[512,128]{1,0:T(8,128)}, f32[512,128]{1,0:T(8,128)}, u32[]{:S(2)}, u32[]{:S(2)}) %collective-permute-start.26) | collective-permute-done | bytes 262176 | tf_op jit(solution)/shard_map/ppermute | solution.py:1161
  119.3 6.2 %sum_mixer.1 = (bf16[16,16,1280]{2,1,0:T(8,128)(2,1)}, bf16[16,16,1280]{2,1,0:T(8,128)(2,1)}, bf16[16,16,1280]{2,1,0:T(8,128)(2,1)}, bf16[16,16,1280]{2,1,0:T(8,128)(2,1)}, bf16[16,64,128]{2,1,0:T(8,128)(2,1)}) custom-call(s32[8]{0:T(128)} %concatenate.3.info, bf16[64,16,1280]{2,1,0:T(8,128)(2,1)} %get-tuple-element.98.keep, ...), custom_call_target="tpu_custom_call" | custom-call | flops 200000000 | bytes 65536 | tf_op jit(solution)/shard_map/sum_mixer/pallas_call | solution.py:851
  125.5 0.4 collective-permute-start.28
  125.9 2.9 %collective-permute-start.29 = (bf16[16,16,1280]{2,1,0:T(8,128)(2,1)}, bf16[16,16,1280]{2,1,0:T(8,128)(2,1)}, u32[]{:S(2)}, u32[]{:S(2)}) collective-permute-start(bf16[16,16,1280]{2,1,0:T(8,128)(2,1)} %get-tuple-element.118), channel_id=1, source_target_pairs={{0,48},{16,0},{32,16},{48,32},{1,49},{17,1},{33,17},{49,33},{2,50}... | collective-permute-start | bytes 1966088 | tf_op jit(solution)/shard_map/ppermute | solution.py:1178
  129.1 17.5 %attend_backward.1 = (bf16[3,256,512]{2,1,0:T(8,128)(2,1)}, bf16[64,16,512]{2,1,0:T(8,128)(2,1)}, bf16[64,16,512]{2,1,0:T(8,128)(2,1)}) custom-call(s32[8]{0:T(128)} %concatenate.3.info, f32[3,2,256,512]{3,2,1,0:T(8,128)} %frames.5, f32[3,256,512]{2,1,0:T(8,128)} %get-tuple-element.105.grad_mixed, bf16[3,1536,256]{2,1,0:T(8,128)(2,1)} %get-tuple-element.106.triple, ...), custom_call_target="tpu_custom_call" | custom-call | flops 200000000 | bytes 65536 | tf_op jit(solution)/shard_map/attend_backward/pallas_call | solution.py:851
  146.6 6.2 %all-to-all-start = ((bf16[16,64,128]{2,1,0:T(8,128)(2,1)}), bf16[16,64,128]{2,1,0:T(8,128)(2,1)}, u32[]{:S(2)}, u32[]{:S(2)}) async-start(bf16[16,64,128]{2,1,0:T(8,128)(2,1)} %get-tuple-element.116), calls=%async_computation | async-start | bytes 524288 | tf_op jit(solution)/shard_map/all_to_all | solution.py:1201
  152.8 6.5 %all-to-all-done.small_terms = bf16[16,64,128]{2,1,0:T(8,128)(2,1)} async-done(((bf16[16,64,128]{2,1,0:T(8,128)(2,1)}), bf16[16,64,128]{2,1,0:T(8,128)(2,1)}, u32[]{:S(2)}, u32[]{:S(2)}) %all-to-all-start) | async-done | bytes 262176 | tf_op jit(solution)/shard_map/all_to_all | solution.py:1201
  159.5 1.7 collective-permute-start.35
  161.1 1.3 collective-permute-done.31.other
  162.5 4.5 %sum_attend.1 = (bf16[17,16,512]{2,1,0:T(8,128)(2,1)}, bf16[17,16,512]{2,1,0:T(8,128)(2,1)}, bf16[17,16,512]{2,1,0:T(8,128)(2,1)}, bf16[17,16,512]{2,1,0:T(8,128)(2,1)}) custom-call(s32[8]{0:T(128)} %concatenate.3.info, bf16[64,16,512]{2,1,0:T(8,128)(2,1)} %get-tuple-element.120.keep, bf16[64,16,512]{2,1,0:T(8,128)(2,1)} %collective-permute-done.31.other, ...), custom_call_target="tpu_custom_call" | custom-call | flops 200000000 | bytes 65536 | tf_op jit(solution)/shard_map/sum_attend/pallas_call | solution.py:851
  167.0 1.5 collective-permute-start.32
  168.5 1.8 collective-permute-start.33
  170.3 2.2 %collective-permute-start.34 = (bf16[17,16,512]{2,1,0:T(8,128)(2,1)}, bf16[17,16,512]{2,1,0:T(8,128)(2,1)}, u32[]{:S(2)}, u32[]{:S(2)}) collective-permute-start(bf16[17,16,512]{2,1,0:T(8,128)(2,1)} %get-tuple-element.126), channel_id=1, source_target_pairs={{0,32},{16,48},{32,0},{48,16},{1,33},{17,49},{33,1},{49,17},{2,34}... | collective-permute-start | bytes 835592 | tf_op jit(solution)/shard_map/ppermute | solution.py:1178
  172.5 3.5 %place_pair.2 = f32[3,2,256,512]{3,2,1,0:T(8,128)} custom-call(s32[8]{0:T(128)} %concatenate.3.info, bf16[3,256,512]{2,1,0:T(8,128)(2,1)} %get-tuple-element.115.own, bf16[3,256,512]{2,1,0:T(8,128)(2,1)} %collective-permute-done.27.other), custom_call_target="tpu_custom_call" | custom-call | flops 200000000 | bytes 65536 | tf_op jit(solution)/shard_map/place_pair/pallas_call | solution.py:851
  176.0 3.5 %sum_four.1.mixer = bf16[16,16,1280]{2,1,0:T(8,128)(2,1)} custom-call(s32[8]{0:T(128)} %concatenate.3.info, bf16[16,16,1280]{2,1,0:T(8,128)(2,1)} %get-tuple-element.127.rest_0_, bf16[16,16,1280]{2,1,0:T(8,128)(2,1)} %collective-permute-done.28.rest_1_, bf16[16,16,1280]{2,1,0:T(8,128)(2,1)} %collective-permute-done.29.rest_2_, ...), custom_call_target="tpu_custom_call" | custom-call | flops 200000000 | bytes 65536 | tf_op jit(solution)/shard_map/sum_four/pallas_call | solution.py:851
  179.8 4.0 %collective-permute-done.34.rest_3_ = bf16[17,16,512]{2,1,0:T(8,128)(2,1)} collective-permute-done((bf16[17,16,512]{2,1,0:T(8,128)(2,1)}, bf16[17,16,512]{2,1,0:T(8,128)(2,1)}, u32[]{:S(2)}, u32[]{:S(2)}) %collective-permute-start.34) | collective-permute-done | bytes 278560 | tf_op jit(solution)/shard_map/ppermute | solution.py:1178
  183.7 3.3 %join_terms.1 = bf16[16,16,2304]{2,1,0:T(8,128)(2,1)} custom-call(s32[8]{0:T(128)} %concatenate.3.info, bf16[16,16,1280]{2,1,0:T(8,128)(2,1)} %sum_four.1.mixer, bf16[17,16,512]{2,1,0:T(8,128)(2,1)} %get-tuple-element.136.rest_0_, bf16[17,16,512]{2,1,0:T(8,128)(2,1)} %collective-permute-done.32.rest_1_, ...), custom_call_target="tpu_custom_call" | custom-call | flops 200000000 | bytes 65536 | tf_op jit(solution)/shard_map/join_terms/pallas_call | solution.py:851
  187.1 6.4 %all-to-all-start.1 = ((bf16[16,16,2304]{2,1,0:T(8,128)(2,1)}), bf16[16,16,2304]{2,1,0:T(8,128)(2,1)}, u32[]{:S(2)}, u32[]{:S(2)}) async-start(bf16[16,16,2304]{2,1,0:T(8,128)(2,1)} %join_terms.1), calls=%async_computation.1 | async-start | bytes 2359296 | tf_op jit(solution)/shard_map/all_to_all | solution.py:1201
  193.5 3.5 %place_pair.3 = f32[3,2,256,512]{3,2,1,0:T(8,128)} custom-call(s32[8]{0:T(128)} %concatenate.3.info, bf16[3,256,512]{2,1,0:T(8,128)(2,1)} %get-tuple-element.131.own, bf16[3,256,512]{2,1,0:T(8,128)(2,1)} %collective-permute-done.35.other), custom_call_target="tpu_custom_call" | custom-call | flops 200000000 | bytes 65536 | tf_op jit(solution)/shard_map/place_pair/pallas_call | solution.py:851
  196.9 14.9 %all-to-all-done.1.terms = bf16[16,16,2304]{2,1,0:T(8,128)(2,1)} async-done(((bf16[16,16,2304]{2,1,0:T(8,128)(2,1)}), bf16[16,16,2304]{2,1,0:T(8,128)(2,1)}, u32[]{:S(2)}, u32[]{:S(2)}) %all-to-all-start.1) | async-done | bytes 1179680 | tf_op jit(solution)/shard_map/all_to_all | solution.py:1201
  211.9 3.7 %finish.1 = (f32[3,8,256]{2,1,0:T(8,128)}, f32[8,256]{1,0:T(8,128)}, f32[8,2,768]{2,1,0:T(2,128)}, f32[8,768]{1,0:T(8,128)}, f32[2,512]{1,0:T(2,128)}, /*index=5...) custom-call(s32[8]{0:T(128)} %concatenate.3.info, ...), custom_call_target="tpu_custom_call" | custom-call | flops 200000000 | bytes 65536 | tf_op jit(solution)/shard_map/finish/pallas_call | solution.py:851
  (41 shorter events, 2.4 us)
Async XLA Ops:
  3.5 2.6 %collective-permute-start = (bf16[8,3328]{1,0:T(8,128)(2,1)}, bf16[8,3328]{1,0:T(8,128)(2,1)}, u32[]{:S(2)}, u32[]{:S(2)}) collective-permute-start(bf16[8,3328]{1,0:T(8,128)(2,1)} %get-tuple-element.83.local), channel_id=1, source_target_pairs={{0,1},{1,0},{2,3},{3,2},{4,5},{5,4},{6,7},{7,6},{8,9},{9,8},{10,11... | collective-permute-start | bytes 159752 | tf_op jit(solution)/shard_map/ppermute | solution.py:1161
  3.5 13.9 %collective-permute-start.4 = (f32[35,768]{1,0:T(8,128)}, f32[35,768]{1,0:T(8,128)}, u32[]{:S(2)}, u32[]{:S(2)}) collective-permute-start(f32[35,768]{1,0:T(8,128)} %get-tuple-element.86.own), channel_id=1, source_target_pairs={{0,64},{64,0},{1,65},{65,1},{2,66},{66,2},{3,67},{67,3},{4,68},{68... | collective-permute-start | bytes 322568 | tf_op jit(solution)/shard_map/ppermute | solution.py:1161
  8.3 6.0 %collective-permute-start.3 = (bf16[16,1664]{1,0:T(8,128)(2,1)}, bf16[16,1664]{1,0:T(8,128)(2,1)}, u32[]{:S(2)}, u32[]{:S(2)}) collective-permute-start(bf16[16,1664]{1,0:T(8,128)(2,1)} %pair_rows.1.rest_0_), channel_id=1, source_target_pairs={{0,2},{64,66},{2,0},{66,64},{1,3},{65,67},{3,1},{67,65},{4,6},{68,... | collective-permute-start | bytes 159752 | tf_op jit(solution)/shard_map/ppermute | solution.py:1172
  8.9 5.4 %collective-permute-start.2 = (bf16[16,1664]{1,0:T(8,128)(2,1)}, bf16[16,1664]{1,0:T(8,128)(2,1)}, u32[]{:S(2)}, u32[]{:S(2)}) collective-permute-start(bf16[16,1664]{1,0:T(8,128)(2,1)} %pair_rows.1.rest_0_), channel_id=1, source_target_pairs={{0,66},{64,0},{2,64},{66,2},{1,67},{65,1},{3,65},{67,3},{4,70},{68... | collective-permute-start | bytes 159752 | tf_op jit(solution)/shard_map/ppermute | solution.py:1172
  10.5 4.7 %collective-permute-start.1 = (bf16[16,1664]{1,0:T(8,128)(2,1)}, bf16[16,1664]{1,0:T(8,128)(2,1)}, u32[]{:S(2)}, u32[]{:S(2)}) collective-permute-start(bf16[16,1664]{1,0:T(8,128)(2,1)} %pair_rows.1.rest_0_), channel_id=1, source_target_pairs={{0,64},{64,2},{2,66},{66,0},{1,65},{65,3},{3,67},{67,1},{4,68},{68... | collective-permute-start | bytes 159752 | tf_op jit(solution)/shard_map/ppermute | solution.py:1172
  17.4 17.4 %collective-permute-start.10 = (bf16[4,16,1280]{2,1,0:T(8,128)(2,1)}, bf16[4,16,1280]{2,1,0:T(8,128)(2,1)}, u32[]{:S(2)}, u32[]{:S(2)}) collective-permute-start(bf16[4,16,1280]{2,1,0:T(8,128)(2,1)} %get-tuple-element.88.rest_4_), channel_id=1, source_target_pairs={{0,32},{16,48},{32,0},{48,16},{1,33},{17,49},{33,1},{49,17},{2,34}... | collective-permute-start | bytes 491528 | tf_op jit(solution)/shard_map/ppermute | solution.py:1178
  20.5 14.4 %collective-permute-start.9 = (bf16[4,16,1280]{2,1,0:T(8,128)(2,1)}, bf16[4,16,1280]{2,1,0:T(8,128)(2,1)}, u32[]{:S(2)}, u32[]{:S(2)}) collective-permute-start(bf16[4,16,1280]{2,1,0:T(8,128)(2,1)} %get-tuple-element.88.rest_4_), channel_id=1, source_target_pairs={{0,48},{16,0},{32,16},{48,32},{1,49},{17,1},{33,17},{49,33},{2,50}... | collective-permute-start | bytes 491528 | tf_op jit(solution)/shard_map/ppermute | solution.py:1178
  21.6 13.3 %collective-permute-start.8 = (bf16[4,16,1280]{2,1,0:T(8,128)(2,1)}, bf16[4,16,1280]{2,1,0:T(8,128)(2,1)}, u32[]{:S(2)}, u32[]{:S(2)}) collective-permute-start(bf16[4,16,1280]{2,1,0:T(8,128)(2,1)} %get-tuple-element.88.rest_4_), channel_id=1, source_target_pairs={{0,16},{16,32},{32,48},{48,0},{1,17},{17,33},{33,49},{49,1},{2,18}... | collective-permute-start | bytes 491528 | tf_op jit(solution)/shard_map/ppermute | solution.py:1178
  22.5 6.3 %collective-permute-start.7 = (bf16[4,16,384]{2,1,0:T(8,128)(2,1)}, bf16[4,16,384]{2,1,0:T(8,128)(2,1)}, u32[]{:S(2)}, u32[]{:S(2)}) collective-permute-start(bf16[4,16,384]{2,1,0:T(8,128)(2,1)} %get-tuple-element.87.rest_0_), channel_id=1, source_target_pairs={{0,8},{4,12},{8,0},{12,4},{1,9},{5,13},{9,1},{13,5},{2,10},{6,14},... | collective-permute-start | bytes 147464 | tf_op jit(solution)/shard_map/ppermute | solution.py:1178
  26.4 4.4 %collective-permute-start.6 = (bf16[4,16,384]{2,1,0:T(8,128)(2,1)}, bf16[4,16,384]{2,1,0:T(8,128)(2,1)}, u32[]{:S(2)}, u32[]{:S(2)}) collective-permute-start(bf16[4,16,384]{2,1,0:T(8,128)(2,1)} %get-tuple-element.87.rest_0_), channel_id=1, source_target_pairs={{0,12},{4,0},{8,4},{12,8},{1,13},{5,1},{9,5},{13,9},{2,14},{6,2},{... | collective-permute-start | bytes 147464 | tf_op jit(solution)/shard_map/ppermute | solution.py:1178
  28.8 6.1 %collective-permute-start.5 = (bf16[4,16,384]{2,1,0:T(8,128)(2,1)}, bf16[4,16,384]{2,1,0:T(8,128)(2,1)}, u32[]{:S(2)}, u32[]{:S(2)}) collective-permute-start(bf16[4,16,384]{2,1,0:T(8,128)(2,1)} %get-tuple-element.87.rest_0_), channel_id=1, source_target_pairs={{0,4},{4,8},{8,12},{12,0},{1,5},{5,9},{9,13},{13,1},{2,6},{6,10},{... | collective-permute-start | bytes 147464 | tf_op jit(solution)/shard_map/ppermute | solution.py:1178
  37.7 7.4 %collective-permute-start.19 = (bf16[2,4,32,384]{3,2,1,0:T(8,128)(2,1)}, bf16[2,4,32,384]{3,2,1,0:T(8,128)(2,1)S(1)}, u32[]{:S(2)}, u32[]{:S(2)}) collective-permute-start(bf16[2,4,32,384]{3,2,1,0:T(8,128)(2,1)} %bitcast.17), channel_id=1, source_target_pairs={{0,32},{16,48},{32,0},{48,16},{1,33},{17,49},{33,1},{49,17},{2,34}... | collective-permute-start | bytes 589832 | tf_op jit(solution)/shard_map/ppermute | solution.py:1178
  38.4 31.8 %collective-permute-start.13 = (bf16[2,4,32,1280]{3,2,1,0:T(8,128)(2,1)}, bf16[2,4,32,1280]{3,2,1,0:T(8,128)(2,1)}, u32[]{:S(2)}, u32[]{:S(2)}) collective-permute-start(bf16[2,4,32,1280]{3,2,1,0:T(8,128)(2,1)} %bitcast.12), channel_id=1, source_target_pairs={{0,8},{4,12},{8,0},{12,4},{1,9},{5,13},{9,1},{13,5},{2,10},{6,14},... | collective-permute-start | bytes 1966088 | tf_op jit(solution)/shard_map/ppermute | solution.py:1178
  40.2 30.0 %collective-permute-start.12 = (bf16[2,4,32,1280]{3,2,1,0:T(8,128)(2,1)}, bf16[2,4,32,1280]{3,2,1,0:T(8,128)(2,1)}, u32[]{:S(2)}, u32[]{:S(2)}) collective-permute-start(bf16[2,4,32,1280]{3,2,1,0:T(8,128)(2,1)} %bitcast.13), channel_id=1, source_target_pairs={{0,12},{4,0},{8,4},{12,8},{1,13},{5,1},{9,5},{13,9},{2,14},{6,2},{... | collective-permute-start | bytes 1966088 | tf_op jit(solution)/shard_map/ppermute | solution.py:1178
  40.9 29.3 %collective-permute-start.11 = (bf16[2,4,32,1280]{3,2,1,0:T(8,128)(2,1)}, bf16[2,4,32,1280]{3,2,1,0:T(8,128)(2,1)}, u32[]{:S(2)}, u32[]{:S(2)}) collective-permute-start(bf16[2,4,32,1280]{3,2,1,0:T(8,128)(2,1)} %bitcast.14), channel_id=1, source_target_pairs={{0,4},{4,8},{8,12},{12,0},{1,5},{5,9},{9,13},{13,1},{2,6},{6,10},{... | collective-permute-start | bytes 1966088 | tf_op jit(solution)/shard_map/ppermute | solution.py:1178
  42.2 6.4 %collective-permute-start.17 = (bf16[2,4,32,384]{3,2,1,0:T(8,128)(2,1)}, bf16[2,4,32,384]{3,2,1,0:T(8,128)(2,1)S(1)}, u32[]{:S(2)}, u32[]{:S(2)}) collective-permute-start(bf16[2,4,32,384]{3,2,1,0:T(8,128)(2,1)} %bitcast.18), channel_id=1, source_target_pairs={{0,48},{16,0},{32,16},{48,32},{1,49},{17,1},{33,17},{49,33},{2,50}... | collective-permute-start | bytes 589832 | tf_op jit(solution)/shard_map/ppermute | solution.py:1178
  45.1 7.8 %copy-start = (bf16[2,4,32,384]{3,2,1,0:T(8,128)(2,1)}, bf16[2,4,32,384]{3,2,1,0:T(8,128)(2,1)S(1)}, u32[]{:S(2)}) copy-start(bf16[2,4,32,384]{3,2,1,0:T(8,128)(2,1)S(1)} %collective-permute-done.19.rest_6_) | copy-start | bytes 589828
  45.1 7.8 %collective-permute-start.15 = (bf16[2,4,32,384]{3,2,1,0:T(8,128)(2,1)}, bf16[2,4,32,384]{3,2,1,0:T(8,128)(2,1)S(1)}, u32[]{:S(2)}, u32[]{:S(2)}) collective-permute-start(bf16[2,4,32,384]{3,2,1,0:T(8,128)(2,1)} %bitcast.19), channel_id=1, source_target_pairs={{0,16},{16,32},{32,48},{48,0},{1,17},{17,33},{33,49},{49,1},{2,18}... | collective-permute-start | bytes 589832 | tf_op jit(solution)/shard_map/ppermute | solution.py:1178
  48.7 5.7 %copy-start.1 = (bf16[2,4,32,384]{3,2,1,0:T(8,128)(2,1)}, bf16[2,4,32,384]{3,2,1,0:T(8,128)(2,1)S(1)}, u32[]{:S(2)}) copy-start(bf16[2,4,32,384]{3,2,1,0:T(8,128)(2,1)S(1)} %collective-permute-done.17.rest_4_) | copy-start | bytes 589828
  48.7 4.3 %collective-permute-start.14 = (bf16[2,4,32,384]{3,2,1,0:T(8,128)(2,1)}, bf16[2,4,32,384]{3,2,1,0:T(8,128)(2,1)S(1)}, u32[]{:S(2)}, u32[]{:S(2)}) collective-permute-start(bf16[2,4,32,384]{3,2,1,0:T(8,128)(2,1)} %bitcast.20), channel_id=1, source_target_pairs={{0,1},{1,0},{2,3},{3,2},{4,5},{5,4},{6,7},{7,6},{8,9},{9,8},{10,11... | collective-permute-start | bytes 589832 | tf_op jit(solution)/shard_map/ppermute | solution.py:1161
  52.9 1.7 copy-start.2
  52.9 1.4 collective-permute-start.20
  53.0 1.7 copy-start.3
  53.0 1.7 collective-permute-start.18
  54.4 0.7 copy-start.4
  54.4 1.6 collective-permute-start.16
  55.1 0.7 copy-start.5
  70.3 2.5 %collective-permute-start.21 = (bf16[2,4,32,1280]{3,2,1,0:T(8,128)(2,1)}, bf16[2,4,32,1280]{3,2,1,0:T(8,128)(2,1)}, u32[]{:S(2)}, u32[]{:S(2)}) collective-permute-start(bf16[2,4,32,1280]{3,2,1,0:T(8,128)(2,1)} %bitcast.15), channel_id=1, source_target_pairs={{0,1},{1,0},{2,3},{3,2},{4,5},{5,4},{6,7},{7,6},{8,9},{9,8},{10,11... | collective-permute-start | bytes 1966088 | tf_op jit(solution)/shard_map/ppermute | solution.py:1161
  70.5 3.2 %collective-permute-start.22 = (bf16[2,4,32,1280]{3,2,1,0:T(8,128)(2,1)}, bf16[2,4,32,1280]{3,2,1,0:T(8,128)(2,1)}, u32[]{:S(2)}, u32[]{:S(2)}) collective-permute-start(bf16[2,4,32,1280]{3,2,1,0:T(8,128)(2,1)} %collective-permute-done.11.rest_2_), channel_id=1, source_target_pairs={{0,1},{1,0},{2,3},{3,2},{4,5},{5,4},{6,7},{7,6},{8,9},{9,8},{10,11... | collective-permute-start | bytes 1966088 | tf_op jit(solution)/shard_map/ppermute | solution.py:1161
  70.8 3.8 %collective-permute-start.23 = (bf16[2,4,32,1280]{3,2,1,0:T(8,128)(2,1)}, bf16[2,4,32,1280]{3,2,1,0:T(8,128)(2,1)}, u32[]{:S(2)}, u32[]{:S(2)}) collective-permute-start(bf16[2,4,32,1280]{3,2,1,0:T(8,128)(2,1)} %collective-permute-done.12.rest_4_), channel_id=1, source_target_pairs={{0,1},{1,0},{2,3},{3,2},{4,5},{5,4},{6,7},{7,6},{8,9},{9,8},{10,11... | collective-permute-start | bytes 1966088 | tf_op jit(solution)/shard_map/ppermute | solution.py:1161
  71.0 4.6 %collective-permute-start.24 = (bf16[2,4,32,1280]{3,2,1,0:T(8,128)(2,1)}, bf16[2,4,32,1280]{3,2,1,0:T(8,128)(2,1)}, u32[]{:S(2)}, u32[]{:S(2)}) collective-permute-start(bf16[2,4,32,1280]{3,2,1,0:T(8,128)(2,1)} %collective-permute-done.13.rest_6_), channel_id=1, source_target_pairs={{0,1},{1,0},{2,3},{3,2},{4,5},{5,4},{6,7},{7,6},{8,9},{9,8},{10,11... | collective-permute-start | bytes 1966088 | tf_op jit(solution)/shard_map/ppermute | solution.py:1161
  113.6 5.7 %collective-permute-start.25 = (bf16[64,16,1280]{2,1,0:T(8,128)(2,1)}, bf16[64,16,1280]{2,1,0:T(8,128)(2,1)}, u32[]{:S(2)}, u32[]{:S(2)}) collective-permute-start(bf16[64,16,1280]{2,1,0:T(8,128)(2,1)} %get-tuple-element.99), channel_id=1, source_target_pairs={{0,1},{1,0},{2,3},{3,2},{4,5},{5,4},{6,7},{7,6},{8,9},{9,8},{10,11... | collective-permute-start | bytes 7864328 | tf_op jit(solution)/shard_map/ppermute | solution.py:1161
  113.8 5.5 %collective-permute-start.26 = (f32[512,128]{1,0:T(8,128)}, f32[512,128]{1,0:T(8,128)}, u32[]{:S(2)}, u32[]{:S(2)}) collective-permute-start(f32[512,128]{1,0:T(8,128)} %get-tuple-element.100.small), channel_id=1, source_target_pairs={{0,1},{1,0},{2,3},{3,2},{4,5},{5,4},{6,7},{7,6},{8,9},{9,8},{10,11... | collective-permute-start | bytes 786440 | tf_op jit(solution)/shard_map/ppermute | solution.py:1161
  114.2 38.7 %collective-permute-start.27 = (bf16[3,256,512]{2,1,0:T(8,128)(2,1)}, bf16[3,256,512]{2,1,0:T(8,128)(2,1)}, u32[]{:S(2)}, u32[]{:S(2)}) collective-permute-start(bf16[3,256,512]{2,1,0:T(8,128)(2,1)} %get-tuple-element.115.own), channel_id=1, source_target_pairs={{0,64},{64,0},{1,65},{65,1},{2,66},{66,2},{3,67},{67,3},{4,68},{68... | collective-permute-start | bytes 2359304 | tf_op jit(solution)/shard_map/ppermute | solution.py:1161
  125.5 33.9 %collective-permute-start.28 = (bf16[16,16,1280]{2,1,0:T(8,128)(2,1)}, bf16[16,16,1280]{2,1,0:T(8,128)(2,1)}, u32[]{:S(2)}, u32[]{:S(2)}) collective-permute-start(bf16[16,16,1280]{2,1,0:T(8,128)(2,1)} %get-tuple-element.117), channel_id=1, source_target_pairs={{0,16},{16,32},{32,48},{48,0},{1,17},{17,33},{33,49},{49,1},{2,18}... | collective-permute-start | bytes 1966088 | tf_op jit(solution)/shard_map/ppermute | solution.py:1178
  125.9 33.5 %collective-permute-start.29 = (bf16[16,16,1280]{2,1,0:T(8,128)(2,1)}, bf16[16,16,1280]{2,1,0:T(8,128)(2,1)}, u32[]{:S(2)}, u32[]{:S(2)}) collective-permute-start(bf16[16,16,1280]{2,1,0:T(8,128)(2,1)} %get-tuple-element.118), channel_id=1, source_target_pairs={{0,48},{16,0},{32,16},{48,32},{1,49},{17,1},{33,17},{49,33},{2,50}... | collective-permute-start | bytes 1966088 | tf_op jit(solution)/shard_map/ppermute | solution.py:1178
  128.8 30.6 %collective-permute-start.30 = (bf16[16,16,1280]{2,1,0:T(8,128)(2,1)}, bf16[16,16,1280]{2,1,0:T(8,128)(2,1)}, u32[]{:S(2)}, u32[]{:S(2)}) collective-permute-start(bf16[16,16,1280]{2,1,0:T(8,128)(2,1)} %get-tuple-element.119), channel_id=1, source_target_pairs={{0,32},{16,48},{32,0},{48,16},{1,33},{17,49},{33,1},{49,17},{2,34}... | collective-permute-start | bytes 1966088 | tf_op jit(solution)/shard_map/ppermute | solution.py:1178
  146.6 12.8 %all-to-all-start = ((bf16[16,64,128]{2,1,0:T(8,128)(2,1)}), bf16[16,64,128]{2,1,0:T(8,128)(2,1)}, u32[]{:S(2)}, u32[]{:S(2)}) async-start(bf16[16,64,128]{2,1,0:T(8,128)(2,1)} %get-tuple-element.116), calls=%async_computation | async-start | bytes 524288 | tf_op jit(solution)/shard_map/all_to_all | solution.py:1201
  159.4 3.1 %collective-permute-start.31 = (bf16[64,16,512]{2,1,0:T(8,128)(2,1)}, bf16[64,16,512]{2,1,0:T(8,128)(2,1)}, u32[]{:S(2)}, u32[]{:S(2)}) collective-permute-start(bf16[64,16,512]{2,1,0:T(8,128)(2,1)} %get-tuple-element.121), channel_id=1, source_target_pairs={{0,1},{1,0},{2,3},{3,2},{4,5},{5,4},{6,7},{7,6},{8,9},{9,8},{10,11... | collective-permute-start | bytes 3145736 | tf_op jit(solution)/shard_map/ppermute | solution.py:1161
  159.5 20.3 %collective-permute-start.35 = (bf16[3,256,512]{2,1,0:T(8,128)(2,1)}, bf16[3,256,512]{2,1,0:T(8,128)(2,1)}, u32[]{:S(2)}, u32[]{:S(2)}) collective-permute-start(bf16[3,256,512]{2,1,0:T(8,128)(2,1)} %get-tuple-element.131.own), channel_id=1, source_target_pairs={{0,64},{64,0},{1,65},{65,1},{2,66},{66,2},{3,67},{67,3},{4,68},{68... | collective-permute-start | bytes 2359304 | tf_op jit(solution)/shard_map/ppermute | solution.py:1161
  167.0 12.7 %collective-permute-start.32 = (bf16[17,16,512]{2,1,0:T(8,128)(2,1)}, bf16[17,16,512]{2,1,0:T(8,128)(2,1)}, u32[]{:S(2)}, u32[]{:S(2)}) collective-permute-start(bf16[17,16,512]{2,1,0:T(8,128)(2,1)} %get-tuple-element.124), channel_id=1, source_target_pairs={{0,16},{16,32},{32,48},{48,0},{1,17},{17,33},{33,49},{49,1},{2,18}... | collective-permute-start | bytes 835592 | tf_op jit(solution)/shard_map/ppermute | solution.py:1178
  168.5 11.3 %collective-permute-start.33 = (bf16[17,16,512]{2,1,0:T(8,128)(2,1)}, bf16[17,16,512]{2,1,0:T(8,128)(2,1)}, u32[]{:S(2)}, u32[]{:S(2)}) collective-permute-start(bf16[17,16,512]{2,1,0:T(8,128)(2,1)} %get-tuple-element.125), channel_id=1, source_target_pairs={{0,48},{16,0},{32,16},{48,32},{1,49},{17,1},{33,17},{49,33},{2,50}... | collective-permute-start | bytes 835592 | tf_op jit(solution)/shard_map/ppermute | solution.py:1178
  170.3 13.4 %collective-permute-start.34 = (bf16[17,16,512]{2,1,0:T(8,128)(2,1)}, bf16[17,16,512]{2,1,0:T(8,128)(2,1)}, u32[]{:S(2)}, u32[]{:S(2)}) collective-permute-start(bf16[17,16,512]{2,1,0:T(8,128)(2,1)} %get-tuple-element.126), channel_id=1, source_target_pairs={{0,32},{16,48},{32,0},{48,16},{1,33},{17,49},{33,1},{49,17},{2,34}... | collective-permute-start | bytes 835592 | tf_op jit(solution)/shard_map/ppermute | solution.py:1178
  187.1 24.8 %all-to-all-start.1 = ((bf16[16,16,2304]{2,1,0:T(8,128)(2,1)}), bf16[16,16,2304]{2,1,0:T(8,128)(2,1)}, u32[]{:S(2)}, u32[]{:S(2)}) async-start(bf16[16,16,2304]{2,1,0:T(8,128)(2,1)} %join_terms.1), calls=%async_computation.1 | async-start | bytes 2359296 | tf_op jit(solution)/shard_map/all_to_all | solution.py:1201

commit v5 on v4

--- a/solution.py
+++ b/solution.py
@@ -440,24 +440,25 @@
         outs = []
         for b in range(2):
             first, second = b * 768, HALF + b * 768
+            into_first = dot_tn(low_s[...], hidden_s[:, first : first + 768])
+            into_second = dot_tn(low_s[...], hidden_s[:, second : second + 768])
+            out = dot_tn(grad_s[...], gated_s[:, first : first + 768])
+            attend = dot_tt(attend_s[...], context_s[b * 256 : (b + 1) * 256, :])
             pairs = [
-                (dot_tn(low_s[...], hidden_s[:, first : first + 256]),
-                 dot_tn(low_s[...], hidden_s[:, second + 512 : second + 768])),
-                (dot_tn(low_s[...], hidden_s[:, first + 256 : first + 512]),
-                 dot_tn(grad_s[...], gated_s[:, first : first + 256])),
-                (dot_tn(low_s[...], hidden_s[:, first + 512 : first + 768]),
-                 dot_tn(grad_s[...], gated_s[:, first + 256 : first + 512])),
-                (dot_tn(low_s[...], hidden_s[:, second : second + 256]),
-                 dot_tn(grad_s[...], gated_s[:, first + 512 : first + 768])),
-                (dot_tn(low_s[...], hidden_s[:, second + 256 : second + 512]),
-                 dot_tt(attend_s[...], context_s[b * 256 : (b + 1) * 256, :])),
+                (into_first[:, 0:256], into_second[:, 512:768]),
+                (into_first[:, 256:768], out[:, 0:512]),
+                (into_second[:, 0:256], out[:, 512:768]),
+                (into_second[:, 256:512], attend),
             ]
-            for i, (upper, lower) in enumerate(pairs):
-                upper, lower = upper.reshape(32, 2, 8, 256), lower.reshape(32, 2, 8, 256)
+            column = 0
+            for upper, lower in pairs:
+                width = upper.shape[1]
+                upper, lower = upper.reshape(32, 2, 8, width), lower.reshape(32, 2, 8, width)
                 for p in range(2):
-                    grads_s[p, b * 32 : (b + 1) * 32, :, i * 256 : (i + 1) * 256] = (
+                    grads_s[p, b * 32 : (b + 1) * 32, :, column : column + width] = (
                         jnp.concatenate([upper[:, p], lower[:, p]], axis=1).astype(BF16)
                     )
+                column += width
             chips = pl.ds(b * 32, 32)
             outs += start_all(
                 [

time: 217 us -> 217 us (level)
  no operation moved by 1% of the time
where the time goes in v5:
time: 217 us; the launch traced here: 216 us
  Pallas kernels  108 us (50%)
  waiting for transfers between devices  53.1 us (24%)
  starting transfers between devices  51.3 us (24%)
  local copies, waits for them, and re-layouts  2.9 us (1%)
    pallas_call x14, Pallas kernels, call(): pl.pallas_call(kernel, grid_spec=pltpu.PrefetchScalarGridSpec(num_scalar_...  108 us
    ppermute x18, starting transfers between devices, move(): lax.ppermute(block, axis, [(i, (i + distance) % 4) for i in range(4)])  29.6 us
    all_to_all x2, waiting for transfers between devices, exchange(): return lax.all_to_all(blocks, axes, 0, 0, tiled=True)  21.5 us
    ppermute x18, waiting for transfers between devices, move(): lax.ppermute(block, axis, [(i, (i + distance) % 4) for i in range(4)])  16 us
    all_to_all x2, starting transfers between devices, exchange(): return lax.all_to_all(blocks, axes, 0, 0, tiled=True)  12.6 us
    ppermute x15, waiting for transfers between devices, swap(): return lax.ppermute(value, axis, [(0, 1), (1, 0)])  11.4 us
    ppermute x15, starting transfers between devices, swap(): return lax.ppermute(value, axis, [(0, 1), (1, 0)])  6.38 us
  transfers between devices with their start and end apart: 38, of which 21 were waited for; matrix products, arithmetic and copies ran while one was open for 1% of the time, Pallas kernels for 27%

profile of v5, /device:TPU:16, one launch (start us, length us, event | category | flops | bytes accessed | tf_op | source)
XLA Modules:
  0.0 216.0 jit_solution(7112348426971333587)
XLA Ops:
  0.6 0.5 call_exported.0.info
  1.2 2.4 %pack_local.1 = (bf16[8,3328]{1,0:T(8,128)(2,1)}, f32[35,768]{1,0:T(8,128)}) custom-call(s32[8]{0:T(128)} %call_exported.0.info, f32[4]{0:T(128)} %slopes.1, bf16[3,8,256]{2,1,0:T(8,128)(2,1)} %bitcast.25, bf16[8,256]{1,0:T(8,128)(2,1)} %att_out.1, bf16[8,2,768]{2,1,0:T(2,128)(2,1)} %mix_in.1, bf16[8,768]{1,0:T(8,128)(2,1)} %mix_out.1, f32[31,768]{1,0:T(8,128)} %taps.1, ...), custom_call_target="tpu_custom_call" | custom-call | flops 200000000 | bytes 65536 | tf_op jit(solution)/shard_map/pack_local/pallas_call | solution.py:852
  3.5 1.3 collective-permute-start.4
  4.8 0.7 dynamic-slice_bitcast_fusion
  5.5 0.6 concatenate.3.info
  6.1 2.1 pair_rows.1.rest_0_
  8.3 0.6 collective-permute-start.3
  8.9 1.6 collective-permute-start.2
  10.5 0.5 collective-permute-start.1
  10.9 3.4 %collective-permute-done.3.rest_3_ = bf16[16,1664]{1,0:T(8,128)(2,1)} collective-permute-done((bf16[16,1664]{1,0:T(8,128)(2,1)}, bf16[16,1664]{1,0:T(8,128)(2,1)}, u32[]{:S(2)}, u32[]{:S(2)}) %collective-permute-start.3) | collective-permute-done | bytes 53280 | tf_op jit(solution)/shard_map/ppermute | solution.py:1173
  14.3 0.9 collective-permute-done.1.rest_1_
  15.2 2.3 %join_y.1 = (bf16[4,16,384]{2,1,0:T(8,128)(2,1)}, bf16[4,16,1280]{2,1,0:T(8,128)(2,1)}) custom-call(s32[8]{0:T(128)} %concatenate.3.info, bf16[16,1664]{1,0:T(8,128)(2,1)} %pair_rows.1.rest_0_, bf16[16,1664]{1,0:T(8,128)(2,1)} %collective-permute-done.1.rest_1_, bf16[16,1664]{1,0:T(8,128)(2,1)} %collective-permute-done.2.rest_2_, ...), custom_call_target="tpu_custom_call" | custom-call | flops 200000000 | bytes 65536 | tf_op jit(solution)/shard_map/join_y/pallas_call | solution.py:852
  17.4 3.0 %collective-permute-start.10 = (bf16[4,16,1280]{2,1,0:T(8,128)(2,1)}, bf16[4,16,1280]{2,1,0:T(8,128)(2,1)}, u32[]{:S(2)}, u32[]{:S(2)}) collective-permute-start(bf16[4,16,1280]{2,1,0:T(8,128)(2,1)} %get-tuple-element.88.rest_4_), channel_id=1, source_target_pairs={{0,32},{16,48},{32,0},{48,16},{1,33},{17,49},{33,1},{49,17},{2,34}... | collective-permute-start | bytes 491528 | tf_op jit(solution)/shard_map/ppermute | solution.py:1179
  20.5 1.1 collective-permute-start.9
  21.6 0.9 collective-permute-start.8
  22.5 3.9 %collective-permute-start.7 = (bf16[4,16,384]{2,1,0:T(8,128)(2,1)}, bf16[4,16,384]{2,1,0:T(8,128)(2,1)}, u32[]{:S(2)}, u32[]{:S(2)}) collective-permute-start(bf16[4,16,384]{2,1,0:T(8,128)(2,1)} %get-tuple-element.87.rest_0_), channel_id=1, source_target_pairs={{0,8},{4,12},{8,0},{12,4},{1,9},{5,13},{9,1},{13,5},{2,10},{6,14},... | collective-permute-start | bytes 147464 | tf_op jit(solution)/shard_map/ppermute | solution.py:1179
  26.4 0.7 collective-permute-start.6
  27.1 1.7 collective-permute-done.7.rest_3_
  28.8 1.6 collective-permute-start.5
  30.3 0.5 collective-permute-done.6.rest_2_
  30.8 4.1 %collective-permute-done.5.rest_1_ = bf16[4,16,384]{2,1,0:T(8,128)(2,1)} collective-permute-done((bf16[4,16,384]{2,1,0:T(8,128)(2,1)}, bf16[4,16,384]{2,1,0:T(8,128)(2,1)}, u32[]{:S(2)}, u32[]{:S(2)}) %collective-permute-start.5) | collective-permute-done | bytes 49184 | tf_op jit(solution)/shard_map/ppermute | solution.py:1179
  34.9 2.9 %join_planes.1 = (bf16[2,8,16,384]{3,2,1,0:T(8,128)(2,1)}, bf16[2,8,16,1280]{3,2,1,0:T(8,128)(2,1)}) custom-call(s32[8]{0:T(128)} %concatenate.3.info, bf16[4,16,384]{2,1,0:T(8,128)(2,1)} %get-tuple-element.87.rest_0_, bf16[4,16,384]{2,1,0:T(8,128)(2,1)} %collective-permute-done.5.rest_1_, bf16[4,16,384]{2,1,0:T(8,128)(2,1)} %collective-permute-done.6.rest_2_, ...), custom_call_target="tpu_custom_call" | custom-call | flops 200000000 | bytes 65536 | tf_op jit(solution)/shard_map/join_planes/pallas_call | solution.py:852
  37.7 0.6 collective-permute-start.19
  38.4 1.8 collective-permute-start.13
  40.2 0.7 collective-permute-start.12
  40.9 1.3 collective-permute-start.11
  42.2 2.6 %collective-permute-start.17 = (bf16[2,4,32,384]{3,2,1,0:T(8,128)(2,1)}, bf16[2,4,32,384]{3,2,1,0:T(8,128)(2,1)S(1)}, u32[]{:S(2)}, u32[]{:S(2)}) collective-permute-start(bf16[2,4,32,384]{3,2,1,0:T(8,128)(2,1)} %bitcast.18), channel_id=1, source_target_pairs={{0,48},{16,0},{32,16},{48,32},{1,49},{17,1},{33,17},{49,33},{2,50}... | collective-permute-start | bytes 589832 | tf_op jit(solution)/shard_map/ppermute | solution.py:1179
  45.1 2.3 %collective-permute-start.15 = (bf16[2,4,32,384]{3,2,1,0:T(8,128)(2,1)}, bf16[2,4,32,384]{3,2,1,0:T(8,128)(2,1)S(1)}, u32[]{:S(2)}, u32[]{:S(2)}) collective-permute-start(bf16[2,4,32,384]{3,2,1,0:T(8,128)(2,1)} %bitcast.19), channel_id=1, source_target_pairs={{0,16},{16,32},{32,48},{48,0},{1,17},{17,33},{33,49},{49,1},{2,18}... | collective-permute-start | bytes 589832 | tf_op jit(solution)/shard_map/ppermute | solution.py:1179
  47.4 1.3 collective-permute-done.17.rest_4_
  48.7 4.3 %collective-permute-done.15.rest_2_ = bf16[2,4,32,384]{3,2,1,0:T(8,128)(2,1)S(1)} collective-permute-done((bf16[2,4,32,384]{3,2,1,0:T(8,128)(2,1)}, bf16[2,4,32,384]{3,2,1,0:T(8,128)(2,1)S(1)}, u32[]{:S(2)}, u32[]{:S(2)}) %collective-permute-start.15) | collective-permute-done | bytes 196640 | tf_op jit(solution)/shard_map/ppermute | solution.py:1179
  53.0 0.5 collective-permute-start.18
  53.5 0.9 collective-permute-done.20.rest_7_
  54.7 0.4 copy-done.4
  55.1 0.7 copy-done.5
  56.0 14.3 %attend_forward.1 = (bf16[3,1536,256]{2,1,0:T(8,128)(2,1)}, bf16[3,512,256]{2,1,0:T(8,128)(2,1)}, f32[3,8,256]{2,1,0:T(8,128)}, bf16[2,4,4,32,768]{4,3,2,1,0:T(8,128)(2,1)}, f32[8,128]{1,0:T(8,128)}) custom-call(s32[8]{0:T(128)} %concatenate.3.info, f32[3,2,256,512]{3,2,1,0:T(8,128)} %frames.5, f32[2,512]{1,0:T(2,128)} %norm.3, ...), custom_call_target="tpu_custom_call" | custom-call | flops 200000000 | bytes 65536 | tf_op jit(solution)/shard_map/attend_forward/pallas_call | solution.py:852
  70.5 0.4 collective-permute-start.22
  71.4 1.4 collective-permute-done.21.rest_1_
  72.8 0.9 collective-permute-done.22.rest_3_
  73.7 0.9 collective-permute-done.23.rest_5_
  74.6 0.9 collective-permute-done.24.rest_7_
  75.6 38.0 %mixer_both.1 = (bf16[3,256,512]{2,1,0:T(8,128)(2,1)}, f32[3,256,512]{2,1,0:T(8,128)}, bf16[3,512,256]{2,1,0:T(8,128)(2,1)}, bf16[64,16,1280]{2,1,0:T(8,128)(2,1...) custom-call(s32[8]{0:T(128)} %concatenate.3.info, f32[3,2,256,512]{3,2,1,0:T(8,128)} %frames.5, ...), custom_call_target="tpu_custom_call" | custom-call | flops 200000000 | bytes 65536 | tf_op jit(solution)/shard_map/mixer_both/pallas_call | solution.py:852
  113.6 0.4 collective-permute-start.25
  114.4 0.8 collective-permute-start.27
  115.2 4.3 %collective-permute-done.26.small_other = f32[512,128]{1,0:T(8,128)} collective-permute-done((f32[512,128]{1,0:T(8,128)}, f32[512,128]{1,0:T(8,128)}, u32[]{:S(2)}, u32[]{:S(2)}) %collective-permute-start.26) | collective-permute-done | bytes 262176 | tf_op jit(solution)/shard_map/ppermute | solution.py:1162
  119.5 6.2 %sum_mixer.1 = (bf16[16,16,1280]{2,1,0:T(8,128)(2,1)}, bf16[16,16,1280]{2,1,0:T(8,128)(2,1)}, bf16[16,16,1280]{2,1,0:T(8,128)(2,1)}, bf16[16,16,1280]{2,1,0:T(8,128)(2,1)}, bf16[16,64,128]{2,1,0:T(8,128)(2,1)}) custom-call(s32[8]{0:T(128)} %concatenate.3.info, bf16[64,16,1280]{2,1,0:T(8,128)(2,1)} %get-tuple-element.98.keep, ...), custom_call_target="tpu_custom_call" | custom-call | flops 200000000 | bytes 65536 | tf_op jit(solution)/shard_map/sum_mixer/pallas_call | solution.py:852
  125.7 0.4 collective-permute-start.28
  126.1 2.9 %collective-permute-start.29 = (bf16[16,16,1280]{2,1,0:T(8,128)(2,1)}, bf16[16,16,1280]{2,1,0:T(8,128)(2,1)}, u32[]{:S(2)}, u32[]{:S(2)}) collective-permute-start(bf16[16,16,1280]{2,1,0:T(8,128)(2,1)} %get-tuple-element.118), channel_id=1, source_target_pairs={{0,48},{16,0},{32,16},{48,32},{1,49},{17,1},{33,17},{49,33},{2,50}... | collective-permute-start | bytes 1966088 | tf_op jit(solution)/shard_map/ppermute | solution.py:1179
  129.3 17.5 %attend_backward.1 = (bf16[3,256,512]{2,1,0:T(8,128)(2,1)}, bf16[64,16,512]{2,1,0:T(8,128)(2,1)}, bf16[64,16,512]{2,1,0:T(8,128)(2,1)}) custom-call(s32[8]{0:T(128)} %concatenate.3.info, f32[3,2,256,512]{3,2,1,0:T(8,128)} %frames.5, f32[3,256,512]{2,1,0:T(8,128)} %get-tuple-element.105.grad_mixed, bf16[3,1536,256]{2,1,0:T(8,128)(2,1)} %get-tuple-element.106.triple, ...), custom_call_target="tpu_custom_call" | custom-call | flops 200000000 | bytes 65536 | tf_op jit(solution)/shard_map/attend_backward/pallas_call | solution.py:852
  146.8 6.2 %all-to-all-start = ((bf16[16,64,128]{2,1,0:T(8,128)(2,1)}), bf16[16,64,128]{2,1,0:T(8,128)(2,1)}, u32[]{:S(2)}, u32[]{:S(2)}) async-start(bf16[16,64,128]{2,1,0:T(8,128)(2,1)} %get-tuple-element.116), calls=%async_computation | async-start | bytes 524288 | tf_op jit(solution)/shard_map/all_to_all | solution.py:1202
  153.0 6.5 %all-to-all-done.small_terms = bf16[16,64,128]{2,1,0:T(8,128)(2,1)} async-done(((bf16[16,64,128]{2,1,0:T(8,128)(2,1)}), bf16[16,64,128]{2,1,0:T(8,128)(2,1)}, u32[]{:S(2)}, u32[]{:S(2)}) %all-to-all-start) | async-done | bytes 262176 | tf_op jit(solution)/shard_map/all_to_all | solution.py:1202
  159.7 1.7 collective-permute-start.35
  161.3 1.3 collective-permute-done.31.other
  162.7 4.5 %sum_attend.1 = (bf16[17,16,512]{2,1,0:T(8,128)(2,1)}, bf16[17,16,512]{2,1,0:T(8,128)(2,1)}, bf16[17,16,512]{2,1,0:T(8,128)(2,1)}, bf16[17,16,512]{2,1,0:T(8,128)(2,1)}) custom-call(s32[8]{0:T(128)} %concatenate.3.info, bf16[64,16,512]{2,1,0:T(8,128)(2,1)} %get-tuple-element.120.keep, bf16[64,16,512]{2,1,0:T(8,128)(2,1)} %collective-permute-done.31.other, ...), custom_call_target="tpu_custom_call" | custom-call | flops 200000000 | bytes 65536 | tf_op jit(solution)/shard_map/sum_attend/pallas_call | solution.py:852
  167.2 1.5 collective-permute-start.32
  168.7 1.8 collective-permute-start.33
  170.5 2.2 %collective-permute-start.34 = (bf16[17,16,512]{2,1,0:T(8,128)(2,1)}, bf16[17,16,512]{2,1,0:T(8,128)(2,1)}, u32[]{:S(2)}, u32[]{:S(2)}) collective-permute-start(bf16[17,16,512]{2,1,0:T(8,128)(2,1)} %get-tuple-element.126), channel_id=1, source_target_pairs={{0,32},{16,48},{32,0},{48,16},{1,33},{17,49},{33,1},{49,17},{2,34}... | collective-permute-start | bytes 835592 | tf_op jit(solution)/shard_map/ppermute | solution.py:1179
  172.7 3.5 %place_pair.2 = f32[3,2,256,512]{3,2,1,0:T(8,128)} custom-call(s32[8]{0:T(128)} %concatenate.3.info, bf16[3,256,512]{2,1,0:T(8,128)(2,1)} %get-tuple-element.115.own, bf16[3,256,512]{2,1,0:T(8,128)(2,1)} %collective-permute-done.27.other), custom_call_target="tpu_custom_call" | custom-call | flops 200000000 | bytes 65536 | tf_op jit(solution)/shard_map/place_pair/pallas_call | solution.py:852
  176.2 3.5 %sum_four.1.mixer = bf16[16,16,1280]{2,1,0:T(8,128)(2,1)} custom-call(s32[8]{0:T(128)} %concatenate.3.info, bf16[16,16,1280]{2,1,0:T(8,128)(2,1)} %get-tuple-element.127.rest_0_, bf16[16,16,1280]{2,1,0:T(8,128)(2,1)} %collective-permute-done.28.rest_1_, bf16[16,16,1280]{2,1,0:T(8,128)(2,1)} %collective-permute-done.29.rest_2_, ...), custom_call_target="tpu_custom_call" | custom-call | flops 200000000 | bytes 65536 | tf_op jit(solution)/shard_map/sum_four/pallas_call | solution.py:852
  180.0 4.0 %collective-permute-done.34.rest_3_ = bf16[17,16,512]{2,1,0:T(8,128)(2,1)} collective-permute-done((bf16[17,16,512]{2,1,0:T(8,128)(2,1)}, bf16[17,16,512]{2,1,0:T(8,128)(2,1)}, u32[]{:S(2)}, u32[]{:S(2)}) %collective-permute-start.34) | collective-permute-done | bytes 278560 | tf_op jit(solution)/shard_map/ppermute | solution.py:1179
  183.9 3.3 %join_terms.1 = bf16[16,16,2304]{2,1,0:T(8,128)(2,1)} custom-call(s32[8]{0:T(128)} %concatenate.3.info, bf16[16,16,1280]{2,1,0:T(8,128)(2,1)} %sum_four.1.mixer, bf16[17,16,512]{2,1,0:T(8,128)(2,1)} %get-tuple-element.136.rest_0_, bf16[17,16,512]{2,1,0:T(8,128)(2,1)} %collective-permute-done.32.rest_1_, ...), custom_call_target="tpu_custom_call" | custom-call | flops 200000000 | bytes 65536 | tf_op jit(solution)/shard_map/join_terms/pallas_call | solution.py:852
  187.3 6.4 %all-to-all-start.1 = ((bf16[16,16,2304]{2,1,0:T(8,128)(2,1)}), bf16[16,16,2304]{2,1,0:T(8,128)(2,1)}, u32[]{:S(2)}, u32[]{:S(2)}) async-start(bf16[16,16,2304]{2,1,0:T(8,128)(2,1)} %join_terms.1), calls=%async_computation.1 | async-start | bytes 2359296 | tf_op jit(solution)/shard_map/all_to_all | solution.py:1202
  193.7 3.5 %place_pair.3 = f32[3,2,256,512]{3,2,1,0:T(8,128)} custom-call(s32[8]{0:T(128)} %concatenate.3.info, bf16[3,256,512]{2,1,0:T(8,128)(2,1)} %get-tuple-element.131.own, bf16[3,256,512]{2,1,0:T(8,128)(2,1)} %collective-permute-done.35.other), custom_call_target="tpu_custom_call" | custom-call | flops 200000000 | bytes 65536 | tf_op jit(solution)/shard_map/place_pair/pallas_call | solution.py:852
  197.2 14.9 %all-to-all-done.1.terms = bf16[16,16,2304]{2,1,0:T(8,128)(2,1)} async-done(((bf16[16,16,2304]{2,1,0:T(8,128)(2,1)}), bf16[16,16,2304]{2,1,0:T(8,128)(2,1)}, u32[]{:S(2)}, u32[]{:S(2)}) %all-to-all-start.1) | async-done | bytes 1179680 | tf_op jit(solution)/shard_map/all_to_all | solution.py:1202
  212.1 3.7 %finish.1 = (f32[3,8,256]{2,1,0:T(8,128)}, f32[8,256]{1,0:T(8,128)}, f32[8,2,768]{2,1,0:T(2,128)}, f32[8,768]{1,0:T(8,128)}, f32[2,512]{1,0:T(2,128)}, /*index=5...) custom-call(s32[8]{0:T(128)} %concatenate.3.info, ...), custom_call_target="tpu_custom_call" | custom-call | flops 200000000 | bytes 65536 | tf_op jit(solution)/shard_map/finish/pallas_call | solution.py:852
  (41 shorter events, 2.5 us)
Async XLA Ops:
  3.5 2.6 %collective-permute-start = (bf16[8,3328]{1,0:T(8,128)(2,1)}, bf16[8,3328]{1,0:T(8,128)(2,1)}, u32[]{:S(2)}, u32[]{:S(2)}) collective-permute-start(bf16[8,3328]{1,0:T(8,128)(2,1)} %get-tuple-element.83.local), channel_id=1, source_target_pairs={{0,1},{1,0},{2,3},{3,2},{4,5},{5,4},{6,7},{7,6},{8,9},{9,8},{10,11... | collective-permute-start | bytes 159752 | tf_op jit(solution)/shard_map/ppermute | solution.py:1162
  3.5 13.9 %collective-permute-start.4 = (f32[35,768]{1,0:T(8,128)}, f32[35,768]{1,0:T(8,128)}, u32[]{:S(2)}, u32[]{:S(2)}) collective-permute-start(f32[35,768]{1,0:T(8,128)} %get-tuple-element.86.own), channel_id=1, source_target_pairs={{0,64},{64,0},{1,65},{65,1},{2,66},{66,2},{3,67},{67,3},{4,68},{68... | collective-permute-start | bytes 322568 | tf_op jit(solution)/shard_map/ppermute | solution.py:1162
  8.3 6.0 %collective-permute-start.3 = (bf16[16,1664]{1,0:T(8,128)(2,1)}, bf16[16,1664]{1,0:T(8,128)(2,1)}, u32[]{:S(2)}, u32[]{:S(2)}) collective-permute-start(bf16[16,1664]{1,0:T(8,128)(2,1)} %pair_rows.1.rest_0_), channel_id=1, source_target_pairs={{0,2},{64,66},{2,0},{66,64},{1,3},{65,67},{3,1},{67,65},{4,6},{68,... | collective-permute-start | bytes 159752 | tf_op jit(solution)/shard_map/ppermute | solution.py:1173
  8.9 5.4 %collective-permute-start.2 = (bf16[16,1664]{1,0:T(8,128)(2,1)}, bf16[16,1664]{1,0:T(8,128)(2,1)}, u32[]{:S(2)}, u32[]{:S(2)}) collective-permute-start(bf16[16,1664]{1,0:T(8,128)(2,1)} %pair_rows.1.rest_0_), channel_id=1, source_target_pairs={{0,66},{64,0},{2,64},{66,2},{1,67},{65,1},{3,65},{67,3},{4,70},{68... | collective-permute-start | bytes 159752 | tf_op jit(solution)/shard_map/ppermute | solution.py:1173
  10.5 4.7 %collective-permute-start.1 = (bf16[16,1664]{1,0:T(8,128)(2,1)}, bf16[16,1664]{1,0:T(8,128)(2,1)}, u32[]{:S(2)}, u32[]{:S(2)}) collective-permute-start(bf16[16,1664]{1,0:T(8,128)(2,1)} %pair_rows.1.rest_0_), channel_id=1, source_target_pairs={{0,64},{64,2},{2,66},{66,0},{1,65},{65,3},{3,67},{67,1},{4,68},{68... | collective-permute-start | bytes 159752 | tf_op jit(solution)/shard_map/ppermute | solution.py:1173
  17.4 17.4 %collective-permute-start.10 = (bf16[4,16,1280]{2,1,0:T(8,128)(2,1)}, bf16[4,16,1280]{2,1,0:T(8,128)(2,1)}, u32[]{:S(2)}, u32[]{:S(2)}) collective-permute-start(bf16[4,16,1280]{2,1,0:T(8,128)(2,1)} %get-tuple-element.88.rest_4_), channel_id=1, source_target_pairs={{0,32},{16,48},{32,0},{48,16},{1,33},{17,49},{33,1},{49,17},{2,34}... | collective-permute-start | bytes 491528 | tf_op jit(solution)/shard_map/ppermute | solution.py:1179
  20.5 14.4 %collective-permute-start.9 = (bf16[4,16,1280]{2,1,0:T(8,128)(2,1)}, bf16[4,16,1280]{2,1,0:T(8,128)(2,1)}, u32[]{:S(2)}, u32[]{:S(2)}) collective-permute-start(bf16[4,16,1280]{2,1,0:T(8,128)(2,1)} %get-tuple-element.88.rest_4_), channel_id=1, source_target_pairs={{0,48},{16,0},{32,16},{48,32},{1,49},{17,1},{33,17},{49,33},{2,50}... | collective-permute-start | bytes 491528 | tf_op jit(solution)/shard_map/ppermute | solution.py:1179
  21.6 13.3 %collective-permute-start.8 = (bf16[4,16,1280]{2,1,0:T(8,128)(2,1)}, bf16[4,16,1280]{2,1,0:T(8,128)(2,1)}, u32[]{:S(2)}, u32[]{:S(2)}) collective-permute-start(bf16[4,16,1280]{2,1,0:T(8,128)(2,1)} %get-tuple-element.88.rest_4_), channel_id=1, source_target_pairs={{0,16},{16,32},{32,48},{48,0},{1,17},{17,33},{33,49},{49,1},{2,18}... | collective-permute-start | bytes 491528 | tf_op jit(solution)/shard_map/ppermute | solution.py:1179
  22.5 6.3 %collective-permute-start.7 = (bf16[4,16,384]{2,1,0:T(8,128)(2,1)}, bf16[4,16,384]{2,1,0:T(8,128)(2,1)}, u32[]{:S(2)}, u32[]{:S(2)}) collective-permute-start(bf16[4,16,384]{2,1,0:T(8,128)(2,1)} %get-tuple-element.87.rest_0_), channel_id=1, source_target_pairs={{0,8},{4,12},{8,0},{12,4},{1,9},{5,13},{9,1},{13,5},{2,10},{6,14},... | collective-permute-start | bytes 147464 | tf_op jit(solution)/shard_map/ppermute | solution.py:1179
  26.4 4.4 %collective-permute-start.6 = (bf16[4,16,384]{2,1,0:T(8,128)(2,1)}, bf16[4,16,384]{2,1,0:T(8,128)(2,1)}, u32[]{:S(2)}, u32[]{:S(2)}) collective-permute-start(bf16[4,16,384]{2,1,0:T(8,128)(2,1)} %get-tuple-element.87.rest_0_), channel_id=1, source_target_pairs={{0,12},{4,0},{8,4},{12,8},{1,13},{5,1},{9,5},{13,9},{2,14},{6,2},{... | collective-permute-start | bytes 147464 | tf_op jit(solution)/shard_map/ppermute | solution.py:1179
  28.8 6.1 %collective-permute-start.5 = (bf16[4,16,384]{2,1,0:T(8,128)(2,1)}, bf16[4,16,384]{2,1,0:T(8,128)(2,1)}, u32[]{:S(2)}, u32[]{:S(2)}) collective-permute-start(bf16[4,16,384]{2,1,0:T(8,128)(2,1)} %get-tuple-element.87.rest_0_), channel_id=1, source_target_pairs={{0,4},{4,8},{8,12},{12,0},{1,5},{5,9},{9,13},{13,1},{2,6},{6,10},{... | collective-permute-start | bytes 147464 | tf_op jit(solution)/shard_map/ppermute | solution.py:1179
  37.7 7.4 %collective-permute-start.19 = (bf16[2,4,32,384]{3,2,1,0:T(8,128)(2,1)}, bf16[2,4,32,384]{3,2,1,0:T(8,128)(2,1)S(1)}, u32[]{:S(2)}, u32[]{:S(2)}) collective-permute-start(bf16[2,4,32,384]{3,2,1,0:T(8,128)(2,1)} %bitcast.17), channel_id=1, source_target_pairs={{0,32},{16,48},{32,0},{48,16},{1,33},{17,49},{33,1},{49,17},{2,34}... | collective-permute-start | bytes 589832 | tf_op jit(solution)/shard_map/ppermute | solution.py:1179
  38.4 31.8 %collective-permute-start.13 = (bf16[2,4,32,1280]{3,2,1,0:T(8,128)(2,1)}, bf16[2,4,32,1280]{3,2,1,0:T(8,128)(2,1)}, u32[]{:S(2)}, u32[]{:S(2)}) collective-permute-start(bf16[2,4,32,1280]{3,2,1,0:T(8,128)(2,1)} %bitcast.12), channel_id=1, source_target_pairs={{0,8},{4,12},{8,0},{12,4},{1,9},{5,13},{9,1},{13,5},{2,10},{6,14},... | collective-permute-start | bytes 1966088 | tf_op jit(solution)/shard_map/ppermute | solution.py:1179
  40.2 30.0 %collective-permute-start.12 = (bf16[2,4,32,1280]{3,2,1,0:T(8,128)(2,1)}, bf16[2,4,32,1280]{3,2,1,0:T(8,128)(2,1)}, u32[]{:S(2)}, u32[]{:S(2)}) collective-permute-start(bf16[2,4,32,1280]{3,2,1,0:T(8,128)(2,1)} %bitcast.13), channel_id=1, source_target_pairs={{0,12},{4,0},{8,4},{12,8},{1,13},{5,1},{9,5},{13,9},{2,14},{6,2},{... | collective-permute-start | bytes 1966088 | tf_op jit(solution)/shard_map/ppermute | solution.py:1179
  40.9 29.3 %collective-permute-start.11 = (bf16[2,4,32,1280]{3,2,1,0:T(8,128)(2,1)}, bf16[2,4,32,1280]{3,2,1,0:T(8,128)(2,1)}, u32[]{:S(2)}, u32[]{:S(2)}) collective-permute-start(bf16[2,4,32,1280]{3,2,1,0:T(8,128)(2,1)} %bitcast.14), channel_id=1, source_target_pairs={{0,4},{4,8},{8,12},{12,0},{1,5},{5,9},{9,13},{13,1},{2,6},{6,10},{... | collective-permute-start | bytes 1966088 | tf_op jit(solution)/shard_map/ppermute | solution.py:1179
  42.2 6.4 %collective-permute-start.17 = (bf16[2,4,32,384]{3,2,1,0:T(8,128)(2,1)}, bf16[2,4,32,384]{3,2,1,0:T(8,128)(2,1)S(1)}, u32[]{:S(2)}, u32[]{:S(2)}) collective-permute-start(bf16[2,4,32,384]{3,2,1,0:T(8,128)(2,1)} %bitcast.18), channel_id=1, source_target_pairs={{0,48},{16,0},{32,16},{48,32},{1,49},{17,1},{33,17},{49,33},{2,50}... | collective-permute-start | bytes 589832 | tf_op jit(solution)/shard_map/ppermute | solution.py:1179
  45.1 7.8 %copy-start = (bf16[2,4,32,384]{3,2,1,0:T(8,128)(2,1)}, bf16[2,4,32,384]{3,2,1,0:T(8,128)(2,1)S(1)}, u32[]{:S(2)}) copy-start(bf16[2,4,32,384]{3,2,1,0:T(8,128)(2,1)S(1)} %collective-permute-done.19.rest_6_) | copy-start | bytes 589828
  45.1 7.8 %collective-permute-start.15 = (bf16[2,4,32,384]{3,2,1,0:T(8,128)(2,1)}, bf16[2,4,32,384]{3,2,1,0:T(8,128)(2,1)S(1)}, u32[]{:S(2)}, u32[]{:S(2)}) collective-permute-start(bf16[2,4,32,384]{3,2,1,0:T(8,128)(2,1)} %bitcast.19), channel_id=1, source_target_pairs={{0,16},{16,32},{32,48},{48,0},{1,17},{17,33},{33,49},{49,1},{2,18}... | collective-permute-start | bytes 589832 | tf_op jit(solution)/shard_map/ppermute | solution.py:1179
  48.7 5.7 %copy-start.1 = (bf16[2,4,32,384]{3,2,1,0:T(8,128)(2,1)}, bf16[2,4,32,384]{3,2,1,0:T(8,128)(2,1)S(1)}, u32[]{:S(2)}) copy-start(bf16[2,4,32,384]{3,2,1,0:T(8,128)(2,1)S(1)} %collective-permute-done.17.rest_4_) | copy-start | bytes 589828
  48.7 4.3 %collective-permute-start.14 = (bf16[2,4,32,384]{3,2,1,0:T(8,128)(2,1)}, bf16[2,4,32,384]{3,2,1,0:T(8,128)(2,1)S(1)}, u32[]{:S(2)}, u32[]{:S(2)}) collective-permute-start(bf16[2,4,32,384]{3,2,1,0:T(8,128)(2,1)} %bitcast.20), channel_id=1, source_target_pairs={{0,1},{1,0},{2,3},{3,2},{4,5},{5,4},{6,7},{7,6},{8,9},{9,8},{10,11... | collective-permute-start | bytes 589832 | tf_op jit(solution)/shard_map/ppermute | solution.py:1162
  52.9 1.7 copy-start.2
  52.9 1.4 collective-permute-start.20
  53.0 1.7 copy-start.3
  53.0 1.7 collective-permute-start.18
  54.4 0.7 copy-start.4
  54.4 1.6 collective-permute-start.16
  55.1 0.7 copy-start.5
  70.3 2.5 %collective-permute-start.21 = (bf16[2,4,32,1280]{3,2,1,0:T(8,128)(2,1)}, bf16[2,4,32,1280]{3,2,1,0:T(8,128)(2,1)}, u32[]{:S(2)}, u32[]{:S(2)}) collective-permute-start(bf16[2,4,32,1280]{3,2,1,0:T(8,128)(2,1)} %bitcast.15), channel_id=1, source_target_pairs={{0,1},{1,0},{2,3},{3,2},{4,5},{5,4},{6,7},{7,6},{8,9},{9,8},{10,11... | collective-permute-start | bytes 1966088 | tf_op jit(solution)/shard_map/ppermute | solution.py:1162
  70.5 3.2 %collective-permute-start.22 = (bf16[2,4,32,1280]{3,2,1,0:T(8,128)(2,1)}, bf16[2,4,32,1280]{3,2,1,0:T(8,128)(2,1)}, u32[]{:S(2)}, u32[]{:S(2)}) collective-permute-start(bf16[2,4,32,1280]{3,2,1,0:T(8,128)(2,1)} %collective-permute-done.11.rest_2_), channel_id=1, source_target_pairs={{0,1},{1,0},{2,3},{3,2},{4,5},{5,4},{6,7},{7,6},{8,9},{9,8},{10,11... | collective-permute-start | bytes 1966088 | tf_op jit(solution)/shard_map/ppermute | solution.py:1162
  70.8 3.8 %collective-permute-start.23 = (bf16[2,4,32,1280]{3,2,1,0:T(8,128)(2,1)}, bf16[2,4,32,1280]{3,2,1,0:T(8,128)(2,1)}, u32[]{:S(2)}, u32[]{:S(2)}) collective-permute-start(bf16[2,4,32,1280]{3,2,1,0:T(8,128)(2,1)} %collective-permute-done.12.rest_4_), channel_id=1, source_target_pairs={{0,1},{1,0},{2,3},{3,2},{4,5},{5,4},{6,7},{7,6},{8,9},{9,8},{10,11... | collective-permute-start | bytes 1966088 | tf_op jit(solution)/shard_map/ppermute | solution.py:1162
  71.0 4.6 %collective-permute-start.24 = (bf16[2,4,32,1280]{3,2,1,0:T(8,128)(2,1)}, bf16[2,4,32,1280]{3,2,1,0:T(8,128)(2,1)}, u32[]{:S(2)}, u32[]{:S(2)}) collective-permute-start(bf16[2,4,32,1280]{3,2,1,0:T(8,128)(2,1)} %collective-permute-done.13.rest_6_), channel_id=1, source_target_pairs={{0,1},{1,0},{2,3},{3,2},{4,5},{5,4},{6,7},{7,6},{8,9},{9,8},{10,11... | collective-permute-start | bytes 1966088 | tf_op jit(solution)/shard_map/ppermute | solution.py:1162
  113.6 5.9 %collective-permute-start.25 = (bf16[64,16,1280]{2,1,0:T(8,128)(2,1)}, bf16[64,16,1280]{2,1,0:T(8,128)(2,1)}, u32[]{:S(2)}, u32[]{:S(2)}) collective-permute-start(bf16[64,16,1280]{2,1,0:T(8,128)(2,1)} %get-tuple-element.99), channel_id=1, source_target_pairs={{0,1},{1,0},{2,3},{3,2},{4,5},{5,4},{6,7},{7,6},{8,9},{9,8},{10,11... | collective-permute-start | bytes 7864328 | tf_op jit(solution)/shard_map/ppermute | solution.py:1162
  114.0 5.5 %collective-permute-start.26 = (f32[512,128]{1,0:T(8,128)}, f32[512,128]{1,0:T(8,128)}, u32[]{:S(2)}, u32[]{:S(2)}) collective-permute-start(f32[512,128]{1,0:T(8,128)} %get-tuple-element.100.small), channel_id=1, source_target_pairs={{0,1},{1,0},{2,3},{3,2},{4,5},{5,4},{6,7},{7,6},{8,9},{9,8},{10,11... | collective-permute-start | bytes 786440 | tf_op jit(solution)/shard_map/ppermute | solution.py:1162
  114.4 38.6 %collective-permute-start.27 = (bf16[3,256,512]{2,1,0:T(8,128)(2,1)}, bf16[3,256,512]{2,1,0:T(8,128)(2,1)}, u32[]{:S(2)}, u32[]{:S(2)}) collective-permute-start(bf16[3,256,512]{2,1,0:T(8,128)(2,1)} %get-tuple-element.115.own), channel_id=1, source_target_pairs={{0,64},{64,0},{1,65},{65,1},{2,66},{66,2},{3,67},{67,3},{4,68},{68... | collective-permute-start | bytes 2359304 | tf_op jit(solution)/shard_map/ppermute | solution.py:1162
  125.7 33.8 %collective-permute-start.28 = (bf16[16,16,1280]{2,1,0:T(8,128)(2,1)}, bf16[16,16,1280]{2,1,0:T(8,128)(2,1)}, u32[]{:S(2)}, u32[]{:S(2)}) collective-permute-start(bf16[16,16,1280]{2,1,0:T(8,128)(2,1)} %get-tuple-element.117), channel_id=1, source_target_pairs={{0,16},{16,32},{32,48},{48,0},{1,17},{17,33},{33,49},{49,1},{2,18}... | collective-permute-start | bytes 1966088 | tf_op jit(solution)/shard_map/ppermute | solution.py:1179
  126.1 33.5 %collective-permute-start.29 = (bf16[16,16,1280]{2,1,0:T(8,128)(2,1)}, bf16[16,16,1280]{2,1,0:T(8,128)(2,1)}, u32[]{:S(2)}, u32[]{:S(2)}) collective-permute-start(bf16[16,16,1280]{2,1,0:T(8,128)(2,1)} %get-tuple-element.118), channel_id=1, source_target_pairs={{0,48},{16,0},{32,16},{48,32},{1,49},{17,1},{33,17},{49,33},{2,50}... | collective-permute-start | bytes 1966088 | tf_op jit(solution)/shard_map/ppermute | solution.py:1179
  129.0 30.5 %collective-permute-start.30 = (bf16[16,16,1280]{2,1,0:T(8,128)(2,1)}, bf16[16,16,1280]{2,1,0:T(8,128)(2,1)}, u32[]{:S(2)}, u32[]{:S(2)}) collective-permute-start(bf16[16,16,1280]{2,1,0:T(8,128)(2,1)} %get-tuple-element.119), channel_id=1, source_target_pairs={{0,32},{16,48},{32,0},{48,16},{1,33},{17,49},{33,1},{49,17},{2,34}... | collective-permute-start | bytes 1966088 | tf_op jit(solution)/shard_map/ppermute | solution.py:1179
  146.8 12.8 %all-to-all-start = ((bf16[16,64,128]{2,1,0:T(8,128)(2,1)}), bf16[16,64,128]{2,1,0:T(8,128)(2,1)}, u32[]{:S(2)}, u32[]{:S(2)}) async-start(bf16[16,64,128]{2,1,0:T(8,128)(2,1)} %get-tuple-element.116), calls=%async_computation | async-start | bytes 524288 | tf_op jit(solution)/shard_map/all_to_all | solution.py:1202
  159.6 3.1 %collective-permute-start.31 = (bf16[64,16,512]{2,1,0:T(8,128)(2,1)}, bf16[64,16,512]{2,1,0:T(8,128)(2,1)}, u32[]{:S(2)}, u32[]{:S(2)}) collective-permute-start(bf16[64,16,512]{2,1,0:T(8,128)(2,1)} %get-tuple-element.121), channel_id=1, source_target_pairs={{0,1},{1,0},{2,3},{3,2},{4,5},{5,4},{6,7},{7,6},{8,9},{9,8},{10,11... | collective-permute-start | bytes 3145736 | tf_op jit(solution)/shard_map/ppermute | solution.py:1162
  159.7 20.3 %collective-permute-start.35 = (bf16[3,256,512]{2,1,0:T(8,128)(2,1)}, bf16[3,256,512]{2,1,0:T(8,128)(2,1)}, u32[]{:S(2)}, u32[]{:S(2)}) collective-permute-start(bf16[3,256,512]{2,1,0:T(8,128)(2,1)} %get-tuple-element.131.own), channel_id=1, source_target_pairs={{0,64},{64,0},{1,65},{65,1},{2,66},{66,2},{3,67},{67,3},{4,68},{68... | collective-permute-start | bytes 2359304 | tf_op jit(solution)/shard_map/ppermute | solution.py:1162
  167.2 12.7 %collective-permute-start.32 = (bf16[17,16,512]{2,1,0:T(8,128)(2,1)}, bf16[17,16,512]{2,1,0:T(8,128)(2,1)}, u32[]{:S(2)}, u32[]{:S(2)}) collective-permute-start(bf16[17,16,512]{2,1,0:T(8,128)(2,1)} %get-tuple-element.124), channel_id=1, source_target_pairs={{0,16},{16,32},{32,48},{48,0},{1,17},{17,33},{33,49},{49,1},{2,18}... | collective-permute-start | bytes 835592 | tf_op jit(solution)/shard_map/ppermute | solution.py:1179
  168.7 11.2 %collective-permute-start.33 = (bf16[17,16,512]{2,1,0:T(8,128)(2,1)}, bf16[17,16,512]{2,1,0:T(8,128)(2,1)}, u32[]{:S(2)}, u32[]{:S(2)}) collective-permute-start(bf16[17,16,512]{2,1,0:T(8,128)(2,1)} %get-tuple-element.125), channel_id=1, source_target_pairs={{0,48},{16,0},{32,16},{48,32},{1,49},{17,1},{33,17},{49,33},{2,50}... | collective-permute-start | bytes 835592 | tf_op jit(solution)/shard_map/ppermute | solution.py:1179
  170.5 13.4 %collective-permute-start.34 = (bf16[17,16,512]{2,1,0:T(8,128)(2,1)}, bf16[17,16,512]{2,1,0:T(8,128)(2,1)}, u32[]{:S(2)}, u32[]{:S(2)}) collective-permute-start(bf16[17,16,512]{2,1,0:T(8,128)(2,1)} %get-tuple-element.126), channel_id=1, source_target_pairs={{0,32},{16,48},{32,0},{48,16},{1,33},{17,49},{33,1},{49,17},{2,34}... | collective-permute-start | bytes 835592 | tf_op jit(solution)/shard_map/ppermute | solution.py:1179
  187.3 24.8 %all-to-all-start.1 = ((bf16[16,16,2304]{2,1,0:T(8,128)(2,1)}), bf16[16,16,2304]{2,1,0:T(8,128)(2,1)}, u32[]{:S(2)}, u32[]{:S(2)}) async-start(bf16[16,16,2304]{2,1,0:T(8,128)(2,1)} %join_terms.1), calls=%async_computation.1 | async-start | bytes 2359296 | tf_op jit(solution)/shard_map/all_to_all | solution.py:1202
